TPU v7x, 32 devices: a whole 2x2x4 slice. The times are simulated.
32 devices in a mesh: runs: 2 (over y), gx: 4 (over z), gy: 2 (over x), gz: 2 (over core).
Axes of the slice: x: 2, y: 2, z: 4, core: 2. Of those that a mesh axis runs over, the one named last changes fastest.
Arguments:
- velocity_start: float32 [3, 64, 32, 256], P(None, ('runs', 'gx'), 'gy', 'gz'), parts along dimension 1, may hold values from -6 to 6
- stress_start: float32 [6, 64, 32, 256], P(None, ('runs', 'gx'), 'gy', 'gz'), parts along dimension 1, may hold values from -6 to 6
- material: float32 [3, 64, 32, 256], P(None, ('runs', 'gx'), 'gy', 'gz'), parts along dimension 1, may hold values from 0.5 to 2
- force_site: int32 [2], P('runs'), parts along dimension 0, may hold values from 0 to 262143
- force_wavelet: float32 [4, 3], P('runs'), parts along dimension 0, may hold values from -8 to 8
- save_cells: int32 [8, 2, 2, 1024], P(('runs', 'gx'), 'gy', 'gz'), parts along dimension 0, may hold values from 0 to 16383
- save_writer: int32 [8, 2, 2, 1024, 1], P(('runs', 'gx'), 'gy', 'gz'), parts along dimension 0, may hold values from 0 to 7; in each aligned block of 1024 rows (0 to 1023, 1024 to 2047, ..., all dimensions but the last counted through in order) at most 256 rows name the same one
Outputs:
- velocity: float32 [3, 64, 32, 256], P(None, ('runs', 'gx'), 'gy', 'gz'), parts along dimension 1
- strain_saved: float32 [4, 12, 16384], P(('runs', 'gz'), None, ('gx', 'gy')), parts along dimension 0
There are 2 independent parts, one for each index of `runs`. A program takes and returns all parts, laid end to end along the dimension named above; each array names one. Nothing has to cross between parts.
Inputs may be any that keep to these rules, and one draw needn't show every extreme that they name: `force_site`: flat index x 32 * 256 + y * 256 + z of the site. `save_cells`: flat index of the grid point within the device's block of 8 x 16 x 128 points, x slowest and depth fastest; several save points may share a grid point. `save_writer`: writer a * 2 + b among the devices (a, b) that hold the same depth index; among the 1024 save points of one device at most 256 name the same writer, and in every draw some device names some writer exactly 256 times.
All inputs are finite; a program needn't handle non-finite values.
Results may differ from a plain program's by a relative error of at most 0.0003.
Values sent between devices are 32-bit elements; how exact they have to be, the bound alone decides.
No kernel may reach another device: no remote copies, remote signals or barrier semaphores. Data moves between devices by JAX's collectives and lax.ppermute only.
A program may use at most 64 MiB of HBM per device.

v0:
```python
import jax
import jax.numpy as jnp
from jax import lax
from jax.sharding import PartitionSpec as P

STEPS = 2


INNER = 9.0 / 8.0
OUTER = -1.0 / 24.0
TIME_STEP = 0.12


def extended(cells, sides, width):
    for axis, dim in sides:
        count = lax.axis_size(axis)
        ends = count - 1
        head = lax.slice_in_dim(cells, 0, width, axis=dim)
        tail = lax.slice_in_dim(cells, cells.shape[dim] - width, cells.shape[dim], axis=dim)
        cells = jnp.concatenate(
            [
                lax.ppermute(tail, axis, [(i, (i + 1) % count) for i in range(ends)]),
                cells,
                lax.ppermute(head, axis, [((i + 1) % count, i) for i in range(ends)]),
            ],
            axis=dim,
        )
    return cells


def shifted(values, offset, dimension):
    config = [(0, 0, 0)] * values.ndim
    config[dimension] = (offset, -offset, 0)
    return lax.pad(values, jnp.zeros((), values.dtype), config)


def forward(values, dimension):
    return INNER * (shifted(values, -1, dimension) - values) + OUTER * (
        shifted(values, -2, dimension) - shifted(values, 1, dimension)
    )


def backward(values, dimension):
    return INNER * (values - shifted(values, 1, dimension)) + OUTER * (
        shifted(values, -1, dimension) - shifted(values, 2, dimension)
    )


def velocity_rates(stress):
    return jnp.stack(
        [
            forward(stress[0], 0) + backward(stress[3], 1) + backward(stress[4], 2),
            backward(stress[3], 0) + forward(stress[1], 1) + backward(stress[5], 2),
            backward(stress[4], 0) + backward(stress[5], 1) + forward(stress[2], 2),
        ]
    )


def velocity_gradients(velocity):
    return jnp.stack(
        [
            backward(velocity[0], 0),
            backward(velocity[1], 1),
            backward(velocity[2], 2),
            forward(velocity[0], 1) + forward(velocity[1], 0),
            forward(velocity[0], 2) + forward(velocity[2], 0),
            forward(velocity[1], 2) + forward(velocity[2], 1),
        ]
    )


def stress_update(stress, gradients, lame_first, shear):
    volume = gradients[0] + gradients[1] + gradients[2]
    normal = stress[:3] + TIME_STEP * (2.0 * shear * gradients[:3] + lame_first * volume)
    sliding = stress[3:] + TIME_STEP * shear * gradients[3:]
    return jnp.concatenate([normal, sliding], axis=0)


def strain_of(points, lame_points, shear_points):
    trace_sum = points[0] + points[1] + points[2]
    shrink = lame_points / (3.0 * lame_points + 2.0 * shear_points) * trace_sum
    normal = (points[:3] - shrink) / (2.0 * shear_points)
    sliding = points[3:] / (2.0 * shear_points)
    return jnp.concatenate([normal, sliding], axis=0)


def bucket_slots(writers, width, capacity):
    onehot = (writers[:, None] == jnp.arange(width, dtype=jnp.int32)[None, :]).astype(jnp.int32)
    before = jnp.cumsum(onehot, axis=0) - onehot
    position = jnp.sum(before * onehot, axis=1)
    return writers * capacity + position


def interior(values, depth):
    return values[
        :,
        depth : values.shape[1] - depth,
        depth : values.shape[2] - depth,
        depth : values.shape[3] - depth,
    ]


def inject(velocity, buoyancy, coords, force):
    inside = jnp.logical_and(coords[0] >= 0, coords[0] < buoyancy.shape[0])
    inside = jnp.logical_and(inside, jnp.logical_and(coords[1] >= 0, coords[1] < buoyancy.shape[1]))
    inside = jnp.logical_and(inside, jnp.logical_and(coords[2] >= 0, coords[2] < buoyancy.shape[2]))
    place_x = jnp.clip(coords[0], 0, buoyancy.shape[0] - 1)
    place_y = jnp.clip(coords[1], 0, buoyancy.shape[1] - 1)
    place_z = jnp.clip(coords[2], 0, buoyancy.shape[2] - 1)
    amount = TIME_STEP * buoyancy[place_x, place_y, place_z] * force
    return velocity.at[:, place_x, place_y, place_z].add(
        jnp.where(inside, amount, jnp.zeros_like(amount))
    )


def sample(stress, cells, lame_points, shear_points):
    points = stress.reshape(6, -1)[:, cells]
    return strain_of(points, lame_points, shear_points)


def per_device(
    velocity_start, stress_start, material, force_site, force_wavelet, save_cells, save_writer
):
    block_x, block_y, block_z = (
        velocity_start.shape[1],
        velocity_start.shape[2],
        velocity_start.shape[3],
    )
    total_y = block_y * lax.axis_size("gy")
    total_z = block_z * lax.axis_size("gz")
    site = force_site[0]
    local_x = site // (total_y * total_z) - lax.axis_index("gx") * block_x
    local_y = site // total_z % total_y - lax.axis_index("gy") * block_y
    local_z = site % total_z - lax.axis_index("gz") * block_z
    cells = save_cells.reshape(-1)
    lame_points = material[0].reshape(-1)[cells]
    shear_points = material[1].reshape(-1)[cells]
    saved = []
    velocity = velocity_start
    stress = stress_start
    lame_first = material[0]
    shear = material[1]
    buoyancy = material[2]
    coords = (local_x, local_y, local_z)
    for step_index in range(STEPS):
        padded = extended(stress, (("gx", 1), ("gy", 2), ("gz", 3)), 2)
        velocity = velocity + TIME_STEP * buoyancy * interior(velocity_rates(padded), 2)
        velocity = inject(velocity, buoyancy, coords, force_wavelet[step_index])
        padded = extended(velocity, (("gx", 1), ("gy", 2), ("gz", 3)), 2)
        stress = stress_update(stress, interior(velocity_gradients(padded), 2), lame_first, shear)
        saved.append(sample(stress, cells, lame_points, shear_points))
    values = jnp.concatenate(saved, axis=0)
    width = lax.axis_size("gx") * lax.axis_size("gy")
    capacity = max(2, 2 * cells.shape[0] // width)
    targets = bucket_slots(save_writer.reshape(-1), width, capacity)
    outgoing = (
        jnp.zeros((values.shape[0], width * capacity), jnp.float32).at[:, targets].set(values)
    )
    arrived = lax.all_to_all(outgoing, ("gx", "gy"), split_axis=1, concat_axis=1, tiled=True)
    return (velocity, arrived.reshape(1, values.shape[0], width * capacity))


def solution(mesh):
    in_specs = (
        P(None, ("runs", "gx"), "gy", "gz"),
        P(None, ("runs", "gx"), "gy", "gz"),
        P(None, ("runs", "gx"), "gy", "gz"),
        P("runs"),
        P("runs", None),
        P(("runs", "gx"), "gy", "gz", None),
        P(("runs", "gx"), "gy", "gz", None, None),
    )
    out_specs = (P(None, ("runs", "gx"), "gy", "gz"), P(("runs", "gz"), None, ("gx", "gy")))
    return jax.shard_map(
        per_device, mesh=mesh, in_specs=in_specs, out_specs=out_specs, check_vma=False
    )
```

profile of v0, /device:TPU:0, one launch (start us, length us, event | category | flops | bytes accessed | tf_op | source)
XLA Modules:
  0.0 159.3 jit_solution(15792259707104944343)
XLA Ops:
  2.9 5.6 %collective-permute-start = (f32[6,2,16,128]{3,2,1,0:T(8,128)S(1)}, f32[6,2,16,128]{3,2,1,0:T(8,128)S(1)}, u32[]{:S(2)}, u32[]{:S(2)}) collective-permute-start(f32[6,2,16,128]{3,2,1,0:T(8,128)S(1)} %get-tuple-element.81), channel_id=1, source_target_pairs={{0,4},{4,8},{8,12},{1,5},{5,9},{9,13},{2,6},{6,10},{10,14},{3,7},{... | collective-permute-start | bytes 294920 | tf_op jit(solution)/shard_map/ppermute | solution.py:22
  12.5 3.8 %collective-permute-start.2 = (f32[6,12,2,128]{3,2,1,0:T(2,128)S(1)}, f32[6,12,2,128]{3,2,1,0:T(2,128)S(1)}, u32[]{:S(2)}, u32[]{:S(2)}) collective-permute-start(f32[6,12,2,128]{3,2,1,0:T(2,128)S(1)} %get-tuple-element.70), channel_id=1, source_target_pairs={{0,2},{1,3},{4,6},{5,7},{8,10},{9,11},{12,14},{13,15},{16,18},{17,... | collective-permute-start | bytes 221192 | tf_op jit(solution)/shard_map/ppermute | solution.py:22
  18.3 4.3 %collective-permute-done.3 = f32[6,12,2,128]{3,2,1,0:T(2,128)S(1)} collective-permute-done((f32[6,12,2,128]{3,2,1,0:T(2,128)S(1)}, f32[6,12,2,128]{3,2,1,0:T(2,128)S(1)}, u32[]{:S(2)}, u32[]{:S(2)}) %collective-permute-start.3) | collective-permute-done | bytes 73760 | tf_op jit(solution)/shard_map/ppermute | solution.py:24
  25.5 3.0 %collective-permute-start.4 = (f32[6,12,20,2]{2,3,1,0:T(2,128)S(1)}, f32[6,12,20,2]{2,3,1,0:T(2,128)S(1)}, u32[]{:S(2)}, u32[]{:S(2)}) collective-permute-start(f32[6,12,20,2]{2,3,1,0:T(2,128)S(1)} %copy.161), channel_id=1, source_target_pairs={{0,1},{2,3},{4,5},{6,7},{8,9},{10,11},{12,13},{14,15},{16,17},{18,... | collective-permute-start | bytes 34568 | tf_op jit(solution)/shard_map/ppermute | solution.py:22
  29.3 2.3 %reduce-window.6 = s32[8,8,128]{2,1,0:T(8,128)S(1)} reduce-window(s32[8,8,128]{2,1,0:T(8,128)S(1)} %fusion.115, s32[]{:T(128)} %constant.122.clone.1), window={size=1x1x128 pad=0_0x0_0x127_0}, to_apply=%region_1.2 | reduce-window | flops 1040384 | bytes 65540 | tf_op jit(solution)/shard_map/reduce-window
  36.1 3.6 %collective-permute-start.6 = (f32[3,2,16,128]{3,2,1,0:T(8,128)S(1)}, f32[3,2,16,128]{3,2,1,0:T(8,128)S(1)}, u32[]{:S(2)}, u32[]{:S(2)}) collective-permute-start(f32[3,2,16,128]{3,2,1,0:T(8,128)S(1)} %get-tuple-element.105), channel_id=1, source_target_pairs={{0,4},{4,8},{8,12},{1,5},{5,9},{9,13},{2,6},{6,10},{10,14},{3,7},{... | collective-permute-start | bytes 147464 | tf_op jit(solution)/shard_map/ppermute | solution.py:22
  41.4 4.2 %collective-permute-done.7 = f32[3,2,16,128]{3,2,1,0:T(8,128)S(1)} collective-permute-done((f32[3,2,16,128]{3,2,1,0:T(8,128)S(1)}, f32[3,2,16,128]{3,2,1,0:T(8,128)S(1)}, u32[]{:S(2)}, u32[]{:S(2)}) %collective-permute-start.7) | collective-permute-done | bytes 49184 | tf_op jit(solution)/shard_map/ppermute | solution.py:24
  48.9 4.2 %collective-permute-done.9 = f32[3,12,2,128]{3,2,1,0:T(2,128)S(1)} collective-permute-done((f32[3,12,2,128]{3,2,1,0:T(2,128)S(1)}, f32[3,12,2,128]{3,2,1,0:T(2,128)S(1)}, u32[]{:S(2)}, u32[]{:S(2)}) %collective-permute-start.9) | collective-permute-done | bytes 36896 | tf_op jit(solution)/shard_map/ppermute | solution.py:24
  56.1 2.3 %collective-permute-done.11 = f32[3,12,20,2]{3,2,1,0:T(8,128)S(1)} collective-permute-done((f32[3,12,20,2]{3,2,1,0:T(8,128)S(1)}, f32[3,12,20,2]{3,2,1,0:T(8,128)S(1)}, u32[]{:S(2)}, u32[]{:S(2)}) %collective-permute-start.11) | collective-permute-done | bytes 5792 | tf_op jit(solution)/shard_map/ppermute | solution.py:24
  60.4 3.5 %collective-permute-start.12 = (f32[6,2,16,128]{3,2,1,0:T(8,128)S(1)}, f32[6,2,16,128]{3,2,1,0:T(8,128)S(1)}, u32[]{:S(2)}, u32[]{:S(2)}) collective-permute-start(f32[6,2,16,128]{3,2,1,0:T(8,128)S(1)} %get-tuple-element.76), channel_id=1, source_target_pairs={{0,4},{4,8},{8,12},{1,5},{5,9},{9,13},{2,6},{6,10},{10,14},{3,7},{... | collective-permute-start | bytes 294920 | tf_op jit(solution)/shard_map/ppermute | solution.py:22
  66.2 4.2 %collective-permute-done.13 = f32[6,2,16,128]{3,2,1,0:T(8,128)S(1)} collective-permute-done((f32[6,2,16,128]{3,2,1,0:T(8,128)S(1)}, f32[6,2,16,128]{3,2,1,0:T(8,128)S(1)}, u32[]{:S(2)}, u32[]{:S(2)}) %collective-permute-start.13) | collective-permute-done | bytes 98336 | tf_op jit(solution)/shard_map/ppermute | solution.py:24
  74.0 4.3 %collective-permute-done.15 = f32[6,12,2,128]{3,2,1,0:T(2,128)S(1)} collective-permute-done((f32[6,12,2,128]{3,2,1,0:T(2,128)S(1)}, f32[6,12,2,128]{3,2,1,0:T(2,128)S(1)}, u32[]{:S(2)}, u32[]{:S(2)}) %collective-permute-start.15) | collective-permute-done | bytes 73760 | tf_op jit(solution)/shard_map/ppermute | solution.py:24
  81.2 3.2 %collective-permute-start.16 = (f32[6,12,20,2]{2,3,1,0:T(2,128)S(1)}, f32[6,12,20,2]{2,3,1,0:T(2,128)S(1)}, u32[]{:S(2)}, u32[]{:S(2)}) collective-permute-start(f32[6,12,20,2]{2,3,1,0:T(2,128)S(1)} %copy.166), channel_id=1, source_target_pairs={{0,1},{2,3},{4,5},{6,7},{8,9},{10,11},{12,13},{14,15},{16,17},{18,... | collective-permute-start | bytes 34568 | tf_op jit(solution)/shard_map/ppermute | solution.py:22
  84.5 6.1 %gather_fusion.2 = f32[1024]{0:T(1024)S(1)} fusion(f32[16384]{0:T(1024)S(1)} %bitcast.140, s32[1024]{0:T(1024)S(1)} %broadcast_clamp_fusion), kind=kCustom, calls=%fused_computation.2 | custom fusion | bytes 12288 | tf_op jit(solution)/shard_map/gather | solution.py:137
  95.1 3.5 %collective-permute-start.18 = (f32[3,2,16,128]{3,2,1,0:T(8,128)S(1)}, f32[3,2,16,128]{3,2,1,0:T(8,128)S(1)}, u32[]{:S(2)}, u32[]{:S(2)}) collective-permute-start(f32[3,2,16,128]{3,2,1,0:T(8,128)S(1)} %get-tuple-element.103), channel_id=1, source_target_pairs={{0,4},{4,8},{8,12},{1,5},{5,9},{9,13},{2,6},{6,10},{10,14},{3,7},{... | collective-permute-start | bytes 147464 | tf_op jit(solution)/shard_map/ppermute | solution.py:22
  100.3 4.3 %collective-permute-done.19 = f32[3,2,16,128]{3,2,1,0:T(8,128)S(1)} collective-permute-done((f32[3,2,16,128]{3,2,1,0:T(8,128)S(1)}, f32[3,2,16,128]{3,2,1,0:T(8,128)S(1)}, u32[]{:S(2)}, u32[]{:S(2)}) %collective-permute-start.19) | collective-permute-done | bytes 49184 | tf_op jit(solution)/shard_map/ppermute | solution.py:24
  107.5 6.2 %gather_fusion.1 = f32[1024]{0:T(1024)S(1)} fusion(f32[16384]{0:T(1024)S(1)} %bitcast.139, s32[1024]{0:T(1024)S(1)} %broadcast_clamp_fusion), kind=kCustom, calls=%fused_computation.1 | custom fusion | bytes 12288 | tf_op jit(solution)/shard_map/gather | solution.py:136
  113.7 4.8 %copy.171 = f32[6,8,16,128]{0,3,2,1:T(8,128)} copy(f32[6,8,16,128]{3,2,1,0:T(8,128)S(1)} %pad_maximum_fusion.6) | data formatting | bytes 786432 | tf_op jit(solution)/shard_map/concatenate | solution.py:76
  118.5 6.2 %gather_fusion = f32[1024,6]{1,0:T(8,128)S(1)} fusion(f32[6,16384]{0,1:T(8,128)} %bitcast.142, s32[1024]{0:T(1024)S(1)} %broadcast_clamp_fusion), kind=kCustom, calls=%fused_computation | custom fusion | bytes 53248 | tf_op jit(solution)/shard_map/gather | solution.py:117
  127.8 2.3 %collective-permute-done.23 = f32[3,12,20,2]{3,2,1,0:T(8,128)S(1)} collective-permute-done((f32[3,12,20,2]{3,2,1,0:T(8,128)S(1)}, f32[3,12,20,2]{3,2,1,0:T(8,128)S(1)}, u32[]{:S(2)}, u32[]{:S(2)}) %collective-permute-start.23) | collective-permute-done | bytes 5792 | tf_op jit(solution)/shard_map/ppermute | solution.py:24
  132.2 4.8 %copy.173 = f32[6,8,16,128]{0,3,2,1:T(8,128)} copy(f32[6,8,16,128]{3,2,1,0:T(8,128)S(1)} %pad_maximum_fusion.9) | data formatting | bytes 786432 | tf_op jit(solution)/shard_map/concatenate | solution.py:76
  137.1 6.2 %gather_fusion.3 = f32[1024,6]{1,0:T(8,128)S(1)} fusion(f32[6,16384]{0,1:T(8,128)} %bitcast.141, s32[1024]{0:T(1024)S(1)} %broadcast_clamp_fusion), kind=kCustom, calls=%fused_computation.3 | custom fusion | bytes 53248 | tf_op jit(solution)/shard_map/gather | solution.py:117
  143.7 3.3 %scatter_custom_fusion = f32[12,2048]{0,1:T(8,128)S(1)} fusion(s32[1024]{0:T(1024)S(1)} %bitcast.157, f32[1024,12]{1,0:T(8,128)S(1)} %copy.175, f32[]{:T(128)} %constant.119.clone.1), kind=kCustom, calls=%fused_computation.16 | custom fusion | bytes 98308 | tf_op jit(solution)/shard_map/scatter | solution.py:157
  147.4 11.1 %all_to_all.9 = f32[12,8,256]{2,0,1:T(8,128)S(1)} all-to-all(f32[12,8,256]{2,0,1:T(8,128)S(1)} %copy.176), channel_id=1, replica_groups=mesh['runs'=2,'gx'=4,'gy'=2,'gz'=2] {'gx','gy'}, dimensions={1} | all-to-all | bytes 196608 | tf_op jit(solution)/shard_map/all_to_all | solution.py:159
  (131 shorter events, 50.0 us)
Async XLA Ops:
  1.6 10.8 %collective-permute-start.1 = (f32[6,2,16,128]{3,2,1,0:T(8,128)S(1)}, f32[6,2,16,128]{3,2,1,0:T(8,128)S(1)}, u32[]{:S(2)}, u32[]{:S(2)}) collective-permute-start(f32[6,2,16,128]{3,2,1,0:T(8,128)S(1)} %get-tuple-element.80), channel_id=1, source_target_pairs={{4,0},{8,4},{12,8},{5,1},{9,5},{13,9},{6,2},{10,6},{14,10},{7,3},{... | collective-permute-start | bytes 294920 | tf_op jit(solution)/shard_map/ppermute | solution.py:24
  2.9 8.5 %collective-permute-start = (f32[6,2,16,128]{3,2,1,0:T(8,128)S(1)}, f32[6,2,16,128]{3,2,1,0:T(8,128)S(1)}, u32[]{:S(2)}, u32[]{:S(2)}) collective-permute-start(f32[6,2,16,128]{3,2,1,0:T(8,128)S(1)} %get-tuple-element.81), channel_id=1, source_target_pairs={{0,4},{4,8},{8,12},{1,5},{5,9},{9,13},{2,6},{6,10},{10,14},{3,7},{... | collective-permute-start | bytes 294920 | tf_op jit(solution)/shard_map/ppermute | solution.py:22
  12.5 5.8 %collective-permute-start.2 = (f32[6,12,2,128]{3,2,1,0:T(2,128)S(1)}, f32[6,12,2,128]{3,2,1,0:T(2,128)S(1)}, u32[]{:S(2)}, u32[]{:S(2)}) collective-permute-start(f32[6,12,2,128]{3,2,1,0:T(2,128)S(1)} %get-tuple-element.70), channel_id=1, source_target_pairs={{0,2},{1,3},{4,6},{5,7},{8,10},{9,11},{12,14},{13,15},{16,18},{17,... | collective-permute-start | bytes 221192 | tf_op jit(solution)/shard_map/ppermute | solution.py:22
  16.4 6.2 %collective-permute-start.3 = (f32[6,12,2,128]{3,2,1,0:T(2,128)S(1)}, f32[6,12,2,128]{3,2,1,0:T(2,128)S(1)}, u32[]{:S(2)}, u32[]{:S(2)}) collective-permute-start(f32[6,12,2,128]{3,2,1,0:T(2,128)S(1)} %get-tuple-element.71), channel_id=1, source_target_pairs={{2,0},{3,1},{6,4},{7,5},{10,8},{11,9},{14,12},{15,13},{18,16},{19,... | collective-permute-start | bytes 221192 | tf_op jit(solution)/shard_map/ppermute | solution.py:24
  24.2 8.0 %collective-permute-start.5 = (f32[6,12,20,2]{2,3,1,0:T(2,128)S(1)}, f32[6,12,20,2]{2,3,1,0:T(2,128)S(1)}, u32[]{:S(2)}, u32[]{:S(2)}) collective-permute-start(f32[6,12,20,2]{2,3,1,0:T(2,128)S(1)} %copy.162), channel_id=1, source_target_pairs={{1,0},{3,2},{5,4},{7,6},{9,8},{11,10},{13,12},{15,14},{17,16},{19,... | collective-permute-start | bytes 34568 | tf_op jit(solution)/shard_map/ppermute | solution.py:24
  25.5 6.1 %collective-permute-start.4 = (f32[6,12,20,2]{2,3,1,0:T(2,128)S(1)}, f32[6,12,20,2]{2,3,1,0:T(2,128)S(1)}, u32[]{:S(2)}, u32[]{:S(2)}) collective-permute-start(f32[6,12,20,2]{2,3,1,0:T(2,128)S(1)} %copy.161), channel_id=1, source_target_pairs={{0,1},{2,3},{4,5},{6,7},{8,9},{10,11},{12,13},{14,15},{16,17},{18,... | collective-permute-start | bytes 34568 | tf_op jit(solution)/shard_map/ppermute | solution.py:22
  36.1 5.3 %collective-permute-start.6 = (f32[3,2,16,128]{3,2,1,0:T(8,128)S(1)}, f32[3,2,16,128]{3,2,1,0:T(8,128)S(1)}, u32[]{:S(2)}, u32[]{:S(2)}) collective-permute-start(f32[3,2,16,128]{3,2,1,0:T(8,128)S(1)} %get-tuple-element.105), channel_id=1, source_target_pairs={{0,4},{4,8},{8,12},{1,5},{5,9},{9,13},{2,6},{6,10},{10,14},{3,7},{... | collective-permute-start | bytes 147464 | tf_op jit(solution)/shard_map/ppermute | solution.py:22
  39.7 6.0 %collective-permute-start.7 = (f32[3,2,16,128]{3,2,1,0:T(8,128)S(1)}, f32[3,2,16,128]{3,2,1,0:T(8,128)S(1)}, u32[]{:S(2)}, u32[]{:S(2)}) collective-permute-start(f32[3,2,16,128]{3,2,1,0:T(8,128)S(1)} %get-tuple-element.106), channel_id=1, source_target_pairs={{4,0},{8,4},{12,8},{5,1},{9,5},{13,9},{6,2},{10,6},{14,10},{7,3},{... | collective-permute-start | bytes 147464 | tf_op jit(solution)/shard_map/ppermute | solution.py:24
  45.7 3.2 %collective-permute-start.8 = (f32[3,12,2,128]{3,2,1,0:T(2,128)S(1)}, f32[3,12,2,128]{3,2,1,0:T(2,128)S(1)}, u32[]{:S(2)}, u32[]{:S(2)}) collective-permute-start(f32[3,12,2,128]{3,2,1,0:T(2,128)S(1)} %get-tuple-element.96), channel_id=1, source_target_pairs={{0,2},{1,3},{4,6},{5,7},{8,10},{9,11},{12,14},{13,15},{16,18},{17,... | collective-permute-start | bytes 110600 | tf_op jit(solution)/shard_map/ppermute | solution.py:22
  47.3 5.9 %collective-permute-start.9 = (f32[3,12,2,128]{3,2,1,0:T(2,128)S(1)}, f32[3,12,2,128]{3,2,1,0:T(2,128)S(1)}, u32[]{:S(2)}, u32[]{:S(2)}) collective-permute-start(f32[3,12,2,128]{3,2,1,0:T(2,128)S(1)} %get-tuple-element.97), channel_id=1, source_target_pairs={{2,0},{3,1},{6,4},{7,5},{10,8},{11,9},{14,12},{15,13},{18,16},{19,... | collective-permute-start | bytes 110600 | tf_op jit(solution)/shard_map/ppermute | solution.py:24
  53.4 2.7 %collective-permute-start.10 = (f32[3,12,20,2]{3,2,1,0:T(8,128)S(1)}, f32[3,12,20,2]{3,2,1,0:T(8,128)S(1)}, u32[]{:S(2)}, u32[]{:S(2)}) collective-permute-start(f32[3,12,20,2]{3,2,1,0:T(8,128)S(1)} %get-tuple-element.74), channel_id=1, source_target_pairs={{0,1},{2,3},{4,5},{6,7},{8,9},{10,11},{12,13},{14,15},{16,17},{18,... | collective-permute-start | bytes 17288 | tf_op jit(solution)/shard_map/ppermute | solution.py:22
  54.7 3.7 %collective-permute-start.11 = (f32[3,12,20,2]{3,2,1,0:T(8,128)S(1)}, f32[3,12,20,2]{3,2,1,0:T(8,128)S(1)}, u32[]{:S(2)}, u32[]{:S(2)}) collective-permute-start(f32[3,12,20,2]{3,2,1,0:T(8,128)S(1)} %get-tuple-element.75), channel_id=1, source_target_pairs={{1,0},{3,2},{5,4},{7,6},{9,8},{11,10},{13,12},{15,14},{17,16},{19,... | collective-permute-start | bytes 17288 | tf_op jit(solution)/shard_map/ppermute | solution.py:24
  60.4 5.8 %collective-permute-start.12 = (f32[6,2,16,128]{3,2,1,0:T(8,128)S(1)}, f32[6,2,16,128]{3,2,1,0:T(8,128)S(1)}, u32[]{:S(2)}, u32[]{:S(2)}) collective-permute-start(f32[6,2,16,128]{3,2,1,0:T(8,128)S(1)} %get-tuple-element.76), channel_id=1, source_target_pairs={{0,4},{4,8},{8,12},{1,5},{5,9},{9,13},{2,6},{6,10},{10,14},{3,7},{... | collective-permute-start | bytes 294920 | tf_op jit(solution)/shard_map/ppermute | solution.py:22
  63.9 6.5 %collective-permute-start.13 = (f32[6,2,16,128]{3,2,1,0:T(8,128)S(1)}, f32[6,2,16,128]{3,2,1,0:T(8,128)S(1)}, u32[]{:S(2)}, u32[]{:S(2)}) collective-permute-start(f32[6,2,16,128]{3,2,1,0:T(8,128)S(1)} %get-tuple-element.77), channel_id=1, source_target_pairs={{4,0},{8,4},{12,8},{5,1},{9,5},{13,9},{6,2},{10,6},{14,10},{7,3},{... | collective-permute-start | bytes 294920 | tf_op jit(solution)/shard_map/ppermute | solution.py:24
  70.5 3.6 %collective-permute-start.14 = (f32[6,12,2,128]{3,2,1,0:T(2,128)S(1)}, f32[6,12,2,128]{3,2,1,0:T(2,128)S(1)}, u32[]{:S(2)}, u32[]{:S(2)}) collective-permute-start(f32[6,12,2,128]{3,2,1,0:T(2,128)S(1)} %get-tuple-element.68), channel_id=1, source_target_pairs={{0,2},{1,3},{4,6},{5,7},{8,10},{9,11},{12,14},{13,15},{16,18},{17,... | collective-permute-start | bytes 221192 | tf_op jit(solution)/shard_map/ppermute | solution.py:22
  72.1 6.2 %collective-permute-start.15 = (f32[6,12,2,128]{3,2,1,0:T(2,128)S(1)}, f32[6,12,2,128]{3,2,1,0:T(2,128)S(1)}, u32[]{:S(2)}, u32[]{:S(2)}) collective-permute-start(f32[6,12,2,128]{3,2,1,0:T(2,128)S(1)} %get-tuple-element.69), channel_id=1, source_target_pairs={{2,0},{3,1},{6,4},{7,5},{10,8},{11,9},{14,12},{15,13},{18,16},{19,... | collective-permute-start | bytes 221192 | tf_op jit(solution)/shard_map/ppermute | solution.py:24
  79.9 11.3 %collective-permute-start.17 = (f32[6,12,20,2]{2,3,1,0:T(2,128)S(1)}, f32[6,12,20,2]{2,3,1,0:T(2,128)S(1)}, u32[]{:S(2)}, u32[]{:S(2)}) collective-permute-start(f32[6,12,20,2]{2,3,1,0:T(2,128)S(1)} %copy.167), channel_id=1, source_target_pairs={{1,0},{3,2},{5,4},{7,6},{9,8},{11,10},{13,12},{15,14},{17,16},{19,... | collective-permute-start | bytes 34568 | tf_op jit(solution)/shard_map/ppermute | solution.py:24
  81.2 9.5 %collective-permute-start.16 = (f32[6,12,20,2]{2,3,1,0:T(2,128)S(1)}, f32[6,12,20,2]{2,3,1,0:T(2,128)S(1)}, u32[]{:S(2)}, u32[]{:S(2)}) collective-permute-start(f32[6,12,20,2]{2,3,1,0:T(2,128)S(1)} %copy.166), channel_id=1, source_target_pairs={{0,1},{2,3},{4,5},{6,7},{8,9},{10,11},{12,13},{14,15},{16,17},{18,... | collective-permute-start | bytes 34568 | tf_op jit(solution)/shard_map/ppermute | solution.py:22
  95.1 5.2 %collective-permute-start.18 = (f32[3,2,16,128]{3,2,1,0:T(8,128)S(1)}, f32[3,2,16,128]{3,2,1,0:T(8,128)S(1)}, u32[]{:S(2)}, u32[]{:S(2)}) collective-permute-start(f32[3,2,16,128]{3,2,1,0:T(8,128)S(1)} %get-tuple-element.103), channel_id=1, source_target_pairs={{0,4},{4,8},{8,12},{1,5},{5,9},{9,13},{2,6},{6,10},{10,14},{3,7},{... | collective-permute-start | bytes 147464 | tf_op jit(solution)/shard_map/ppermute | solution.py:22
  98.6 6.0 %collective-permute-start.19 = (f32[3,2,16,128]{3,2,1,0:T(8,128)S(1)}, f32[3,2,16,128]{3,2,1,0:T(8,128)S(1)}, u32[]{:S(2)}, u32[]{:S(2)}) collective-permute-start(f32[3,2,16,128]{3,2,1,0:T(8,128)S(1)} %get-tuple-element.104), channel_id=1, source_target_pairs={{4,0},{8,4},{12,8},{5,1},{9,5},{13,9},{6,2},{10,6},{14,10},{7,3},{... | collective-permute-start | bytes 147464 | tf_op jit(solution)/shard_map/ppermute | solution.py:24
  104.6 20.3 %collective-permute-start.20 = (f32[3,12,2,128]{3,2,1,0:T(2,128)S(1)}, f32[3,12,2,128]{3,2,1,0:T(2,128)S(1)}, u32[]{:S(2)}, u32[]{:S(2)}) collective-permute-start(f32[3,12,2,128]{3,2,1,0:T(2,128)S(1)} %get-tuple-element.88), channel_id=1, source_target_pairs={{0,2},{1,3},{4,6},{5,7},{8,10},{9,11},{12,14},{13,15},{16,18},{17,... | collective-permute-start | bytes 110600 | tf_op jit(solution)/shard_map/ppermute | solution.py:22
  106.2 18.7 %collective-permute-start.21 = (f32[3,12,2,128]{3,2,1,0:T(2,128)S(1)}, f32[3,12,2,128]{3,2,1,0:T(2,128)S(1)}, u32[]{:S(2)}, u32[]{:S(2)}) collective-permute-start(f32[3,12,2,128]{3,2,1,0:T(2,128)S(1)} %get-tuple-element.89), channel_id=1, source_target_pairs={{2,0},{3,1},{6,4},{7,5},{10,8},{11,9},{14,12},{15,13},{18,16},{19,... | collective-permute-start | bytes 110600 | tf_op jit(solution)/shard_map/ppermute | solution.py:24
  125.1 2.7 %collective-permute-start.22 = (f32[3,12,20,2]{3,2,1,0:T(8,128)S(1)}, f32[3,12,20,2]{3,2,1,0:T(8,128)S(1)}, u32[]{:S(2)}, u32[]{:S(2)}) collective-permute-start(f32[3,12,20,2]{3,2,1,0:T(8,128)S(1)} %get-tuple-element.72), channel_id=1, source_target_pairs={{0,1},{2,3},{4,5},{6,7},{8,9},{10,11},{12,13},{14,15},{16,17},{18,... | collective-permute-start | bytes 17288 | tf_op jit(solution)/shard_map/ppermute | solution.py:22
  126.4 3.7 %collective-permute-start.23 = (f32[3,12,20,2]{3,2,1,0:T(8,128)S(1)}, f32[3,12,20,2]{3,2,1,0:T(8,128)S(1)}, u32[]{:S(2)}, u32[]{:S(2)}) collective-permute-start(f32[3,12,20,2]{3,2,1,0:T(8,128)S(1)} %get-tuple-element.73), channel_id=1, source_target_pairs={{1,0},{3,2},{5,4},{7,6},{9,8},{11,10},{13,12},{15,14},{17,16},{19,... | collective-permute-start | bytes 17288 | tf_op jit(solution)/shard_map/ppermute | solution.py:24
  (8 other events, 94.8 us)
where the time goes:
time: 160 us; the launch traced here: 159 us
  starting transfers between devices  49.1 us (31%)
  local copies, waits for them, and re-layouts  48.2 us (30%)
  waiting for transfers between devices  32.5 us (20%)
  other arithmetic  16.3 us (10%)
  blocking collectives  11.1 us (7%)
  between operations  2.09 us (1%)
    ppermute x12, starting transfers between devices, extended(): lax.ppermute(tail, axis, [(i, (i + 1) % count) for i in range(ends)])  33.6 us
    ppermute x12, waiting for transfers between devices, extended(): lax.ppermute(head, axis, [((i + 1) % count, i) for i in range(ends)])  30.1 us
    ppermute x12, starting transfers between devices, extended(): lax.ppermute(head, axis, [((i + 1) % count, i) for i in range(ends)])  15.5 us
    gather x4, local copies, waits for them, and re-layouts, sample(): points = stress.reshape(6, -1)[:, cells]  12.7 us
    all_to_all x1, blocking collectives, per_device(): lax.all_to_all(outgoing, ('gx', 'gy'), split_axis=1, concat_axis=1, tiled...  11.1 us
    concatenate x2, local copies, waits for them, and re-layouts, stress_update(): return jnp.concatenate([normal, sliding], axis=0)  9.61 us
    gather x1, local copies, waits for them, and re-layouts, per_device(): lame_points = material[0].reshape(-1)[cells]  6.15 us
    gather x1, local copies, waits for them, and re-layouts, per_device(): shear_points = material[1].reshape(-1)[cells]  6.15 us
  transfers between devices with their start and end apart: 24, of which 12 were waited for; matrix products, arithmetic and copies ran while one was open for 20% of the time, Pallas kernels for 0%

commit v1 on v0

v1 whole, which is shorter than its diff:
```python
import jax
import jax.numpy as jnp
from jax import lax
from jax.experimental import pallas as pl
from jax.experimental.pallas import tpu as pltpu
from jax.sharding import PartitionSpec as P

STEPS = 2
TIME_STEP = 0.12

SXX, SYY, SZZ, SXY, SXZ, SYZ, VX, VY, VZ, LAM, MU, BUOY = range(12)
FIELDS = 12
DEPTHS = (6, 5, 5, 6, 6, 5, 5, 5, 5, 3, 3, 5)
OFFSETS = tuple(sum(DEPTHS[:f]) for f in range(FIELDS + 1))
HALO = 6
LAYERS = OFFSETS[-1]
ROWS = 8
STRIP = 8
LANES = 128
CORNER_WHOLE = tuple((f, d) for f in (SXX, SYY, SXY, SXZ, SYZ) for d in (1, 2))
CORNER_HALF = (
    tuple((f, d) for f in (SXX, SYY, SXY, SXZ, SYZ) for d in (3, 4, 5))
    + tuple((f, d) for f in (SZZ, VX, VY, VZ, BUOY) for d in (1, 2, 3))
    + tuple((f, d) for f in (LAM, MU) for d in (1, 2))
)
CORNERS = len(CORNER_WHOLE) + (len(CORNER_HALF) + 1) // 2
VMEM_LIMIT = 40 * 1024 * 1024
VMEM = pl.BlockSpec(memory_space=pltpu.VMEM)
SMEM = pl.BlockSpec(memory_space=pltpu.SMEM)


def f32(*shape):
    return jax.ShapeDtypeStruct(shape, jnp.float32)


def groups(count):
    return -(-count // (LANES // STRIP))


def iota(dimension, shape=(ROWS, LANES)):
    return lax.broadcasted_iota(jnp.int32, shape, dimension)


def pack_strips(tiles, head):
    slot = iota(1) // STRIP
    packed = None
    for at, tile in enumerate(tiles):
        turned = pltpu.roll(tile, (STRIP * at + head) & (LANES - 1), 1)
        packed = turned if packed is None else jnp.where(slot == at, turned, packed)
    return packed


def source(refs, field):
    stress, velocity, material = refs
    if field < VX:
        return stress, field
    if field < LAM:
        return velocity, field - VX
    return material, field - LAM


class Grid:
    def __init__(self, block, counts):
        self.cx, self.cy, self.cz = block
        self.gx, self.gy, self.gz = counts
        self.x_pairs = ("even", "odd") if self.gx > 2 else ("even",)
        self.y_pairs = ("even", "odd") if self.gy > 2 else ("even",)
        self.rows = self.cy + ROWS * len(self.y_pairs)
        self.layers = self.cx + 2 * HALO
        self.tiles_y = self.cy // ROWS

    def pairs(self, count, kind):
        start = 0 if kind == "even" else 1
        out = []
        for i in range(start, count - 1, 2):
            out += [(i, i + 1), (i + 1, i)]
        return out

    def pieces(self):
        out = [(("x", a), LAYERS * self.tiles_y) for a in self.x_pairs]
        out += [(("y", b), FIELDS * self.cx) for b in self.y_pairs]
        out += [(("d", a, b), CORNERS) for b in self.y_pairs for a in self.x_pairs]
        return out

    def shape(self, name):
        if name[0] == "x":
            return (LAYERS, self.cy, self.cz)
        if name[0] == "y":
            return (FIELDS, self.cx, ROWS, self.cz)
        return (CORNERS, ROWS, self.cz)


def above(axis, kind):
    parity = lax.rem(lax.axis_index(axis), 2)
    return parity == (0 if kind == "even" else 1)


def pack_kernel(grid, *refs):
    sources = refs[:3]
    outs = refs[3:]
    own = outs[-1]
    sub = iota(0)
    for (name, _), out in zip(grid.pieces(), outs):
        if name[0] == "x":
            high = above("gx", name[1])
            for f in range(FIELDS):
                ref, at = source(sources, f)
                n = DEPTHS[f]
                start = jnp.where(high, grid.cx - n, 0)
                out[OFFSETS[f] : OFFSETS[f + 1]] = ref[at, pl.ds(start, n)]
        elif name[0] == "y":
            row = pl.multiple_of(jnp.where(above("gy", name[1]), grid.cy - ROWS, 0), ROWS)
            for f in range(FIELDS):
                ref, at = source(sources, f)
                out[f] = ref[at, :, pl.ds(row, ROWS), :]
        else:
            high = above("gx", name[1])
            up = above("gy", name[2])
            row = pl.multiple_of(jnp.where(up, grid.cy - ROWS, 0), ROWS)

            def tile(field, distance):
                ref, at = source(sources, field)
                layer = jnp.where(high, grid.cx - distance, distance - 1)
                return ref[at, layer, pl.ds(row, ROWS), :]

            for i, (f, d) in enumerate(CORNER_WHOLE):
                out[i] = tile(f, d)
            for i in range(0, len(CORNER_HALF), 2):
                first = tile(*CORNER_HALF[i])
                second = tile(*CORNER_HALF[min(i + 1, len(CORNER_HALF) - 1)])
                turned = pltpu.roll(jnp.where(up, first, second), 4, 0)
                lower = jnp.where(up, turned, first)
                upper = jnp.where(up, second, turned)
                out[len(CORNER_WHOLE) + i // 2] = jnp.where(sub < 4, lower, upper)
    head = jnp.where(lax.axis_index("gz") == 0, STRIP, 0)
    tiles = [(f, x, r) for f in range(FIELDS) for x in range(grid.cx) for r in range(grid.tiles_y)]
    for g in range(groups(len(tiles))):
        part = []
        for f, x, r in tiles[16 * g : 16 * g + 16]:
            ref, at = source(sources, f)
            part.append(ref[at, x, ROWS * r : ROWS * r + ROWS, :])
        own[g] = pack_strips(part, head)


def piece_tile(name, ref, at, grid):
    if name[0] == "x":
        r = at % grid.tiles_y
        return ref[at // grid.tiles_y, ROWS * r : ROWS * r + ROWS, :]
    if name[0] == "y":
        return ref[at // grid.cx, at % grid.cx]
    return ref[at]


def strip_kernel(grid, *refs):
    out = refs[-1]
    head = jnp.where(lax.axis_index("gz") == 0, STRIP, 0)
    base = 0
    for (name, count), ref in zip(grid.pieces(), refs[:-1]):
        for g in range(groups(count)):
            tiles = [
                piece_tile(name, ref, at, grid) for at in range(16 * g, min(16 * g + 16, count))
            ]
            out[base + g] = pack_strips(tiles, head)
        base += groups(count)


def slot_kernel(width, capacity, cz, cells_ref, writers_ref, lanes_ref, rows_ref):
    count = cells_ref.shape[1]
    cells = cells_ref[...]
    writers = writers_ref[...]
    padded = max(16, width)
    named = (iota(0, (padded, count)) == writers).astype(jnp.float32)
    earlier = (iota(0, (count, count)) < iota(1, (count, count))).astype(jnp.float32)
    before = jnp.dot(
        named.astype(jnp.bfloat16), earlier.astype(jnp.bfloat16), preferred_element_type=jnp.float32
    )
    position = jnp.sum(before * named, axis=0, keepdims=True).astype(jnp.int32)
    target = writers * capacity + position
    which = iota(0, (16, count))
    lane = lax.rem(cells, cz)
    row = lax.div(cells, cz)
    values = jnp.where(which == 0, lane, jnp.where(which == 1, row, jnp.where(which == 2, 1, 0)))
    values = values.astype(jnp.float32).astype(jnp.bfloat16)
    step = 256
    for n in range(width * capacity // step):
        hit = (iota(0, (step, count)) + n * step == target).astype(jnp.float32)
        table = lax.dot_general(
            values,
            hit.astype(jnp.bfloat16),
            (((1,), (1,)), ((), ())),
            preferred_element_type=jnp.float32,
        )
        lane_of = jnp.where(table[2:3] > 0.5, table[0:1], -1.0).astype(jnp.int32)
        marks = (iota(0, (cz, step)) == lane_of).astype(jnp.float32).astype(jnp.bfloat16)
        lanes_ref[0:cz, n * step : (n + 1) * step] = marks
        lanes_ref[cz : 2 * cz, n * step : (n + 1) * step] = marks
        rows_ref[:, n * step : (n + 1) * step] = jnp.broadcast_to(
            table[1:2].astype(jnp.int32), (ROWS, step)
        )


def main_kernel(grid, *refs):
    pieces = grid.pieces()
    n = len(pieces)
    sources = refs[:3]
    own_strips = refs[3]
    arrived = refs[4 : 4 + n]
    strips, lanes_ref, rows_ref, site_ref, wavelet_ref = refs[4 + n : 9 + n]
    velocity_out, table_out = refs[9 + n : 11 + n]
    ext, sampled = refs[11 + n :]
    rows = grid.rows
    cx, cy, cz = grid.cx, grid.cy, grid.cz
    half = lax.axis_index("gz")
    other = 1 - half
    sub = iota(0)
    lead = jnp.where(half == 0, 0, LANES - STRIP)

    def edge(up):
        if len(grid.y_pairs) > 1:
            return lambda tile: tile
        low, top = jnp.where(up, 6, 0), jnp.where(up, 8, 2)
        keep = jnp.logical_or(sub < low, sub >= top)
        return lambda tile: jnp.where(keep, tile, 0.0)

    def row_of(up):
        if len(grid.y_pairs) == 1:
            return cy
        return pl.multiple_of(jnp.where(up, cy, cy + ROWS), ROWS)

    for f in range(FIELDS):
        for x in list(range(HALO)) + list(range(HALO + cx, grid.layers)):
            for h in range(2):
                ext[f, h, x, cy:rows, :] = jnp.zeros((rows - cy, cz), jnp.float32)

    def unpack(ref, base, at):
        return pltpu.roll(ref[base + at // 16], (lead - STRIP * (at % 16)) & (LANES - 1), 1)

    at = 0
    for f in range(FIELDS):
        ref, k = source(sources, f)
        for x in range(cx):
            ext[f, half, HALO + x, 0:cy, :] = ref[k, x]
            for r in range(grid.tiles_y):
                ext[f, other, HALO + x, ROWS * r : ROWS * r + ROWS, :] = unpack(own_strips, 0, at)
                at += 1
    base = 0
    for (name, count), ref in zip(pieces, arrived):
        if name[0] == "x":
            high = above("gx", name[1])
            at = 0
            for f in range(FIELDS):
                start = jnp.where(high, HALO + cx, HALO - DEPTHS[f])
                for d in range(DEPTHS[f]):
                    ext[f, half, start + d, 0:cy, :] = ref[OFFSETS[f] + d]
                    for r in range(grid.tiles_y):
                        ext[f, other, start + d, ROWS * r : ROWS * r + ROWS, :] = unpack(
                            strips, base, at
                        )
                        at += 1
        elif name[0] == "y":
            up = above("gy", name[1])
            clear = edge(up)
            place = row_of(up)
            for f in range(FIELDS):
                for x in range(cx):
                    ext[f, half, HALO + x, pl.ds(place, ROWS), :] = clear(ref[f, x])
                    ext[f, other, HALO + x, pl.ds(place, ROWS), :] = clear(
                        unpack(strips, base, f * cx + x)
                    )
        else:
            high = above("gx", name[1])
            up = above("gy", name[2])
            clear = edge(up)
            place = row_of(up)

            def put(h, field, distance, tile):
                layer = jnp.where(high, HALO + cx - 1 + distance, HALO - distance)
                ext[field, h, layer, pl.ds(place, ROWS), :] = clear(tile)

            for h, tile_of in ((half, lambda i: ref[i]), (other, lambda i: unpack(strips, base, i))):
                for i, (f, d) in enumerate(CORNER_WHOLE):
                    put(h, f, d, tile_of(i))
                for i in range(0, len(CORNER_HALF), 2):
                    tile = tile_of(len(CORNER_WHOLE) + i // 2)
                    turned = pltpu.roll(tile, 4, 0)
                    put(h, *CORNER_HALF[i], jnp.where(up, tile, turned))
                    if i + 1 < len(CORNER_HALF):
                        put(h, *CORNER_HALF[i + 1], jnp.where(up, turned, tile))
        base += groups(count)

    lane_all = iota(1, (rows, cz))
    lane = iota(1)

    def pair(field, x):
        return ext[field, 0, x], ext[field, 1, x]

    def add(a, b):
        return a[0] + b[0], a[1] + b[1]

    def sub_(a, b):
        return a[0] - b[0], a[1] - b[1]

    def along_x(field, x):
        return (
            sub_(pair(field, x + 1), pair(field, x)),
            sub_(pair(field, x + 2), pair(field, x - 1)),
        )

    def moved_y(a, offset):
        return tuple(pltpu.roll(v, -offset % rows, 0) for v in a)

    def moved_z(a, offset):
        low = pltpu.roll(a[0], -offset % cz, 1)
        high = pltpu.roll(a[1], -offset % cz, 1)
        if offset > 0:
            inside = lane_all < cz - offset
            return jnp.where(inside, low, high), jnp.where(inside, high, 0.0)
        inside = lane_all >= -offset
        return jnp.where(inside, low, 0.0), jnp.where(inside, high, low)

    def forward(a, move):
        return sub_(move(a, 1), a), sub_(move(a, 2), move(a, -1))

    def backward(a, move):
        return sub_(a, move(a, -1)), sub_(move(a, 1), move(a, -2))

    def total(*terms):
        near, far = terms[0]
        for other_near, other_far in terms[1:]:
            near, far = add(near, other_near), add(far, other_far)
        return tuple(27.0 * p - q for p, q in zip(near, far))

    scale = TIME_STEP / 24.0

    def velocity_layer(x):
        y = x + 1
        sxy_x, sxz_x = pair(SXY, x), pair(SXZ, x)
        rate_x = total(along_x(SXX, x), backward(sxy_x, moved_y), backward(sxz_x, moved_z))
        syz = pair(SYZ, y)
        rate_y = total(
            along_x(SXY, y - 1), forward(pair(SYY, y), moved_y), backward(syz, moved_z)
        )
        rate_z = total(
            along_x(SXZ, y - 1), backward(syz, moved_y), forward(pair(SZZ, y), moved_z)
        )
        for h in range(2):
            b = scale * ext[BUOY, h, x]
            ext[VX, h, x] = ext[VX, h, x] + b * rate_x[h]
            b = scale * ext[BUOY, h, y]
            ext[VY, h, y] = ext[VY, h, y] + b * rate_y[h]
            ext[VZ, h, y] = ext[VZ, h, y] + b * rate_z[h]

    def stress_layer(x):
        vx, vy, vz = pair(VX, x), pair(VY, x), pair(VZ, x)
        gxx = total(along_x(VX, x - 1))
        gyy = total(backward(vy, moved_y))
        gzz = total(backward(vz, moved_z))
        gxy = total(forward(vx, moved_y), along_x(VY, x))
        gxz = total(forward(vx, moved_z), along_x(VZ, x))
        gyz = total(forward(vy, moved_z), forward(vz, moved_y))
        for h in range(2):
            shear = scale * ext[MU, h, x]
            volume = scale * ext[LAM, h, x] * (gxx[h] + gyy[h] + gzz[h])
            twice = 2.0 * shear
            ext[SXX, h, x] = ext[SXX, h, x] + (twice * gxx[h] + volume)
            ext[SYY, h, x] = ext[SYY, h, x] + (twice * gyy[h] + volume)
            ext[SZZ, h, x] = ext[SZZ, h, x] + (twice * gzz[h] + volume)
            ext[SXY, h, x] = ext[SXY, h, x] + shear * gxy[h]
            ext[SXZ, h, x] = ext[SXZ, h, x] + shear * gxz[h]
            ext[SYZ, h, x] = ext[SYZ, h, x] + shear * gyz[h]

    def loop(first, last, body):
        def step(x, carry):
            body(x)
            return carry

        lax.fori_loop(HALO + first, HALO + last + 1, step, 0)

    site = site_ref[0]
    total_y, total_z = cy * grid.gy, cz * grid.gz
    site_x = lax.div(site, total_y * total_z) - lax.axis_index("gx") * cx
    site_y = lax.rem(lax.div(site, total_z), total_y) - lax.axis_index("gy") * cy
    site_z = lax.rem(site, total_z)
    near = jnp.logical_and(site_x >= -HALO, site_x < cx + HALO)
    near = jnp.logical_and(near, jnp.logical_and(site_y >= -ROWS, site_y < cy + ROWS))
    site_row = jnp.where(site_y < 0, site_y + rows, site_y)

    def inject(step):
        @pl.when(near)
        def _():
            h = lax.div(site_z, cz)
            x = site_x + HALO
            row = pl.multiple_of(lax.div(site_row, ROWS) * ROWS, ROWS)
            here = jnp.logical_and(sub == lax.rem(site_row, ROWS), lane == lax.rem(site_z, cz))
            amount = jnp.where(here, TIME_STEP * ext[BUOY, h, x, pl.ds(row, ROWS), :], 0.0)
            for c in range(3):
                ext[VX + c, h, x, pl.ds(row, ROWS), :] = (
                    ext[VX + c, h, x, pl.ds(row, ROWS), :] + amount * wavelet_ref[step, c]
                )

    def strain_layer(x):
        lam = ext[LAM, half, x, 0:cy, :]
        shear = ext[MU, half, x, 0:cy, :]
        parts = [ext[f, half, x, 0:cy, :] for f in range(6)]
        shrink = lam / (3.0 * lam + 2.0 * shear) * (parts[0] + parts[1] + parts[2])
        inverse = 0.5 / shear
        for f in range(6):
            value = (parts[f] - shrink if f < 3 else parts[f]) * inverse
            head = value.astype(jnp.bfloat16)
            tail = (value - head.astype(jnp.float32)).astype(jnp.bfloat16)
            row = pl.multiple_of(f * cx * cy + (x - HALO) * cy, cy)
            sampled[pl.ds(row, cy), 0:cz] = head
            sampled[pl.ds(row, cy), cz : 2 * cz] = tail

    step_slots = 256
    block = cx * cy

    def sample(step):
        def body(k, carry):
            where = pl.ds(pl.multiple_of(k * step_slots, step_slots), step_slots)
            found = jnp.dot(
                sampled[...], lanes_ref[:, where], preferred_element_type=jnp.float32
            )
            row = rows_ref[:, where]
            for f in range(6):
                acc = jnp.zeros((ROWS, step_slots), jnp.float32)
                for r in range(block // ROWS):
                    tile = found[f * block + r * ROWS : f * block + r * ROWS + ROWS]
                    acc = acc + jnp.where(row == r * ROWS + iota(0, (ROWS, step_slots)), tile, 0.0)
                table_out[k, step * 6 + f : step * 6 + f + 1, :] = jnp.sum(
                    acc, axis=0, keepdims=True
                )
            return carry

        lax.fori_loop(0, lanes_ref.shape[1] // step_slots, body, 0)

    velocity_ranges = ((-5, cx + 3), (-2, cx))
    stress_ranges = ((-3, cx + 2), (0, cx - 1))
    for step in range(STEPS):
        loop(*velocity_ranges[step], velocity_layer)
        inject(step)
        loop(*stress_ranges[step], stress_layer)
        loop(0, cx - 1, strain_layer)
        sample(step)
    for c in range(3):
        for x in range(cx):
            velocity_out[c, x] = ext[VX + c, half, HALO + x, 0:cy, :]


def per_device(
    velocity_start, stress_start, material, force_site, force_wavelet, save_cells, save_writer
):
    counts = tuple(lax.axis_size(axis) for axis in ("gx", "gy", "gz"))
    grid = Grid(velocity_start.shape[1:], counts)
    pieces = grid.pieces()
    params = pltpu.CompilerParams(vmem_limit_bytes=VMEM_LIMIT)
    own_tiles = FIELDS * grid.cx * grid.tiles_y
    sources = (stress_start, velocity_start, material)
    packed = pl.pallas_call(
        lambda *refs: pack_kernel(grid, *refs),
        out_shape=[f32(*grid.shape(name)) for name, _ in pieces]
        + [f32(groups(own_tiles), ROWS, LANES)],
        in_specs=[VMEM] * 3,
        out_specs=[VMEM] * (len(pieces) + 1),
        compiler_params=params,
        name="pack_halos",
    )(*sources)
    swap = [(0, 1), (1, 0)]
    arrived = []
    for (name, _), piece in zip(pieces, packed):
        if name[0] == "x":
            arrived.append(lax.ppermute(piece, "gx", grid.pairs(grid.gx, name[1])))
        elif name[0] == "y":
            arrived.append(lax.ppermute(piece, "gy", grid.pairs(grid.gy, name[1])))
        else:
            pairs = [
                (a * grid.gy + b, c * grid.gy + d)
                for a, c in grid.pairs(grid.gx, name[1])
                for b, d in grid.pairs(grid.gy, name[2])
            ]
            arrived.append(lax.ppermute(piece, ("gx", "gy"), pairs))
    own_strips = lax.ppermute(packed[-1], "gz", swap)

    count = save_cells.size
    width = grid.gx * grid.gy
    capacity = max(2, 2 * count // width)
    slots = width * capacity
    lanes, rows = pl.pallas_call(
        lambda *refs: slot_kernel(width, capacity, grid.cz, *refs),
        out_shape=[
            jax.ShapeDtypeStruct((2 * grid.cz, slots), jnp.bfloat16),
            jax.ShapeDtypeStruct((ROWS, slots), jnp.int32),
        ],
        in_specs=[VMEM] * 2,
        out_specs=[VMEM] * 2,
        compiler_params=params,
        name="slot_tables",
    )(save_cells.reshape(1, count), save_writer.reshape(1, count))

    strips = pl.pallas_call(
        lambda *refs: strip_kernel(grid, *refs),
        out_shape=f32(sum(groups(c) for _, c in pieces), ROWS, LANES),
        in_specs=[VMEM] * len(pieces),
        out_specs=VMEM,
        compiler_params=params,
        name="pack_strips",
    )(*arrived)
    strips = lax.ppermute(strips, "gz", swap)

    velocity, table = pl.pallas_call(
        lambda *refs: main_kernel(grid, *refs),
        out_shape=[f32(*velocity_start.shape), f32(slots // 256, 6 * STEPS, 256)],
        in_specs=[VMEM] * (4 + len(pieces) + 3) + [SMEM] * 2,
        out_specs=[VMEM] * 2,
        scratch_shapes=[
            pltpu.VMEM((FIELDS, 2, grid.layers, grid.rows, grid.cz), jnp.float32),
            pltpu.VMEM((6 * grid.cx * grid.cy, 2 * grid.cz), jnp.bfloat16),
        ],
        compiler_params=params,
        name="two_steps",
    )(*sources, own_strips, *arrived, strips, lanes, rows, force_site, force_wavelet)

    values = 6 * STEPS
    if capacity != 256:
        table = table.transpose(1, 0, 2).reshape(values, width, capacity).transpose(1, 0, 2)
    sent = lax.all_to_all(table, ("gx", "gy"), split_axis=0, concat_axis=0, tiled=True)
    return velocity, sent.transpose(1, 0, 2).reshape(1, values, slots)


def solution(mesh):
    in_specs = (
        P(None, ("runs", "gx"), "gy", "gz"),
        P(None, ("runs", "gx"), "gy", "gz"),
        P(None, ("runs", "gx"), "gy", "gz"),
        P("runs"),
        P("runs", None),
        P(("runs", "gx"), "gy", "gz", None),
        P(("runs", "gx"), "gy", "gz", None, None),
    )
    out_specs = (P(None, ("runs", "gx"), "gy", "gz"), P(("runs", "gz"), None, ("gx", "gy")))
    return jax.shard_map(
        per_device, mesh=mesh, in_specs=in_specs, out_specs=out_specs, check_vma=False
    )
```

time: 160 us -> 55.3 us (0.35)
  local copies, waits for them, and re-layouts: 48.2 us -> 4.33 us
  starting transfers between devices: 49.1 us -> 11 us
  waiting for transfers between devices: 32.5 us -> 7.13 us
  other arithmetic: 16.3 us -> 0 us
  Pallas kernels: 0 us -> 16.1 us
  blocking collectives: 11.1 us -> 15 us
    ppermute x24 -> x7, starting transfers between devices: 49.1 us -> 11 us  [the longest x2 5.13 us: per_device(): arrived.append(lax.ppermute(piece, ('gx', 'gy'), pairs))]
    ppermute x24 -> x7, waiting for transfers between devices: 32.5 us -> 7.13 us  [the longest x2 7.12 us: per_device(): arrived.append(lax.ppermute(piece, ('gx', 'gy'), pairs))]
    gather x6 -> x0, local copies, waits for them, and re-layouts: 25 us -> none  [the longest x4 12.7 us: sample(): points = stress.reshape(6, -1)[:, cells]]
    pallas_call x0 -> x4, Pallas kernels: none -> 16.1 us  [the longest x1 13.6 us: per_device(): pl.pallas_call(lambda *refs: main_kernel(grid, *refs), out_shape=[f32(*ve...]
    concatenate x4 -> x0, local copies, waits for them, and re-layouts: 9.83 us -> none  [the longest x2 9.61 us: stress_update(): return jnp.concatenate([normal, sliding], axis=0)]
    another operation x15 -> x0, other arithmetic: 8.59 us -> none
    slice x12 -> x0, local copies, waits for them, and re-layouts: 4.2 us -> none  [the longest x9 2.15 us: extended(): lax.slice_in_dim(cells, cells.shape[dim] - width, cells.shape[dim], axis=...]
    all_to_all x1, blocking collectives: 11.1 us -> 15 us  [per_device(): lax.all_to_all(table, ('gx', 'gy'), split_axis=0, concat_axis=0, tiled=True)]
  transfers between devices with their start and end apart: 24 -> 7, of which waited for: 12 -> 1; matrix products, arithmetic and copies ran while one was open for 20% -> 0% of each run, Pallas kernels for 0% -> 3%
where the time goes in v1:
time: 55.3 us; the launch traced here: 55 us
  Pallas kernels  16.1 us (29%)
  blocking collectives  15 us (27%)
  starting transfers between devices  11 us (20%)
  waiting for transfers between devices  7.13 us (13%)
  local copies, waits for them, and re-layouts  4.33 us (8%)
  between operations  1.42 us (3%)
    all_to_all x1, blocking collectives, per_device(): lax.all_to_all(table, ('gx', 'gy'), split_axis=0, concat_axis=0, tiled=True)  15 us
    pallas_call x1, Pallas kernels, per_device(): pl.pallas_call(lambda *refs: main_kernel(grid, *refs), out_shape=[f32(*ve...  13.6 us
    ppermute x2, waiting for transfers between devices, per_device(): arrived.append(lax.ppermute(piece, ('gx', 'gy'), pairs))  7.12 us
    ppermute x2, starting transfers between devices, per_device(): arrived.append(lax.ppermute(piece, ('gx', 'gy'), pairs))  5.13 us
    ppermute x2, starting transfers between devices, per_device(): arrived.append(lax.ppermute(piece, 'gx', grid.pairs(grid.gx, name[1])))  3.77 us
    unnamed x14, local copies, waits for them, and re-layouts  3.52 us
    pallas_call x1, Pallas kernels, per_device(): pl.pallas_call(lambda *refs: slot_kernel(width, capacity, grid.cz, *refs)...  1.69 us
    ppermute x1, starting transfers between devices, per_device(): arrived.append(lax.ppermute(piece, 'gy', grid.pairs(grid.gy, name[1])))  1.55 us
  transfers between devices with their start and end apart: 7, of which 1 were waited for; matrix products, arithmetic and copies ran while one was open for 0% of the time, Pallas kernels for 3%

profile of v1, /device:TPU:0, one launch (start us, length us, event | category | flops | bytes accessed | tf_op | source)
XLA Modules:
  0.0 55.0 jit_solution(8559022660911509480)
XLA Ops:
  0.6 0.0 copy-start
  0.6 1.0 %copy-done = f32[6,8,16,128]{3,2,1,0:T(8,128)S(1)} copy-done((f32[6,8,16,128]{3,2,1,0:T(8,128)S(1)}, f32[6,8,16,128]{3,2,1,0:T(8,128)}, u32[]{:S(2)}) %copy-start) | copy-done | bytes 393240
  1.6 0.9 %copy-done.2 = f32[3,8,16,128]{3,2,1,0:T(8,128)S(1)} copy-done((f32[3,8,16,128]{3,2,1,0:T(8,128)S(1)}, f32[3,8,16,128]{3,2,1,0:T(8,128)}, u32[]{:S(2)}) %copy-start.2) | copy-done | bytes 196632
  2.6 0.9 %copy-done.3 = f32[3,8,16,128]{3,2,1,0:T(8,128)S(1)} copy-done((f32[3,8,16,128]{3,2,1,0:T(8,128)S(1)}, f32[3,8,16,128]{3,2,1,0:T(8,128)}, u32[]{:S(2)}) %copy-start.3) | copy-done | bytes 196632
  3.5 0.4 pack_halos.1
  3.9 3.1 %collective-permute-start.1 = (f32[59,16,128]{2,1,0:T(8,128)S(1)}, f32[59,16,128]{2,1,0:T(8,128)S(1)}, u32[]{:S(2)}, u32[]{:S(2)}) collective-permute-start(f32[59,16,128]{2,1,0:T(8,128)S(1)} %get-tuple-element.13), channel_id=1, source_target_pairs={{0,4},{4,0},{8,12},{12,8},{1,5},{5,1},{9,13},{13,9},{2,6},{6,2},{1... | collective-permute-start | bytes 1449992 | tf_op jit(solution)/shard_map/ppermute | solution.py:472
  7.0 0.7 %collective-permute-start.2 = (f32[59,16,128]{2,1,0:T(8,128)S(1)}, f32[59,16,128]{2,1,0:T(8,128)S(1)}, u32[]{:S(2)}, u32[]{:S(2)}) collective-permute-start(f32[59,16,128]{2,1,0:T(8,128)S(1)} %get-tuple-element.14), channel_id=1, source_target_pairs={{4,8},{8,4},{5,9},{9,5},{6,10},{10,6},{7,11},{11,7},{20,24},{24,20... | collective-permute-start | bytes 1449992 | tf_op jit(solution)/shard_map/ppermute | solution.py:472
  7.6 1.6 %collective-permute-start.3 = (f32[12,8,8,128]{3,2,1,0:T(8,128)S(1)}, f32[12,8,8,128]{3,2,1,0:T(8,128)S(1)}, u32[]{:S(2)}, u32[]{:S(2)}) collective-permute-start(f32[12,8,8,128]{3,2,1,0:T(8,128)S(1)} %get-tuple-element.15), channel_id=1, source_target_pairs={{0,2},{2,0},{1,3},{3,1},{4,6},{6,4},{5,7},{7,5},{8,10},{10,8},{9,1... | collective-permute-start | bytes 1179656 | tf_op jit(solution)/shard_map/ppermute | solution.py:474
  9.2 4.3 %collective-permute-start.4 = (f32[27,8,128]{2,1,0:T(8,128)S(1)}, f32[27,8,128]{2,1,0:T(8,128)S(1)}, u32[]{:S(2)}, u32[]{:S(2)}) collective-permute-start(f32[27,8,128]{2,1,0:T(8,128)S(1)} %get-tuple-element.16), channel_id=1, source_target_pairs={{0,6},{2,4},{4,2},{6,0},{8,14},{10,12},{12,10},{14,8},{1,7},{3,5},... | collective-permute-start | bytes 331784 | tf_op jit(solution)/shard_map/ppermute | solution.py:481
  13.5 0.8 %collective-permute-start.5 = (f32[27,8,128]{2,1,0:T(8,128)S(1)}, f32[27,8,128]{2,1,0:T(8,128)S(1)}, u32[]{:S(2)}, u32[]{:S(2)}) collective-permute-start(f32[27,8,128]{2,1,0:T(8,128)S(1)} %get-tuple-element.17), channel_id=1, source_target_pairs={{4,10},{6,8},{8,6},{10,4},{5,11},{7,9},{9,7},{11,5},{20,26},{22,24... | collective-permute-start | bytes 331784 | tf_op jit(solution)/shard_map/ppermute | solution.py:481
  14.3 7.1 %collective-permute-done.4.refs_3_.refs_7_ = f32[27,8,128]{2,1,0:T(8,128)S(1)} collective-permute-done((f32[27,8,128]{2,1,0:T(8,128)S(1)}, f32[27,8,128]{2,1,0:T(8,128)S(1)}, u32[]{:S(2)}, u32[]{:S(2)}) %collective-permute-start.4) | collective-permute-done | bytes 110624 | tf_op jit(solution)/shard_map/ppermute | solution.py:481
  21.5 0.0 collective-permute-done.5.refs_4_.refs_8_
  21.5 0.0 copy-start.5
  21.5 0.5 pack_strips.1
  22.0 0.0 copy-start.4
  22.0 0.1 collective-permute-start.6
  22.1 0.5 collective-permute-start
  23.2 1.7 %slot_tables.1 = (bf16[256,2048]{1,0:T(8,128)(2,1)S(1)}, s32[8,2048]{1,0:T(8,128)S(1)}) custom-call(s32[1,1024]{1,0:T(1,128)S(1)} %bitcast.3, s32[1,1024]{1,0:T(1,128)S(1)} %bitcast.4), custom_call_target="tpu_custom_call" | custom-call | tf_op jit(solution)/shard_map/slot_tables/pallas_call | solution.py:488
  25.0 0.0 copy-start.6
  25.0 0.7 %copy-done.6 = f32[2,3]{1,0:T(2,128)S(1)} copy-done((f32[2,3]{1,0:T(2,128)S(1)}, f32[2,3]{1,0:T(2,128)}, u32[]{:S(2)}) %copy-start.6) | copy-done | bytes 48
  25.6 13.6 %two_steps.1 = (f32[3,8,16,128]{3,2,1,0:T(8,128)}, f32[8,12,256]{2,1,0:T(8,128)S(1)}) custom-call(f32[6,8,16,128]{3,2,1,0:T(8,128)S(1)} %copy-done.1, f32[3,8,16,128]{3,2,1,0:T(8,128)S(1)} %copy-done.2, f32[3,8,16,128]{3,2,1,0:T(8,128)S(1)} %copy-done.3, f32[12,8,128]{2,1,0:T(8,128)S(1)} %collective-permute-done.refs_3_, ...), custom_call_target="tpu_custom_call" | custom-call | tf_op jit(solution)/shard_map/two_steps/pallas_call | solution.py:510
  39.2 15.0 %all_to_all.5 = f32[8,12,256]{2,1,0:T(8,128)S(1)} all-to-all(f32[8,12,256]{2,1,0:T(8,128)S(1)} %get-tuple-element.21), channel_id=1, replica_groups=mesh['runs'=2,'gx'=4,'gy'=2,'gz'=2] {'gx','gy'}, dimensions={0} | all-to-all | bytes 196608 | tf_op jit(solution)/shard_map/all_to_all | solution.py:526
  54.2 0.1 copy.9
  54.2 0.7 %reshape.16 = f32[1,12,2048]{2,0,1:T(1,128)} reshape(f32[12,8,256]{2,1,0:T(8,128)S(1)} %copy.9) | data formatting | bytes 196608 | tf_op jit(solution)/shard_map/reshape | solution.py:527
  (11 shorter events, 0.0 us)
Async XLA Ops:
  0.6 1.0 %copy-start = (f32[6,8,16,128]{3,2,1,0:T(8,128)S(1)}, f32[6,8,16,128]{3,2,1,0:T(8,128)}, u32[]{:S(2)}) copy-start(f32[6,8,16,128]{3,2,1,0:T(8,128)} %refs_0_.3) | copy-start | bytes 1179652
  1.6 0.9 %copy-start.2 = (f32[3,8,16,128]{3,2,1,0:T(8,128)S(1)}, f32[3,8,16,128]{3,2,1,0:T(8,128)}, u32[]{:S(2)}) copy-start(f32[3,8,16,128]{3,2,1,0:T(8,128)} %refs_1_.3) | copy-start | bytes 589828
  2.6 0.9 %copy-start.3 = (f32[3,8,16,128]{3,2,1,0:T(8,128)S(1)}, f32[3,8,16,128]{3,2,1,0:T(8,128)}, u32[]{:S(2)}) copy-start(f32[3,8,16,128]{3,2,1,0:T(8,128)} %refs_2_.3) | copy-start | bytes 589828
  3.9 17.6 %collective-permute-start.1 = (f32[59,16,128]{2,1,0:T(8,128)S(1)}, f32[59,16,128]{2,1,0:T(8,128)S(1)}, u32[]{:S(2)}, u32[]{:S(2)}) collective-permute-start(f32[59,16,128]{2,1,0:T(8,128)S(1)} %get-tuple-element.13), channel_id=1, source_target_pairs={{0,4},{4,0},{8,12},{12,8},{1,5},{5,1},{9,13},{13,9},{2,6},{6,2},{1... | collective-permute-start | bytes 1449992 | tf_op jit(solution)/shard_map/ppermute | solution.py:472
  7.0 14.5 %collective-permute-start.2 = (f32[59,16,128]{2,1,0:T(8,128)S(1)}, f32[59,16,128]{2,1,0:T(8,128)S(1)}, u32[]{:S(2)}, u32[]{:S(2)}) collective-permute-start(f32[59,16,128]{2,1,0:T(8,128)S(1)} %get-tuple-element.14), channel_id=1, source_target_pairs={{4,8},{8,4},{5,9},{9,5},{6,10},{10,6},{7,11},{11,7},{20,24},{24,20... | collective-permute-start | bytes 1449992 | tf_op jit(solution)/shard_map/ppermute | solution.py:472
  7.6 13.8 %collective-permute-start.3 = (f32[12,8,8,128]{3,2,1,0:T(8,128)S(1)}, f32[12,8,8,128]{3,2,1,0:T(8,128)S(1)}, u32[]{:S(2)}, u32[]{:S(2)}) collective-permute-start(f32[12,8,8,128]{3,2,1,0:T(8,128)S(1)} %get-tuple-element.15), channel_id=1, source_target_pairs={{0,2},{2,0},{1,3},{3,1},{4,6},{6,4},{5,7},{7,5},{8,10},{10,8},{9,1... | collective-permute-start | bytes 1179656 | tf_op jit(solution)/shard_map/ppermute | solution.py:474
  9.2 12.3 %collective-permute-start.4 = (f32[27,8,128]{2,1,0:T(8,128)S(1)}, f32[27,8,128]{2,1,0:T(8,128)S(1)}, u32[]{:S(2)}, u32[]{:S(2)}) collective-permute-start(f32[27,8,128]{2,1,0:T(8,128)S(1)} %get-tuple-element.16), channel_id=1, source_target_pairs={{0,6},{2,4},{4,2},{6,0},{8,14},{10,12},{12,10},{14,8},{1,7},{3,5},... | collective-permute-start | bytes 331784 | tf_op jit(solution)/shard_map/ppermute | solution.py:481
  13.5 11.4 %copy-start.1 = (f32[6,8,16,128]{3,2,1,0:T(8,128)S(1)}, f32[6,8,16,128]{3,2,1,0:T(8,128)}, u32[]{:S(2)}) copy-start(f32[6,8,16,128]{3,2,1,0:T(8,128)} %refs_0_.3) | copy-start | bytes 1179652
  13.5 7.9 %collective-permute-start.5 = (f32[27,8,128]{2,1,0:T(8,128)S(1)}, f32[27,8,128]{2,1,0:T(8,128)S(1)}, u32[]{:S(2)}, u32[]{:S(2)}) collective-permute-start(f32[27,8,128]{2,1,0:T(8,128)S(1)} %get-tuple-element.17), channel_id=1, source_target_pairs={{4,10},{6,8},{8,6},{10,4},{5,11},{7,9},{9,7},{11,5},{20,26},{22,24... | collective-permute-start | bytes 331784 | tf_op jit(solution)/shard_map/ppermute | solution.py:481
  21.5 1.7 %copy-start.5 = (s32[1,1,1,1024,1]{3,4,2,1,0:T(1,128)S(1)}, s32[1,1,1,1024,1]{3,4,2,1,0:T(1,128)}, u32[]{:S(2)}) copy-start(s32[1,1,1,1024,1]{3,4,2,1,0:T(1,128)} %param.13) | copy-start | bytes 12292
  22.0 1.3 %copy-start.4 = (s32[1,1,1,1024]{3,2,1,0:T(1,128)S(1)}, s32[1,1,1,1024]{3,2,1,0:T(1,128)}, u32[]{:S(2)}) copy-start(s32[1,1,1,1024]{3,2,1,0:T(1,128)} %param.12) | copy-start | bytes 12292
  22.0 3.0 %collective-permute-start.6 = (f32[26,8,128]{2,1,0:T(8,128)S(1)}, f32[26,8,128]{2,1,0:T(8,128)S(1)}, u32[]{:S(2)}, u32[]{:S(2)}) collective-permute-start(f32[26,8,128]{2,1,0:T(8,128)S(1)} %pack_strips.1), channel_id=1, source_target_pairs={{0,1},{1,0},{2,3},{3,2},{4,5},{5,4},{6,7},{7,6},{8,9},{9,8},{10,11... | collective-permute-start | bytes 319496 | tf_op jit(solution)/shard_map/ppermute | solution.py:508
  22.1 2.9 %collective-permute-start = (f32[12,8,128]{2,1,0:T(8,128)S(1)}, f32[12,8,128]{2,1,0:T(8,128)S(1)}, u32[]{:S(2)}, u32[]{:S(2)}) collective-permute-start(f32[12,8,128]{2,1,0:T(8,128)S(1)} %get-tuple-element.12), channel_id=1, source_target_pairs={{0,1},{1,0},{2,3},{3,2},{4,5},{5,4},{6,7},{7,6},{8,9},{9,8},{10,11... | collective-permute-start | bytes 147464 | tf_op jit(solution)/shard_map/ppermute | solution.py:482
  25.0 0.7 %copy-start.6 = (f32[2,3]{1,0:T(2,128)S(1)}, f32[2,3]{1,0:T(2,128)}, u32[]{:S(2)}) copy-start(f32[2,3]{1,0:T(2,128)} %refs_13_.1) | copy-start | bytes 76

commit v2 on v1

--- a/solution.py
+++ b/solution.py
@@ -1,3 +1,5 @@
+import functools
+
 import jax
 import jax.numpy as jnp
 from jax import lax
@@ -25,8 +27,11 @@
 )
 CORNERS = len(CORNER_WHOLE) + (len(CORNER_HALF) + 1) // 2
 VMEM_LIMIT = 40 * 1024 * 1024
+UNROLL = 8
+SAMPLE_UNROLL = 4
+PART = 4
 VMEM = pl.BlockSpec(memory_space=pltpu.VMEM)
-SMEM = pl.BlockSpec(memory_space=pltpu.SMEM)
+HBM = pl.BlockSpec(memory_space=pltpu.HBM)
 
 
 def f32(*shape):
@@ -48,15 +53,6 @@
         turned = pltpu.roll(tile, (STRIP * at + head) & (LANES - 1), 1)
         packed = turned if packed is None else jnp.where(slot == at, turned, packed)
     return packed
-
-
-def source(refs, field):
-    stress, velocity, material = refs
-    if field < VX:
-        return stress, field
-    if field < LAM:
-        return velocity, field - VX
-    return material, field - LAM
 
 
 class Grid:
@@ -96,32 +92,29 @@
 
 
 def pack_kernel(grid, *refs):
-    sources = refs[:3]
-    outs = refs[3:]
+    fields = refs[0]
+    outs = refs[1:]
     own = outs[-1]
     sub = iota(0)
     for (name, _), out in zip(grid.pieces(), outs):
         if name[0] == "x":
             high = above("gx", name[1])
             for f in range(FIELDS):
-                ref, at = source(sources, f)
                 n = DEPTHS[f]
                 start = jnp.where(high, grid.cx - n, 0)
-                out[OFFSETS[f] : OFFSETS[f + 1]] = ref[at, pl.ds(start, n)]
+                out[OFFSETS[f] : OFFSETS[f + 1]] = fields[f, pl.ds(start, n)]
         elif name[0] == "y":
             row = pl.multiple_of(jnp.where(above("gy", name[1]), grid.cy - ROWS, 0), ROWS)
             for f in range(FIELDS):
-                ref, at = source(sources, f)
-                out[f] = ref[at, :, pl.ds(row, ROWS), :]
+                out[f] = fields[f, :, pl.ds(row, ROWS), :]
         else:
             high = above("gx", name[1])
             up = above("gy", name[2])
             row = pl.multiple_of(jnp.where(up, grid.cy - ROWS, 0), ROWS)
 
             def tile(field, distance):
-                ref, at = source(sources, field)
                 layer = jnp.where(high, grid.cx - distance, distance - 1)
-                return ref[at, layer, pl.ds(row, ROWS), :]
+                return fields[field, layer, pl.ds(row, ROWS), :]
 
             for i, (f, d) in enumerate(CORNER_WHOLE):
                 out[i] = tile(f, d)
@@ -137,8 +130,7 @@
     for g in range(groups(len(tiles))):
         part = []
         for f, x, r in tiles[16 * g : 16 * g + 16]:
-            ref, at = source(sources, f)
-            part.append(ref[at, x, ROWS * r : ROWS * r + ROWS, :])
+            part.append(fields[f, x, ROWS * r : ROWS * r + ROWS, :])
         own[g] = pack_strips(part, head)
 
 
@@ -199,100 +191,126 @@
         )
 
 
-def main_kernel(grid, *refs):
-    pieces = grid.pieces()
-    n = len(pieces)
-    sources = refs[:3]
-    own_strips = refs[3]
-    arrived = refs[4 : 4 + n]
-    strips, lanes_ref, rows_ref, site_ref, wavelet_ref = refs[4 + n : 9 + n]
-    velocity_out, table_out = refs[9 + n : 11 + n]
-    ext, sampled = refs[11 + n :]
-    rows = grid.rows
-    cx, cy, cz = grid.cx, grid.cy, grid.cz
-    half = lax.axis_index("gz")
-    other = 1 - half
+def edge(grid, up):
+    if len(grid.y_pairs) > 1:
+        return lambda tile: tile
     sub = iota(0)
-    lead = jnp.where(half == 0, 0, LANES - STRIP)
-
-    def edge(up):
-        if len(grid.y_pairs) > 1:
-            return lambda tile: tile
-        low, top = jnp.where(up, 6, 0), jnp.where(up, 8, 2)
-        keep = jnp.logical_or(sub < low, sub >= top)
-        return lambda tile: jnp.where(keep, tile, 0.0)
-
-    def row_of(up):
-        if len(grid.y_pairs) == 1:
-            return cy
-        return pl.multiple_of(jnp.where(up, cy, cy + ROWS), ROWS)
-
+    keep = jnp.logical_or(sub < jnp.where(up, 6, 0), sub >= jnp.where(up, 8, 2))
+    return lambda tile: jnp.where(keep, tile, 0.0)
+
+
+def halo_row(grid, up):
+    if len(grid.y_pairs) == 1:
+        return grid.cy
+    return pl.multiple_of(jnp.where(up, grid.cy, grid.cy + ROWS), ROWS)
+
+
+def lay_own(grid, ext, own):
+    cx, cy = grid.cx, grid.cy
     for f in range(FIELDS):
         for x in list(range(HALO)) + list(range(HALO + cx, grid.layers)):
-            for h in range(2):
-                ext[f, h, x, cy:rows, :] = jnp.zeros((rows - cy, cz), jnp.float32)
-
-    def unpack(ref, base, at):
-        return pltpu.roll(ref[base + at // 16], (lead - STRIP * (at % 16)) & (LANES - 1), 1)
-
+            for row in range(cy, grid.rows, ROWS):
+                ext[f, x, row : row + ROWS, :] = jnp.zeros((ROWS, grid.cz), jnp.float32)
     at = 0
     for f in range(FIELDS):
-        ref, k = source(sources, f)
         for x in range(cx):
-            ext[f, half, HALO + x, 0:cy, :] = ref[k, x]
             for r in range(grid.tiles_y):
-                ext[f, other, HALO + x, ROWS * r : ROWS * r + ROWS, :] = unpack(own_strips, 0, at)
+                ext[f, HALO + x, ROWS * r : ROWS * r + ROWS, :] = own(at)
                 at += 1
-    base = 0
-    for (name, count), ref in zip(pieces, arrived):
+
+
+def lay_halos(grid, ext, arrived):
+    cx, cy = grid.cx, grid.cy
+    for (name, count), tile_of in zip(grid.pieces(), arrived):
         if name[0] == "x":
             high = above("gx", name[1])
             at = 0
             for f in range(FIELDS):
                 start = jnp.where(high, HALO + cx, HALO - DEPTHS[f])
                 for d in range(DEPTHS[f]):
-                    ext[f, half, start + d, 0:cy, :] = ref[OFFSETS[f] + d]
                     for r in range(grid.tiles_y):
-                        ext[f, other, start + d, ROWS * r : ROWS * r + ROWS, :] = unpack(
-                            strips, base, at
-                        )
+                        ext[f, start + d, ROWS * r : ROWS * r + ROWS, :] = tile_of(at)
                         at += 1
-        elif name[0] == "y":
-            up = above("gy", name[1])
-            clear = edge(up)
-            place = row_of(up)
+            continue
+        up = above("gy", name[-1])
+        clear = edge(grid, up)
+        place = halo_row(grid, up)
+        if name[0] == "y":
             for f in range(FIELDS):
                 for x in range(cx):
-                    ext[f, half, HALO + x, pl.ds(place, ROWS), :] = clear(ref[f, x])
-                    ext[f, other, HALO + x, pl.ds(place, ROWS), :] = clear(
-                        unpack(strips, base, f * cx + x)
-                    )
-        else:
-            high = above("gx", name[1])
-            up = above("gy", name[2])
-            clear = edge(up)
-            place = row_of(up)
-
-            def put(h, field, distance, tile):
-                layer = jnp.where(high, HALO + cx - 1 + distance, HALO - distance)
-                ext[field, h, layer, pl.ds(place, ROWS), :] = clear(tile)
-
-            for h, tile_of in ((half, lambda i: ref[i]), (other, lambda i: unpack(strips, base, i))):
-                for i, (f, d) in enumerate(CORNER_WHOLE):
-                    put(h, f, d, tile_of(i))
-                for i in range(0, len(CORNER_HALF), 2):
-                    tile = tile_of(len(CORNER_WHOLE) + i // 2)
-                    turned = pltpu.roll(tile, 4, 0)
-                    put(h, *CORNER_HALF[i], jnp.where(up, tile, turned))
-                    if i + 1 < len(CORNER_HALF):
-                        put(h, *CORNER_HALF[i + 1], jnp.where(up, turned, tile))
-        base += groups(count)
-
+                    ext[f, HALO + x, pl.ds(place, ROWS), :] = clear(tile_of(f * cx + x))
+            continue
+        high = above("gx", name[1])
+
+        def put(field, distance, tile):
+            layer = jnp.where(high, HALO + cx - 1 + distance, HALO - distance)
+            ext[field, layer, pl.ds(place, ROWS), :] = clear(tile)
+
+        for i, (f, d) in enumerate(CORNER_WHOLE):
+            put(f, d, tile_of(i))
+        for i in range(0, len(CORNER_HALF), 2):
+            tile = tile_of(len(CORNER_WHOLE) + i // 2)
+            turned = pltpu.roll(tile, 4, 0)
+            put(*CORNER_HALF[i], jnp.where(up, tile, turned))
+            if i + 1 < len(CORNER_HALF):
+                put(*CORNER_HALF[i + 1], jnp.where(up, turned, tile))
+
+
+def known_lanes():
+    lead = jnp.where(lax.axis_index("gz") == 0, 0, LANES - STRIP)
+    lane = iota(1)
+    return lead, jnp.logical_and(lane >= lead, lane < lead + STRIP)
+
+
+def unpack(ref, base, at):
+    lead, known = known_lanes()
+    turned = pltpu.roll(ref[base + at // 16], (lead - STRIP * (at % 16)) & (LANES - 1), 1)
+    return jnp.where(known, turned, 0.0)
+
+
+def begin_kernel(grid, *refs):
+    fields, own_strips, ext, beside = refs
+
+    def own(at):
+        x, r = at // grid.tiles_y % grid.cx, at % grid.tiles_y
+        return fields[at // (grid.tiles_y * grid.cx), x, ROWS * r : ROWS * r + ROWS, :]
+
+    lay_own(grid, ext, own)
+    lay_own(grid, beside, functools.partial(unpack, own_strips, 0))
+
+
+def assemble_kernel(grid, *refs):
+    arrived, ext = refs[1:-1], refs[-1]
+    tiles = [
+        functools.partial(piece_tile, name, ref, grid=grid)
+        for (name, _), ref in zip(grid.pieces(), arrived)
+    ]
+    lay_halos(grid, ext, tiles)
+
+
+def main_kernel(grid, *refs):
+    strips, lanes_ref, rows_ref, site_hbm, wavelet_hbm = refs[2:7]
+    ext, beside, velocity_out, table_out = refs[7:11]
+    sampled, site_ref, wavelet_ref, sems = refs[11:]
+    copies = (
+        pltpu.make_async_copy(site_hbm, site_ref, sems.at[0]),
+        pltpu.make_async_copy(wavelet_hbm, wavelet_ref, sems.at[1]),
+    )
+    for copy in copies:
+        copy.start()
+    rows = grid.rows
+    cx, cy, cz = grid.cx, grid.cy, grid.cz
+    half = lax.axis_index("gz")
+    sub = iota(0)
+    lane = iota(1)
+    bases = [0]
+    for _, count in grid.pieces():
+        bases.append(bases[-1] + groups(count))
+    lay_halos(grid, beside, [functools.partial(unpack, strips, base) for base in bases[:-1]])
     lane_all = iota(1, (rows, cz))
-    lane = iota(1)
 
     def pair(field, x):
-        return ext[field, 0, x], ext[field, 1, x]
+        return ext[field, x], beside[field, x]
 
     def add(a, b):
         return a[0] + b[0], a[1] + b[1]
@@ -310,13 +328,10 @@
         return tuple(pltpu.roll(v, -offset % rows, 0) for v in a)
 
     def moved_z(a, offset):
-        low = pltpu.roll(a[0], -offset % cz, 1)
-        high = pltpu.roll(a[1], -offset % cz, 1)
-        if offset > 0:
-            inside = lane_all < cz - offset
-            return jnp.where(inside, low, high), jnp.where(inside, high, 0.0)
-        inside = lane_all >= -offset
-        return jnp.where(inside, low, 0.0), jnp.where(inside, high, low)
+        own = pltpu.roll(a[0], -offset % cz, 1)
+        far = pltpu.roll(a[1], -offset % cz, 1)
+        inside = lane_all < cz - offset if offset > 0 else lane_all >= -offset
+        return jnp.where(inside, own, far), jnp.where(inside, far, own)
 
     def forward(a, move):
         return sub_(move(a, 1), a), sub_(move(a, 2), move(a, -1))
@@ -343,12 +358,12 @@
         rate_z = total(
             along_x(SXZ, y - 1), backward(syz, moved_y), forward(pair(SZZ, y), moved_z)
         )
-        for h in range(2):
-            b = scale * ext[BUOY, h, x]
-            ext[VX, h, x] = ext[VX, h, x] + b * rate_x[h]
-            b = scale * ext[BUOY, h, y]
-            ext[VY, h, y] = ext[VY, h, y] + b * rate_y[h]
-            ext[VZ, h, y] = ext[VZ, h, y] + b * rate_z[h]
+        for h, block in enumerate((ext, beside)):
+            b = scale * block[BUOY, x]
+            block[VX, x] = block[VX, x] + b * rate_x[h]
+            b = scale * block[BUOY, y]
+            block[VY, y] = block[VY, y] + b * rate_y[h]
+            block[VZ, y] = block[VZ, y] + b * rate_z[h]
 
     def stress_layer(x):
         vx, vy, vz = pair(VX, x), pair(VY, x), pair(VZ, x)
@@ -358,24 +373,27 @@
         gxy = total(forward(vx, moved_y), along_x(VY, x))
         gxz = total(forward(vx, moved_z), along_x(VZ, x))
         gyz = total(forward(vy, moved_z), forward(vz, moved_y))
-        for h in range(2):
-            shear = scale * ext[MU, h, x]
-            volume = scale * ext[LAM, h, x] * (gxx[h] + gyy[h] + gzz[h])
+        for h, block in enumerate((ext, beside)):
+            shear = scale * block[MU, x]
+            volume = scale * block[LAM, x] * (gxx[h] + gyy[h] + gzz[h])
             twice = 2.0 * shear
-            ext[SXX, h, x] = ext[SXX, h, x] + (twice * gxx[h] + volume)
-            ext[SYY, h, x] = ext[SYY, h, x] + (twice * gyy[h] + volume)
-            ext[SZZ, h, x] = ext[SZZ, h, x] + (twice * gzz[h] + volume)
-            ext[SXY, h, x] = ext[SXY, h, x] + shear * gxy[h]
-            ext[SXZ, h, x] = ext[SXZ, h, x] + shear * gxz[h]
-            ext[SYZ, h, x] = ext[SYZ, h, x] + shear * gyz[h]
-
-    def loop(first, last, body):
+            block[SXX, x] = block[SXX, x] + (twice * gxx[h] + volume)
+            block[SYY, x] = block[SYY, x] + (twice * gyy[h] + volume)
+            block[SZZ, x] = block[SZZ, x] + (twice * gzz[h] + volume)
+            block[SXY, x] = block[SXY, x] + shear * gxy[h]
+            block[SXZ, x] = block[SXZ, x] + shear * gxz[h]
+            block[SYZ, x] = block[SYZ, x] + shear * gyz[h]
+
+    def loop(first, last, body, unroll=UNROLL):
         def step(x, carry):
             body(x)
             return carry
 
-        lax.fori_loop(HALO + first, HALO + last + 1, step, 0)
-
+        lax.fori_loop(HALO + first, HALO + last + 1, step, 0, unroll=unroll)
+
+    loop(-5, cx + 3, velocity_layer)
+    for copy in copies:
+        copy.wait()
     site = site_ref[0]
     total_y, total_z = cy * grid.gy, cz * grid.gz
     site_x = lax.div(site, total_y * total_z) - lax.axis_index("gx") * cx
@@ -386,65 +404,69 @@
     site_row = jnp.where(site_y < 0, site_y + rows, site_y)
 
     def inject(step):
-        @pl.when(near)
-        def _():
-            h = lax.div(site_z, cz)
-            x = site_x + HALO
-            row = pl.multiple_of(lax.div(site_row, ROWS) * ROWS, ROWS)
-            here = jnp.logical_and(sub == lax.rem(site_row, ROWS), lane == lax.rem(site_z, cz))
-            amount = jnp.where(here, TIME_STEP * ext[BUOY, h, x, pl.ds(row, ROWS), :], 0.0)
-            for c in range(3):
-                ext[VX + c, h, x, pl.ds(row, ROWS), :] = (
-                    ext[VX + c, h, x, pl.ds(row, ROWS), :] + amount * wavelet_ref[step, c]
-                )
-
-    def strain_layer(x):
-        lam = ext[LAM, half, x, 0:cy, :]
-        shear = ext[MU, half, x, 0:cy, :]
-        parts = [ext[f, half, x, 0:cy, :] for f in range(6)]
+        x = site_x + HALO
+        row = pl.multiple_of(lax.div(site_row, ROWS) * ROWS, ROWS)
+        here = jnp.logical_and(sub == lax.rem(site_row, ROWS), lane == lax.rem(site_z, cz))
+        own = lax.div(site_z, cz) == half
+        for mine, block in ((True, ext), (False, beside)):
+
+            @pl.when(jnp.logical_and(near, own if mine else jnp.logical_not(own)))
+            def _():
+                amount = jnp.where(here, TIME_STEP * block[BUOY, x, pl.ds(row, ROWS), :], 0.0)
+                for c in range(3):
+                    block[VX + c, x, pl.ds(row, ROWS), :] = (
+                        block[VX + c, x, pl.ds(row, ROWS), :] + amount * wavelet_ref[step, c]
+                    )
+
+    def strain_layer(step, x):
+        lam = ext[LAM, x, 0:cy, :]
+        shear = ext[MU, x, 0:cy, :]
+        parts = [ext[f, x, 0:cy, :] for f in range(6)]
         shrink = lam / (3.0 * lam + 2.0 * shear) * (parts[0] + parts[1] + parts[2])
         inverse = 0.5 / shear
         for f in range(6):
             value = (parts[f] - shrink if f < 3 else parts[f]) * inverse
             head = value.astype(jnp.bfloat16)
             tail = (value - head.astype(jnp.float32)).astype(jnp.bfloat16)
-            row = pl.multiple_of(f * cx * cy + (x - HALO) * cy, cy)
+            row = pl.multiple_of((6 * step + f) * cx * cy + (x - HALO) * cy, cy)
             sampled[pl.ds(row, cy), 0:cz] = head
             sampled[pl.ds(row, cy), cz : 2 * cz] = tail
 
     step_slots = 256
     block = cx * cy
 
-    def sample(step):
-        def body(k, carry):
-            where = pl.ds(pl.multiple_of(k * step_slots, step_slots), step_slots)
+    def sample(k, carry):
+        where = pl.ds(pl.multiple_of(k * step_slots, step_slots), step_slots)
+        row = rows_ref[:, where]
+        marks = [row == r * ROWS + iota(0, (ROWS, step_slots)) for r in range(block // ROWS)]
+        for part in range(6 * STEPS // PART):
             found = jnp.dot(
-                sampled[...], lanes_ref[:, where], preferred_element_type=jnp.float32
+                sampled[part * PART * block : (part + 1) * PART * block, :],
+                lanes_ref[:, where],
+                preferred_element_type=jnp.float32,
             )
-            row = rows_ref[:, where]
-            for f in range(6):
+            for f in range(PART):
                 acc = jnp.zeros((ROWS, step_slots), jnp.float32)
                 for r in range(block // ROWS):
                     tile = found[f * block + r * ROWS : f * block + r * ROWS + ROWS]
-                    acc = acc + jnp.where(row == r * ROWS + iota(0, (ROWS, step_slots)), tile, 0.0)
-                table_out[k, step * 6 + f : step * 6 + f + 1, :] = jnp.sum(
-                    acc, axis=0, keepdims=True
-                )
-            return carry
-
-        lax.fori_loop(0, lanes_ref.shape[1] // step_slots, body, 0)
-
-    velocity_ranges = ((-5, cx + 3), (-2, cx))
-    stress_ranges = ((-3, cx + 2), (0, cx - 1))
-    for step in range(STEPS):
-        loop(*velocity_ranges[step], velocity_layer)
-        inject(step)
-        loop(*stress_ranges[step], stress_layer)
-        loop(0, cx - 1, strain_layer)
-        sample(step)
-    for c in range(3):
-        for x in range(cx):
-            velocity_out[c, x] = ext[VX + c, half, HALO + x, 0:cy, :]
+                    acc = acc + jnp.where(marks[r], tile, 0.0)
+                to = part * PART + f
+                table_out[k, to : to + 1, :] = jnp.sum(acc, axis=0, keepdims=True)
+        return carry
+
+    inject(0)
+    loop(-3, cx + 2, stress_layer)
+    loop(0, cx - 1, functools.partial(strain_layer, 0))
+    loop(-2, cx, velocity_layer)
+    inject(1)
+    leaving = pltpu.make_async_copy(
+        ext.at[VX : VX + 3, HALO : HALO + cx, 0:cy, :], velocity_out, sems.at[2]
+    )
+    leaving.start()
+    loop(0, cx - 1, stress_layer)
+    loop(0, cx - 1, functools.partial(strain_layer, 1))
+    lax.fori_loop(0, lanes_ref.shape[1] // step_slots, sample, 0, unroll=SAMPLE_UNROLL)
+    leaving.wait()
 
 
 def per_device(
@@ -455,16 +477,19 @@
     pieces = grid.pieces()
     params = pltpu.CompilerParams(vmem_limit_bytes=VMEM_LIMIT)
     own_tiles = FIELDS * grid.cx * grid.tiles_y
-    sources = (stress_start, velocity_start, material)
+    fields = sum(
+        lax.pad(part, jnp.float32(0.0), [(first, FIELDS - first - part.shape[0], 0)] + [(0, 0, 0)] * 3)
+        for first, part in ((SXX, stress_start), (VX, velocity_start), (LAM, material))
+    )
     packed = pl.pallas_call(
         lambda *refs: pack_kernel(grid, *refs),
         out_shape=[f32(*grid.shape(name)) for name, _ in pieces]
         + [f32(groups(own_tiles), ROWS, LANES)],
-        in_specs=[VMEM] * 3,
+        in_specs=[VMEM],
         out_specs=[VMEM] * (len(pieces) + 1),
         compiler_params=params,
         name="pack_halos",
-    )(*sources)
+    )(fields)
     swap = [(0, 1), (1, 0)]
     arrived = []
     for (name, _), piece in zip(pieces, packed):
@@ -497,28 +522,56 @@
         name="slot_tables",
     )(save_cells.reshape(1, count), save_writer.reshape(1, count))
 
+    extended = f32(FIELDS, grid.layers, grid.rows, grid.cz)
+    block, beside = pl.pallas_call(
+        lambda *refs: begin_kernel(grid, *refs),
+        out_shape=[extended] * 2,
+        in_specs=[VMEM] * 2,
+        out_specs=[VMEM] * 2,
+        compiler_params=params,
+        name="begin_block",
+    )(fields, own_strips)
+
     strips = pl.pallas_call(
-        lambda *refs: strip_kernel(grid, *refs),
+        lambda *refs: strip_kernel(grid, *refs[3:]),
         out_shape=f32(sum(groups(c) for _, c in pieces), ROWS, LANES),
-        in_specs=[VMEM] * len(pieces),
+        in_specs=[VMEM] * (len(pieces) + 3),
         out_specs=VMEM,
         compiler_params=params,
         name="pack_strips",
-    )(*arrived)
+    )(rows, block, beside, *arrived)
     strips = lax.ppermute(strips, "gz", swap)
 
-    velocity, table = pl.pallas_call(
+    block = pl.pallas_call(
+        lambda *refs: assemble_kernel(grid, *refs),
+        out_shape=extended,
+        in_specs=[VMEM] * (1 + len(pieces)),
+        out_specs=VMEM,
+        input_output_aliases={0: 0},
+        compiler_params=params,
+        name="assemble",
+    )(block, *arrived)
+
+    _, _, velocity, table = pl.pallas_call(
         lambda *refs: main_kernel(grid, *refs),
-        out_shape=[f32(*velocity_start.shape), f32(slots // 256, 6 * STEPS, 256)],
-        in_specs=[VMEM] * (4 + len(pieces) + 3) + [SMEM] * 2,
-        out_specs=[VMEM] * 2,
+        out_shape=[
+            extended,
+            extended,
+            f32(*velocity_start.shape),
+            f32(slots // 256, 6 * STEPS, 256),
+        ],
+        in_specs=[VMEM] * 5 + [HBM] * 2,
+        out_specs=[VMEM, VMEM, HBM, VMEM],
         scratch_shapes=[
-            pltpu.VMEM((FIELDS, 2, grid.layers, grid.rows, grid.cz), jnp.float32),
-            pltpu.VMEM((6 * grid.cx * grid.cy, 2 * grid.cz), jnp.bfloat16),
+            pltpu.VMEM((STEPS * 6 * grid.cx * grid.cy, 2 * grid.cz), jnp.bfloat16),
+            pltpu.SMEM(force_site.shape, jnp.int32),
+            pltpu.SMEM(force_wavelet.shape, jnp.float32),
+            pltpu.SemaphoreType.DMA((3,)),
         ],
+        input_output_aliases={0: 0, 1: 1},
         compiler_params=params,
         name="two_steps",
-    )(*sources, own_strips, *arrived, strips, lanes, rows, force_site, force_wavelet)
+    )(block, beside, strips, lanes, rows, force_site, force_wavelet)
 
     values = 6 * STEPS
     if capacity != 256:

time: 55.3 us -> 45.3 us (0.82)
  Pallas kernels: 16.1 us -> 10.2 us
  waiting for transfers between devices: 7.13 us -> 4.32 us
  local copies, waits for them, and re-layouts: 4.33 us -> 2.21 us
  other arithmetic: 0 us -> 1.27 us
  starting transfers between devices: 11 us -> 10.4 us
    pallas_call x2 -> x4, Pallas kernels: 14 us -> 8.07 us  [the longest x1 7.1 us: per_device(): pl.pallas_call(lambda *refs: main_kernel(grid, *refs), out_shape=[extende...]
    ppermute x2, waiting for transfers between devices: 7.12 us -> 3.83 us  [per_device(): arrived.append(lax.ppermute(piece, ('gx', 'gy'), pairs))]
    unnamed x14 -> x6, local copies, waits for them, and re-layouts: 3.52 us -> 1.4 us
    add x0 -> x1, other arithmetic: none -> 1.27 us  [per_device(): sum((lax.pad(part, jnp.float32(0.0), [(first, FIELDS - first - part.shape...]
  transfers between devices with their start and end apart: 7 -> 7, of which waited for: 1 -> 2; matrix products, arithmetic and copies ran while one was open for 0% -> 0% of each run, Pallas kernels for 3% -> 5%
where the time goes in v2:
time: 45.3 us; the launch traced here: 45 us
  blocking collectives  15.3 us (34%)
  starting transfers between devices  10.4 us (23%)
  Pallas kernels  10.2 us (23%)
  waiting for transfers between devices  4.32 us (10%)
  local copies, waits for them, and re-layouts  2.21 us (5%)
  between operations  1.39 us (3%)
  other arithmetic  1.27 us (3%)
    all_to_all x1, blocking collectives, per_device(): lax.all_to_all(table, ('gx', 'gy'), split_axis=0, concat_axis=0, tiled=True)  15.3 us
    pallas_call x1, Pallas kernels, per_device(): pl.pallas_call(lambda *refs: main_kernel(grid, *refs), out_shape=[extende...  7.1 us
    ppermute x2, starting transfers between devices, per_device(): arrived.append(lax.ppermute(piece, ('gx', 'gy'), pairs))  5 us
    ppermute x2, waiting for transfers between devices, per_device(): arrived.append(lax.ppermute(piece, ('gx', 'gy'), pairs))  3.83 us
    ppermute x2, starting transfers between devices, per_device(): arrived.append(lax.ppermute(piece, 'gx', grid.pairs(grid.gx, name[1])))  3.77 us
    pallas_call x1, Pallas kernels, per_device(): pl.pallas_call(lambda *refs: slot_kernel(width, capacity, grid.cz, *refs)...  1.68 us
    ppermute x1, starting transfers between devices, per_device(): arrived.append(lax.ppermute(piece, 'gy', grid.pairs(grid.gy, name[1])))  1.55 us
    unnamed x6, local copies, waits for them, and re-layouts  1.4 us
  transfers between devices with their start and end apart: 7, of which 2 were waited for; matrix products, arithmetic and copies ran while one was open for 0% of the time, Pallas kernels for 5%

profile of v2, /device:TPU:0, one launch (start us, length us, event | category | flops | bytes accessed | tf_op | source)
XLA Modules:
  0.0 45.0 jit_solution(16784369323688806346)
XLA Ops:
  0.6 1.3 %pad_add_fusion.refs_0_ = f32[12,8,16,128]{3,2,1,0:T(8,128)S(1)} fusion(f32[3,8,16,128]{3,2,1,0:T(8,128)} %param.9, f32[3,8,16,128]{3,2,1,0:T(8,128)} %param.7, f32[6,8,16,128]{3,2,1,0:T(8,128)} %param.8), kind=kLoop, calls=%fused_computation | loop fusion | flops 393216 | bytes 1572864 | tf_op jit(solution)/shard_map/add | solution.py:480
  1.9 0.4 pack_halos.1
  2.3 3.1 %collective-permute-start.1 = (f32[59,16,128]{2,1,0:T(8,128)S(1)}, f32[59,16,128]{2,1,0:T(8,128)S(1)}, u32[]{:S(2)}, u32[]{:S(2)}) collective-permute-start(f32[59,16,128]{2,1,0:T(8,128)S(1)} %get-tuple-element.16), channel_id=1, source_target_pairs={{0,4},{4,0},{8,12},{12,8},{1,5},{5,1},{9,13},{13,9},{2,6},{6,2},{1... | collective-permute-start | bytes 1449992 | tf_op jit(solution)/shard_map/ppermute | solution.py:497
  5.4 0.7 %collective-permute-start.2 = (f32[59,16,128]{2,1,0:T(8,128)S(1)}, f32[59,16,128]{2,1,0:T(8,128)S(1)}, u32[]{:S(2)}, u32[]{:S(2)}) collective-permute-start(f32[59,16,128]{2,1,0:T(8,128)S(1)} %get-tuple-element.17), channel_id=1, source_target_pairs={{4,8},{8,4},{5,9},{9,5},{6,10},{10,6},{7,11},{11,7},{20,24},{24,20... | collective-permute-start | bytes 1449992 | tf_op jit(solution)/shard_map/ppermute | solution.py:497
  6.1 1.6 %collective-permute-start.3 = (f32[12,8,8,128]{3,2,1,0:T(8,128)S(1)}, f32[12,8,8,128]{3,2,1,0:T(8,128)S(1)}, u32[]{:S(2)}, u32[]{:S(2)}) collective-permute-start(f32[12,8,8,128]{3,2,1,0:T(8,128)S(1)} %get-tuple-element.18), channel_id=1, source_target_pairs={{0,2},{2,0},{1,3},{3,1},{4,6},{6,4},{5,7},{7,5},{8,10},{10,8},{9,1... | collective-permute-start | bytes 1179656 | tf_op jit(solution)/shard_map/ppermute | solution.py:499
  7.6 4.3 %collective-permute-start.4 = (f32[27,8,128]{2,1,0:T(8,128)S(1)}, f32[27,8,128]{2,1,0:T(8,128)S(1)}, u32[]{:S(2)}, u32[]{:S(2)}) collective-permute-start(f32[27,8,128]{2,1,0:T(8,128)S(1)} %get-tuple-element.19), channel_id=1, source_target_pairs={{0,6},{2,4},{4,2},{6,0},{8,14},{10,12},{12,10},{14,8},{1,7},{3,5},... | collective-permute-start | bytes 331784 | tf_op jit(solution)/shard_map/ppermute | solution.py:506
  12.0 0.7 %collective-permute-start.5 = (f32[27,8,128]{2,1,0:T(8,128)S(1)}, f32[27,8,128]{2,1,0:T(8,128)S(1)}, u32[]{:S(2)}, u32[]{:S(2)}) collective-permute-start(f32[27,8,128]{2,1,0:T(8,128)S(1)} %get-tuple-element.20), channel_id=1, source_target_pairs={{4,10},{6,8},{8,6},{10,4},{5,11},{7,9},{9,7},{11,5},{20,26},{22,24... | collective-permute-start | bytes 331784 | tf_op jit(solution)/shard_map/ppermute | solution.py:506
  12.7 0.0 copy-start
  12.7 0.7 %copy-done = s32[1,1,1,1024]{3,2,1,0:T(1,128)S(1)} copy-done((s32[1,1,1,1024]{3,2,1,0:T(1,128)S(1)}, s32[1,1,1,1024]{3,2,1,0:T(1,128)}, u32[]{:S(2)}) %copy-start) | copy-done | bytes 4120
  13.3 0.7 %copy-done.1 = s32[1,1,1,1024,1]{3,4,2,1,0:T(1,128)S(1)} copy-done((s32[1,1,1,1024,1]{3,4,2,1,0:T(1,128)S(1)}, s32[1,1,1,1024,1]{3,4,2,1,0:T(1,128)}, u32[]{:S(2)}) %copy-start.1) | copy-done | bytes 4120
  14.0 1.7 %slot_tables.1 = (bf16[256,2048]{1,0:T(8,128)(2,1)S(1)}, s32[8,2048]{1,0:T(8,128)S(1)}) custom-call(s32[1,1024]{1,0:T(1,128)S(1)} %bitcast.3, s32[1,1024]{1,0:T(1,128)S(1)} %bitcast.4), custom_call_target="tpu_custom_call" | custom-call | tf_op jit(solution)/shard_map/slot_tables/pallas_call | solution.py:513
  15.7 0.3 begin_block.1
  16.1 3.8 %collective-permute-done.4.refs_4_.refs_6_ = f32[27,8,128]{2,1,0:T(8,128)S(1)} collective-permute-done((f32[27,8,128]{2,1,0:T(8,128)S(1)}, f32[27,8,128]{2,1,0:T(8,128)S(1)}, u32[]{:S(2)}, u32[]{:S(2)}) %collective-permute-start.4) | collective-permute-done | bytes 110624 | tf_op jit(solution)/shard_map/ppermute | solution.py:506
  19.9 0.0 collective-permute-done.2.refs_2_.refs_4_
  19.9 0.5 %pack_strips.1 = f32[26,8,128]{2,1,0:T(8,128)S(1)} custom-call(s32[8,2048]{1,0:T(8,128)S(1)} %get-tuple-element.22.refs_0_.refs_4_, f32[12,20,24,128]{3,2,1,0:T(8,128)S(1)} %get-tuple-element.15.refs_0_.refs_1_, f32[12,20,24,128]{3,2,1,0:T(8,128)S(1)} %get-tuple-element.21.refs_2_.refs_1_, f32[59,16,128]{2,1,0:T(8,128)S(1)} %collective-permute-done.1.refs_1_.refs_3_, ...), custom_call_target="tpu_custom_call" | custom-call | tf_op jit(solution)/shard_map/pack_strips/pallas_call | solution.py:535
  20.4 0.1 collective-permute-start.6
  21.1 0.0 copy-start.2
  21.1 0.2 assemble.1.refs_0_
  21.3 0.5 %collective-permute-done.6.refs_2_ = f32[26,8,128]{2,1,0:T(8,128)S(1)} collective-permute-done((f32[26,8,128]{2,1,0:T(8,128)S(1)}, f32[26,8,128]{2,1,0:T(8,128)S(1)}, u32[]{:S(2)}, u32[]{:S(2)}) %collective-permute-start.6) | collective-permute-done | bytes 106528 | tf_op jit(solution)/shard_map/ppermute | solution.py:543
  21.8 0.0 copy-done.2
  21.8 7.1 %two_steps.1 = (f32[12,20,24,128]{3,2,1,0:T(8,128)S(1)}, f32[12,20,24,128]{3,2,1,0:T(8,128)S(1)}, f32[3,8,16,128]{3,2,1,0:T(8,128)}, f32[8,12,256]{2,1,0:T(8,128)S(1)}) custom-call(f32[12,20,24,128]{3,2,1,0:T(8,128)S(1)} %assemble.1.refs_0_, f32[12,20,24,128]{3,2,1,0:T(8,128)S(1)} %get-tuple-element.21.refs_2_.refs_1_, ...), custom_call_target="tpu_custom_call", output_to_operand_aliasing={{0}: (0, {}), {1}: (1, {})} | custom-call | tf_op jit(solution)/shard_map/two_steps/pallas_call | solution.py:555
  28.9 15.3 %all_to_all.5 = f32[8,12,256]{2,1,0:T(8,128)S(1)} all-to-all(f32[8,12,256]{2,1,0:T(8,128)S(1)} %get-tuple-element.25), channel_id=1, replica_groups=mesh['runs'=2,'gx'=4,'gy'=2,'gz'=2] {'gx','gy'}, dimensions={0} | all-to-all | bytes 196608 | tf_op jit(solution)/shard_map/all_to_all | solution.py:579
  44.2 0.1 copy.12
  44.3 0.7 %reshape.16 = f32[1,12,2048]{2,0,1:T(1,128)} reshape(f32[12,8,256]{2,1,0:T(8,128)S(1)} %copy.12) | data formatting | bytes 196608 | tf_op jit(solution)/shard_map/reshape | solution.py:580
  (6 shorter events, 0.0 us)
Async XLA Ops:
  2.3 17.6 %collective-permute-start.1 = (f32[59,16,128]{2,1,0:T(8,128)S(1)}, f32[59,16,128]{2,1,0:T(8,128)S(1)}, u32[]{:S(2)}, u32[]{:S(2)}) collective-permute-start(f32[59,16,128]{2,1,0:T(8,128)S(1)} %get-tuple-element.16), channel_id=1, source_target_pairs={{0,4},{4,0},{8,12},{12,8},{1,5},{5,1},{9,13},{13,9},{2,6},{6,2},{1... | collective-permute-start | bytes 1449992 | tf_op jit(solution)/shard_map/ppermute | solution.py:497
  5.4 14.5 %collective-permute-start.2 = (f32[59,16,128]{2,1,0:T(8,128)S(1)}, f32[59,16,128]{2,1,0:T(8,128)S(1)}, u32[]{:S(2)}, u32[]{:S(2)}) collective-permute-start(f32[59,16,128]{2,1,0:T(8,128)S(1)} %get-tuple-element.17), channel_id=1, source_target_pairs={{4,8},{8,4},{5,9},{9,5},{6,10},{10,6},{7,11},{11,7},{20,24},{24,20... | collective-permute-start | bytes 1449992 | tf_op jit(solution)/shard_map/ppermute | solution.py:497
  6.1 13.8 %collective-permute-start.3 = (f32[12,8,8,128]{3,2,1,0:T(8,128)S(1)}, f32[12,8,8,128]{3,2,1,0:T(8,128)S(1)}, u32[]{:S(2)}, u32[]{:S(2)}) collective-permute-start(f32[12,8,8,128]{3,2,1,0:T(8,128)S(1)} %get-tuple-element.18), channel_id=1, source_target_pairs={{0,2},{2,0},{1,3},{3,1},{4,6},{6,4},{5,7},{7,5},{8,10},{10,8},{9,1... | collective-permute-start | bytes 1179656 | tf_op jit(solution)/shard_map/ppermute | solution.py:499
  7.6 4.4 %collective-permute-start = (f32[12,8,128]{2,1,0:T(8,128)S(1)}, f32[12,8,128]{2,1,0:T(8,128)S(1)}, u32[]{:S(2)}, u32[]{:S(2)}) collective-permute-start(f32[12,8,128]{2,1,0:T(8,128)S(1)} %get-tuple-element.14), channel_id=1, source_target_pairs={{0,1},{1,0},{2,3},{3,2},{4,5},{5,4},{6,7},{7,6},{8,9},{9,8},{10,11... | collective-permute-start | bytes 147464 | tf_op jit(solution)/shard_map/ppermute | solution.py:507
  7.6 12.3 %collective-permute-start.4 = (f32[27,8,128]{2,1,0:T(8,128)S(1)}, f32[27,8,128]{2,1,0:T(8,128)S(1)}, u32[]{:S(2)}, u32[]{:S(2)}) collective-permute-start(f32[27,8,128]{2,1,0:T(8,128)S(1)} %get-tuple-element.19), channel_id=1, source_target_pairs={{0,6},{2,4},{4,2},{6,0},{8,14},{10,12},{12,10},{14,8},{1,7},{3,5},... | collective-permute-start | bytes 331784 | tf_op jit(solution)/shard_map/ppermute | solution.py:506
  12.0 7.9 %collective-permute-start.5 = (f32[27,8,128]{2,1,0:T(8,128)S(1)}, f32[27,8,128]{2,1,0:T(8,128)S(1)}, u32[]{:S(2)}, u32[]{:S(2)}) collective-permute-start(f32[27,8,128]{2,1,0:T(8,128)S(1)} %get-tuple-element.20), channel_id=1, source_target_pairs={{4,10},{6,8},{8,6},{10,4},{5,11},{7,9},{9,7},{11,5},{20,26},{22,24... | collective-permute-start | bytes 331784 | tf_op jit(solution)/shard_map/ppermute | solution.py:506
  12.7 0.7 %copy-start = (s32[1,1,1,1024]{3,2,1,0:T(1,128)S(1)}, s32[1,1,1,1024]{3,2,1,0:T(1,128)}, u32[]{:S(2)}) copy-start(s32[1,1,1,1024]{3,2,1,0:T(1,128)} %param.12) | copy-start | bytes 12292
  13.3 0.7 %copy-start.1 = (s32[1,1,1,1024,1]{3,4,2,1,0:T(1,128)S(1)}, s32[1,1,1,1024,1]{3,4,2,1,0:T(1,128)}, u32[]{:S(2)}) copy-start(s32[1,1,1,1024,1]{3,4,2,1,0:T(1,128)} %param.13) | copy-start | bytes 12292
  20.4 1.4 %collective-permute-start.6 = (f32[26,8,128]{2,1,0:T(8,128)S(1)}, f32[26,8,128]{2,1,0:T(8,128)S(1)}, u32[]{:S(2)}, u32[]{:S(2)}) collective-permute-start(f32[26,8,128]{2,1,0:T(8,128)S(1)} %pack_strips.1), channel_id=1, source_target_pairs={{0,1},{1,0},{2,3},{3,2},{4,5},{5,4},{6,7},{7,6},{8,9},{9,8},{10,11... | collective-permute-start | bytes 319496 | tf_op jit(solution)/shard_map/ppermute | solution.py:543
  21.1 0.7 %copy-start.2 = (f32[2,3]{1,0:T(2,128)S(1)}, f32[2,3]{1,0:T(2,128)}, u32[]{:S(2)}) copy-start(f32[2,3]{1,0:T(2,128)} %refs_6_.1) | copy-start | bytes 76

commit v3 on v2

--- a/solution.py
+++ b/solution.py
@@ -19,19 +19,35 @@
 ROWS = 8
 STRIP = 8
 LANES = 128
-CORNER_WHOLE = tuple((f, d) for f in (SXX, SYY, SXY, SXZ, SYZ) for d in (1, 2))
-CORNER_HALF = (
-    tuple((f, d) for f in (SXX, SYY, SXY, SXZ, SYZ) for d in (3, 4, 5))
-    + tuple((f, d) for f in (SZZ, VX, VY, VZ, BUOY) for d in (1, 2, 3))
-    + tuple((f, d) for f in (LAM, MU) for d in (1, 2))
-)
-CORNERS = len(CORNER_WHOLE) + (len(CORNER_HALF) + 1) // 2
+CORNER_ROWS = {f: (5, 5, 3, 2, 2) for f in (SXX, SYY, SXY, SXZ, SYZ)}
+CORNER_ROWS.update({f: (3, 3, 2) for f in (SZZ, VX, VY, VZ, BUOY)})
+CORNER_ROWS.update({f: (2, 2) for f in (LAM, MU)})
+
+
+def corner_tiles():
+    parts = [(n, f, d + 1) for f, counts in CORNER_ROWS.items() for d, n in enumerate(counts)]
+    tiles = []
+    for n, f, d in sorted(parts, reverse=True):
+        for tile in tiles:
+            used = sum(part[2] for part in tile)
+            if used + n <= ROWS:
+                tile.append((f, d, n, used))
+                break
+        else:
+            tiles.append([(f, d, n, 0)])
+    return tiles
+
+
+CORNER_TILES = corner_tiles()
+CORNERS = len(CORNER_TILES)
+SLOT_STEP = 256
 VMEM_LIMIT = 40 * 1024 * 1024
 UNROLL = 8
 SAMPLE_UNROLL = 4
-PART = 4
+PART = 6
 VMEM = pl.BlockSpec(memory_space=pltpu.VMEM)
 HBM = pl.BlockSpec(memory_space=pltpu.HBM)
+IDLE = pl.CostEstimate(flops=0, bytes_accessed=0, transcendentals=0)
 
 
 def f32(*shape):
@@ -59,7 +75,7 @@
     def __init__(self, block, counts):
         self.cx, self.cy, self.cz = block
         self.gx, self.gy, self.gz = counts
-        self.x_pairs = ("even", "odd") if self.gx > 2 else ("even",)
+        self.x_pairs = ("odd", "even") if self.gx > 2 else ("even",)
         self.y_pairs = ("even", "odd") if self.gy > 2 else ("even",)
         self.rows = self.cy + ROWS * len(self.y_pairs)
         self.layers = self.cx + 2 * HALO
@@ -73,8 +89,8 @@
         return out
 
     def pieces(self):
-        out = [(("x", a), LAYERS * self.tiles_y) for a in self.x_pairs]
-        out += [(("y", b), FIELDS * self.cx) for b in self.y_pairs]
+        out = [(("y", b), FIELDS * self.cx) for b in self.y_pairs]
+        out += [(("x", a), LAYERS * self.tiles_y) for a in self.x_pairs]
         out += [(("d", a, b), CORNERS) for b in self.y_pairs for a in self.x_pairs]
         return out
 
@@ -94,7 +110,6 @@
 def pack_kernel(grid, *refs):
     fields = refs[0]
     outs = refs[1:]
-    own = outs[-1]
     sub = iota(0)
     for (name, _), out in zip(grid.pieces(), outs):
         if name[0] == "x":
@@ -116,15 +131,20 @@
                 layer = jnp.where(high, grid.cx - distance, distance - 1)
                 return fields[field, layer, pl.ds(row, ROWS), :]
 
-            for i, (f, d) in enumerate(CORNER_WHOLE):
-                out[i] = tile(f, d)
-            for i in range(0, len(CORNER_HALF), 2):
-                first = tile(*CORNER_HALF[i])
-                second = tile(*CORNER_HALF[min(i + 1, len(CORNER_HALF) - 1)])
-                turned = pltpu.roll(jnp.where(up, first, second), 4, 0)
-                lower = jnp.where(up, turned, first)
-                upper = jnp.where(up, second, turned)
-                out[len(CORNER_WHOLE) + i // 2] = jnp.where(sub < 4, lower, upper)
+            for i, parts in enumerate(CORNER_TILES):
+                packed = None
+                for f, d, n, first in parts:
+                    whole = tile(f, d)
+                    turned = jnp.where(
+                        up,
+                        pltpu.roll(whole, (first + n) % ROWS, 0),
+                        pltpu.roll(whole, first, 0) if first else whole,
+                    )
+                    packed = turned if packed is None else jnp.where(sub < first, packed, turned)
+                out[i] = packed
+
+
+def own_strip_kernel(grid, after, fields, own):
     head = jnp.where(lax.axis_index("gz") == 0, STRIP, 0)
     tiles = [(f, x, r) for f in range(FIELDS) for x in range(grid.cx) for r in range(grid.tiles_y)]
     for g in range(groups(len(tiles))):
@@ -156,39 +176,47 @@
         base += groups(count)
 
 
-def slot_kernel(width, capacity, cz, cells_ref, writers_ref, lanes_ref, rows_ref):
+def slot_kernel(width, cz, cells_ref, writers_ref, lanes_ref, rows_ref, spans_ref):
     count = cells_ref.shape[1]
     cells = cells_ref[...]
     writers = writers_ref[...]
-    padded = max(16, width)
-    named = (iota(0, (padded, count)) == writers).astype(jnp.float32)
+    padded = max(LANES, width)
+    writer = iota(0, (padded, count))
+    named = (writer == writers).astype(jnp.float32)
+    fewer = (writers < writer).astype(jnp.float32)
     earlier = (iota(0, (count, count)) < iota(1, (count, count))).astype(jnp.float32)
     before = jnp.dot(
         named.astype(jnp.bfloat16), earlier.astype(jnp.bfloat16), preferred_element_type=jnp.float32
     )
-    position = jnp.sum(before * named, axis=0, keepdims=True).astype(jnp.int32)
-    target = writers * capacity + position
+    start = jnp.sum(fewer, axis=1, keepdims=True)
+    rank = jnp.sum((before + start) * named, axis=0, keepdims=True).astype(jnp.int32)
+    ones = jnp.ones((16, count), jnp.bfloat16)
+
+    def across(marks):
+        return lax.dot_general(
+            ones,
+            marks.astype(jnp.bfloat16),
+            (((1,), (1,)), ((), ())),
+            preferred_element_type=jnp.float32,
+        ).astype(jnp.int32)
+
+    spans_ref[0:ROWS, :] = across(fewer)[0:ROWS]
+    spans_ref[ROWS : 2 * ROWS, :] = across(named)[0:ROWS]
     which = iota(0, (16, count))
-    lane = lax.rem(cells, cz)
-    row = lax.div(cells, cz)
-    values = jnp.where(which == 0, lane, jnp.where(which == 1, row, jnp.where(which == 2, 1, 0)))
+    values = jnp.where(which == 0, lax.rem(cells, cz), jnp.where(which == 1, lax.div(cells, cz), 0))
     values = values.astype(jnp.float32).astype(jnp.bfloat16)
-    step = 256
-    for n in range(width * capacity // step):
-        hit = (iota(0, (step, count)) + n * step == target).astype(jnp.float32)
+    for n in range(0, count, SLOT_STEP):
+        hit = (iota(0, (SLOT_STEP, count)) + n == rank).astype(jnp.float32)
         table = lax.dot_general(
             values,
             hit.astype(jnp.bfloat16),
             (((1,), (1,)), ((), ())),
             preferred_element_type=jnp.float32,
-        )
-        lane_of = jnp.where(table[2:3] > 0.5, table[0:1], -1.0).astype(jnp.int32)
-        marks = (iota(0, (cz, step)) == lane_of).astype(jnp.float32).astype(jnp.bfloat16)
-        lanes_ref[0:cz, n * step : (n + 1) * step] = marks
-        lanes_ref[cz : 2 * cz, n * step : (n + 1) * step] = marks
-        rows_ref[:, n * step : (n + 1) * step] = jnp.broadcast_to(
-            table[1:2].astype(jnp.int32), (ROWS, step)
-        )
+        ).astype(jnp.int32)
+        marks = (iota(0, (cz, SLOT_STEP)) == table[0:1]).astype(jnp.float32).astype(jnp.bfloat16)
+        lanes_ref[0:cz, n : n + SLOT_STEP] = marks
+        lanes_ref[cz : 2 * cz, n : n + SLOT_STEP] = marks
+        rows_ref[:, n : n + SLOT_STEP] = jnp.broadcast_to(table[1:2], (ROWS, SLOT_STEP))
 
 
 def edge(grid, up):
@@ -246,14 +274,15 @@
             layer = jnp.where(high, HALO + cx - 1 + distance, HALO - distance)
             ext[field, layer, pl.ds(place, ROWS), :] = clear(tile)
 
-        for i, (f, d) in enumerate(CORNER_WHOLE):
-            put(f, d, tile_of(i))
-        for i in range(0, len(CORNER_HALF), 2):
-            tile = tile_of(len(CORNER_WHOLE) + i // 2)
-            turned = pltpu.roll(tile, 4, 0)
-            put(*CORNER_HALF[i], jnp.where(up, tile, turned))
-            if i + 1 < len(CORNER_HALF):
-                put(*CORNER_HALF[i + 1], jnp.where(up, turned, tile))
+        for i, parts in enumerate(CORNER_TILES):
+            tile = tile_of(i)
+            for f, d, n, first in parts:
+                turned = jnp.where(
+                    up,
+                    pltpu.roll(tile, ROWS - first, 0) if first else tile,
+                    pltpu.roll(tile, (-first - n) % ROWS, 0),
+                )
+                put(f, d, turned)
 
 
 def known_lanes():
@@ -288,13 +317,14 @@
     lay_halos(grid, ext, tiles)
 
 
-def main_kernel(grid, *refs):
-    strips, lanes_ref, rows_ref, site_hbm, wavelet_hbm = refs[2:7]
-    ext, beside, velocity_out, table_out = refs[7:11]
-    sampled, site_ref, wavelet_ref, sems = refs[11:]
+def main_kernel(grid, width, capacity, *refs):
+    strips, lanes_ref, rows_ref, spans_vmem, site_hbm, wavelet_hbm = refs[2:8]
+    ext, beside, velocity_out, table_out = refs[8:12]
+    sampled, compact, site_ref, wavelet_ref, spans_ref, sems = refs[12:]
     copies = (
         pltpu.make_async_copy(site_hbm, site_ref, sems.at[0]),
         pltpu.make_async_copy(wavelet_hbm, wavelet_ref, sems.at[1]),
+        pltpu.make_async_copy(spans_vmem, spans_ref, sems.at[2]),
     )
     for copy in copies:
         copy.start()
@@ -330,7 +360,8 @@
     def moved_z(a, offset):
         own = pltpu.roll(a[0], -offset % cz, 1)
         far = pltpu.roll(a[1], -offset % cz, 1)
-        inside = lane_all < cz - offset if offset > 0 else lane_all >= -offset
+        inside = lane_all[: own.shape[0]]
+        inside = inside < cz - offset if offset > 0 else inside >= -offset
         return jnp.where(inside, own, far), jnp.where(inside, far, own)
 
     def forward(a, move):
@@ -365,24 +396,41 @@
             block[VY, y] = block[VY, y] + b * rate_y[h]
             block[VZ, y] = block[VZ, y] + b * rate_z[h]
 
-    def stress_layer(x):
+    def stress_layer(x, last=False):
+        kept = cy if last else rows
+
+        def cut(a):
+            return tuple(v[:kept] for v in a)
+
+        def across_y(move, a):
+            return tuple(cut(v) for v in move(a, moved_y))
+
+        def along(move, a):
+            return move(cut(a), moved_z)
+
+        def beyond(field, at):
+            return tuple(cut(v) for v in along_x(field, at))
+
         vx, vy, vz = pair(VX, x), pair(VY, x), pair(VZ, x)
-        gxx = total(along_x(VX, x - 1))
-        gyy = total(backward(vy, moved_y))
-        gzz = total(backward(vz, moved_z))
-        gxy = total(forward(vx, moved_y), along_x(VY, x))
-        gxz = total(forward(vx, moved_z), along_x(VZ, x))
-        gyz = total(forward(vy, moved_z), forward(vz, moved_y))
-        for h, block in enumerate((ext, beside)):
-            shear = scale * block[MU, x]
-            volume = scale * block[LAM, x] * (gxx[h] + gyy[h] + gzz[h])
+        gxx = total(beyond(VX, x - 1))
+        gyy = total(across_y(backward, vy))
+        gzz = total(along(backward, vz))
+        gxy = total(across_y(forward, vx), beyond(VY, x))
+        gxz = total(along(forward, vx), beyond(VZ, x))
+        gyz = total(along(forward, vy), across_y(forward, vz))
+        for h, block in enumerate((ext,) if last else (ext, beside)):
+            shear = scale * block[MU, x, 0:kept]
+            volume = scale * block[LAM, x, 0:kept] * (gxx[h] + gyy[h] + gzz[h])
             twice = 2.0 * shear
-            block[SXX, x] = block[SXX, x] + (twice * gxx[h] + volume)
-            block[SYY, x] = block[SYY, x] + (twice * gyy[h] + volume)
-            block[SZZ, x] = block[SZZ, x] + (twice * gzz[h] + volume)
-            block[SXY, x] = block[SXY, x] + shear * gxy[h]
-            block[SXZ, x] = block[SXZ, x] + shear * gxz[h]
-            block[SYZ, x] = block[SYZ, x] + shear * gyz[h]
+            for f, change in (
+                (SXX, twice * gxx[h] + volume),
+                (SYY, twice * gyy[h] + volume),
+                (SZZ, twice * gzz[h] + volume),
+                (SXY, shear * gxy[h]),
+                (SXZ, shear * gxz[h]),
+                (SYZ, shear * gyz[h]),
+            ):
+                block[f, x, 0:kept] = block[f, x, 0:kept] + change
 
     def loop(first, last, body, unroll=UNROLL):
         def step(x, carry):
@@ -432,13 +480,13 @@
             sampled[pl.ds(row, cy), 0:cz] = head
             sampled[pl.ds(row, cy), cz : 2 * cz] = tail
 
-    step_slots = 256
     block = cx * cy
 
     def sample(k, carry):
-        where = pl.ds(pl.multiple_of(k * step_slots, step_slots), step_slots)
+        where = pl.ds(pl.multiple_of(k * SLOT_STEP, SLOT_STEP), SLOT_STEP)
+        to_lanes = pl.ds(pl.multiple_of(k * SLOT_STEP + LANES, LANES), SLOT_STEP)
         row = rows_ref[:, where]
-        marks = [row == r * ROWS + iota(0, (ROWS, step_slots)) for r in range(block // ROWS)]
+        marks = [row == r * ROWS + iota(0, (ROWS, SLOT_STEP)) for r in range(block // ROWS)]
         for part in range(6 * STEPS // PART):
             found = jnp.dot(
                 sampled[part * PART * block : (part + 1) * PART * block, :],
@@ -446,13 +494,31 @@
                 preferred_element_type=jnp.float32,
             )
             for f in range(PART):
-                acc = jnp.zeros((ROWS, step_slots), jnp.float32)
+                acc = jnp.zeros((ROWS, SLOT_STEP), jnp.float32)
                 for r in range(block // ROWS):
                     tile = found[f * block + r * ROWS : f * block + r * ROWS + ROWS]
                     acc = acc + jnp.where(marks[r], tile, 0.0)
                 to = part * PART + f
-                table_out[k, to : to + 1, :] = jnp.sum(acc, axis=0, keepdims=True)
+                compact[to : to + 1, to_lanes] = jnp.sum(acc, axis=0, keepdims=True)
         return carry
+
+    def spread():
+        values = 6 * STEPS
+        lanes_at = iota(1, (values, LANES))
+        for t in range(width * capacity // LANES):
+            out = jnp.zeros((values, LANES), jnp.float32)
+            for w in range(t * LANES // capacity, -(-(t + 1) * LANES // capacity)):
+                skip = t * LANES - w * capacity
+                start = spans_ref[0, w] + skip + LANES
+                base = pl.multiple_of(lax.div(start, LANES) * LANES, LANES)
+                shift = lax.rem(start, LANES)
+                near = pltpu.roll(compact[0:values, pl.ds(base, LANES)], LANES - shift, 1)
+                far = pltpu.roll(compact[0:values, pl.ds(base + LANES, LANES)], LANES - shift, 1)
+                place = lanes_at + skip
+                mine = jnp.logical_and(place >= 0, place < spans_ref[ROWS, w])
+                out = jnp.where(mine, jnp.where(lanes_at < LANES - shift, near, far), out)
+            per = 256 // LANES
+            table_out[t // per, :, t % per * LANES : (t % per + 1) * LANES] = out
 
     inject(0)
     loop(-3, cx + 2, stress_layer)
@@ -460,12 +526,13 @@
     loop(-2, cx, velocity_layer)
     inject(1)
     leaving = pltpu.make_async_copy(
-        ext.at[VX : VX + 3, HALO : HALO + cx, 0:cy, :], velocity_out, sems.at[2]
+        ext.at[VX : VX + 3, HALO : HALO + cx, 0:cy, :], velocity_out, sems.at[3]
     )
     leaving.start()
-    loop(0, cx - 1, stress_layer)
+    loop(0, cx - 1, functools.partial(stress_layer, last=True))
     loop(0, cx - 1, functools.partial(strain_layer, 1))
-    lax.fori_loop(0, lanes_ref.shape[1] // step_slots, sample, 0, unroll=SAMPLE_UNROLL)
+    lax.fori_loop(0, lanes_ref.shape[1] // SLOT_STEP, sample, 0, unroll=SAMPLE_UNROLL)
+    spread()
     leaving.wait()
 
 
@@ -483,10 +550,9 @@
     )
     packed = pl.pallas_call(
         lambda *refs: pack_kernel(grid, *refs),
-        out_shape=[f32(*grid.shape(name)) for name, _ in pieces]
-        + [f32(groups(own_tiles), ROWS, LANES)],
+        out_shape=[f32(*grid.shape(name)) for name, _ in pieces],
         in_specs=[VMEM],
-        out_specs=[VMEM] * (len(pieces) + 1),
+        out_specs=[VMEM] * len(pieces),
         compiler_params=params,
         name="pack_halos",
     )(fields)
@@ -504,23 +570,34 @@
                 for b, d in grid.pairs(grid.gy, name[2])
             ]
             arrived.append(lax.ppermute(piece, ("gx", "gy"), pairs))
-    own_strips = lax.ppermute(packed[-1], "gz", swap)
-
     count = save_cells.size
     width = grid.gx * grid.gy
     capacity = max(2, 2 * count // width)
     slots = width * capacity
-    lanes, rows = pl.pallas_call(
-        lambda *refs: slot_kernel(width, capacity, grid.cz, *refs),
+    lanes, rows, spans = pl.pallas_call(
+        functools.partial(slot_kernel, width, grid.cz),
         out_shape=[
-            jax.ShapeDtypeStruct((2 * grid.cz, slots), jnp.bfloat16),
-            jax.ShapeDtypeStruct((ROWS, slots), jnp.int32),
+            jax.ShapeDtypeStruct((2 * grid.cz, count), jnp.bfloat16),
+            jax.ShapeDtypeStruct((ROWS, count), jnp.int32),
+            jax.ShapeDtypeStruct((2 * ROWS, max(LANES, width)), jnp.int32),
         ],
         in_specs=[VMEM] * 2,
-        out_specs=[VMEM] * 2,
+        out_specs=[VMEM] * 3,
         compiler_params=params,
+        cost_estimate=IDLE,
         name="slot_tables",
     )(save_cells.reshape(1, count), save_writer.reshape(1, count))
+
+    own_strips = pl.pallas_call(
+        functools.partial(own_strip_kernel, grid),
+        out_shape=f32(groups(own_tiles), ROWS, LANES),
+        in_specs=[VMEM] * 2,
+        out_specs=VMEM,
+        compiler_params=params,
+        cost_estimate=IDLE,
+        name="pack_own_strips",
+    )(rows, fields)
+    own_strips = lax.ppermute(own_strips, "gz", swap)
 
     extended = f32(FIELDS, grid.layers, grid.rows, grid.cz)
     block, beside = pl.pallas_call(
@@ -529,6 +606,7 @@
         in_specs=[VMEM] * 2,
         out_specs=[VMEM] * 2,
         compiler_params=params,
+        cost_estimate=IDLE,
         name="begin_block",
     )(fields, own_strips)
 
@@ -553,25 +631,27 @@
     )(block, *arrived)
 
     _, _, velocity, table = pl.pallas_call(
-        lambda *refs: main_kernel(grid, *refs),
+        functools.partial(main_kernel, grid, width, capacity),
         out_shape=[
             extended,
             extended,
             f32(*velocity_start.shape),
             f32(slots // 256, 6 * STEPS, 256),
         ],
-        in_specs=[VMEM] * 5 + [HBM] * 2,
+        in_specs=[VMEM] * 6 + [HBM] * 2,
         out_specs=[VMEM, VMEM, HBM, VMEM],
         scratch_shapes=[
             pltpu.VMEM((STEPS * 6 * grid.cx * grid.cy, 2 * grid.cz), jnp.bfloat16),
+            pltpu.VMEM((16, count + 4 * LANES), jnp.float32),
             pltpu.SMEM(force_site.shape, jnp.int32),
             pltpu.SMEM(force_wavelet.shape, jnp.float32),
-            pltpu.SemaphoreType.DMA((3,)),
+            pltpu.SMEM(spans.shape, jnp.int32),
+            pltpu.SemaphoreType.DMA((4,)),
         ],
         input_output_aliases={0: 0, 1: 1},
         compiler_params=params,
         name="two_steps",
-    )(block, beside, strips, lanes, rows, force_site, force_wavelet)
+    )(block, beside, strips, lanes, rows, spans, force_site, force_wavelet)
 
     values = 6 * STEPS
     if capacity != 256:

time: 45.3 us -> 41.5 us (0.916)
  blocking collectives: 15.3 us -> 11 us
  Pallas kernels: 10.2 us -> 8.32 us
  waiting for transfers between devices: 4.32 us -> 5.96 us
  starting transfers between devices: 10.4 us -> 11.1 us
    all_to_all x1, blocking collectives: 15.3 us -> 11 us  [per_device(): lax.all_to_all(table, ('gx', 'gy'), split_axis=0, concat_axis=0, tiled=True)]
    ppermute x2, starting transfers between devices: 3.77 us -> 6.57 us  [per_device(): arrived.append(lax.ppermute(piece, 'gx', grid.pairs(grid.gx, name[1])))]
    ppermute x2, starting transfers between devices: 5 us -> 2.86 us  [per_device(): arrived.append(lax.ppermute(piece, ('gx', 'gy'), pairs))]
    pallas_call x2 -> x3, Pallas kernels: 8.78 us -> 7.23 us  [the longest x1 5.7 us: per_device(): pl.pallas_call(functools.partial(main_kernel, grid, width, capacity), out...]
    ppermute x2, waiting for transfers between devices: 3.83 us -> 4.93 us  [per_device(): arrived.append(lax.ppermute(piece, ('gx', 'gy'), pairs))]
    ppermute x1, waiting for transfers between devices: 0.01 us -> 0.54 us  [per_device(): own_strips = lax.ppermute(own_strips, 'gz', swap)]
  transfers between devices with their start and end apart: 7 -> 7, of which waited for: 2 -> 3; matrix products, arithmetic and copies ran while one was open for 0% -> 0% of each run, Pallas kernels for 5% -> 5%
where the time goes in v3:
time: 41.5 us; the launch traced here: 41.2 us
  starting transfers between devices  11.1 us (27%)
  blocking collectives  11 us (27%)
  Pallas kernels  8.32 us (20%)
  waiting for transfers between devices  5.96 us (14%)
  local copies, waits for them, and re-layouts  2.21 us (5%)
  between operations  1.4 us (3%)
  other arithmetic  1.27 us (3%)
    all_to_all x1, blocking collectives, per_device(): lax.all_to_all(table, ('gx', 'gy'), split_axis=0, concat_axis=0, tiled=True)  11 us
    ppermute x2, starting transfers between devices, per_device(): arrived.append(lax.ppermute(piece, 'gx', grid.pairs(grid.gx, name[1])))  6.57 us
    pallas_call x1, Pallas kernels, per_device(): pl.pallas_call(functools.partial(main_kernel, grid, width, capacity), out...  5.7 us
    ppermute x2, waiting for transfers between devices, per_device(): arrived.append(lax.ppermute(piece, ('gx', 'gy'), pairs))  4.93 us
    ppermute x2, starting transfers between devices, per_device(): arrived.append(lax.ppermute(piece, ('gx', 'gy'), pairs))  2.86 us
    ppermute x1, starting transfers between devices, per_device(): arrived.append(lax.ppermute(piece, 'gy', grid.pairs(grid.gy, name[1])))  1.49 us
    unnamed x6, local copies, waits for them, and re-layouts  1.41 us
    add x1, other arithmetic, per_device(): sum((lax.pad(part, jnp.float32(0.0), [(first, FIELDS - first - part.shape...  1.27 us
  transfers between devices with their start and end apart: 7, of which 3 were waited for; matrix products, arithmetic and copies ran while one was open for 0% of the time, Pallas kernels for 5%

profile of v3, /device:TPU:0, one launch (start us, length us, event | category | flops | bytes accessed | tf_op | source)
XLA Modules:
  0.0 41.2 jit_solution(963732733978582380)
XLA Ops:
  0.6 1.3 %pad_add_fusion.fields.refs_0_ = f32[12,8,16,128]{3,2,1,0:T(8,128)S(1)} fusion(f32[3,8,16,128]{3,2,1,0:T(8,128)} %param.9, f32[3,8,16,128]{3,2,1,0:T(8,128)} %param.7, f32[6,8,16,128]{3,2,1,0:T(8,128)} %param.8), kind=kLoop, calls=%fused_computation | loop fusion | flops 393216 | bytes 1572864 | tf_op jit(solution)/shard_map/add | solution.py:547
  1.9 0.2 pack_halos.1
  2.1 0.7 %collective-permute-start.2 = (f32[59,16,128]{2,1,0:T(8,128)S(1)}, f32[59,16,128]{2,1,0:T(8,128)S(1)}, u32[]{:S(2)}, u32[]{:S(2)}) collective-permute-start(f32[59,16,128]{2,1,0:T(8,128)S(1)} %get-tuple-element.17), channel_id=1, source_target_pairs={{4,8},{8,4},{5,9},{9,5},{6,10},{10,6},{7,11},{11,7},{20,24},{24,20... | collective-permute-start | bytes 1449992 | tf_op jit(solution)/shard_map/ppermute | solution.py:563
  2.8 5.9 %collective-permute-start.3 = (f32[59,16,128]{2,1,0:T(8,128)S(1)}, f32[59,16,128]{2,1,0:T(8,128)S(1)}, u32[]{:S(2)}, u32[]{:S(2)}) collective-permute-start(f32[59,16,128]{2,1,0:T(8,128)S(1)} %get-tuple-element.18), channel_id=1, source_target_pairs={{0,4},{4,0},{8,12},{12,8},{1,5},{5,1},{9,13},{13,9},{2,6},{6,2},{1... | collective-permute-start | bytes 1449992 | tf_op jit(solution)/shard_map/ppermute | solution.py:563
  8.7 1.5 %collective-permute-start.1 = (f32[12,8,8,128]{3,2,1,0:T(8,128)S(1)}, f32[12,8,8,128]{3,2,1,0:T(8,128)S(1)}, u32[]{:S(2)}, u32[]{:S(2)}) collective-permute-start(f32[12,8,8,128]{3,2,1,0:T(8,128)S(1)} %get-tuple-element.16), channel_id=1, source_target_pairs={{0,2},{2,0},{1,3},{3,1},{4,6},{6,4},{5,7},{7,5},{8,10},{10,8},{9,1... | collective-permute-start | bytes 1179656 | tf_op jit(solution)/shard_map/ppermute | solution.py:565
  10.1 0.7 %copy-done = s32[1,1,1,1024]{3,2,1,0:T(1,128)S(1)} copy-done((s32[1,1,1,1024]{3,2,1,0:T(1,128)S(1)}, s32[1,1,1,1024]{3,2,1,0:T(1,128)}, u32[]{:S(2)}) %copy-start) | copy-done | bytes 4120
  10.8 0.7 %copy-done.1 = s32[1,1,1,1024,1]{3,4,2,1,0:T(1,128)S(1)} copy-done((s32[1,1,1,1024,1]{3,4,2,1,0:T(1,128)S(1)}, s32[1,1,1,1024,1]{3,4,2,1,0:T(1,128)}, u32[]{:S(2)}) %copy-start.1) | copy-done | bytes 4120
  11.5 1.3 %slot_tables.1 = (bf16[256,1024]{1,0:T(8,128)(2,1)S(1)}, s32[8,1024]{1,0:T(8,128)S(1)}, s32[16,128]{1,0:T(8,128)S(1)}) custom-call(s32[1,1024]{1,0:T(1,128)S(1)} %bitcast.3, s32[1,1024]{1,0:T(1,128)S(1)} %bitcast.4), custom_call_target="tpu_custom_call" | custom-call | tf_op jit(solution)/shard_map/slot_tables/pallas_call | solution.py:577
  12.8 0.3 pack_own_strips.1
  13.1 0.1 collective-permute-start
  13.1 0.7 %collective-permute-start.4 = (f32[17,8,128]{2,1,0:T(8,128)S(1)}, f32[17,8,128]{2,1,0:T(8,128)S(1)}, u32[]{:S(2)}, u32[]{:S(2)}) collective-permute-start(f32[17,8,128]{2,1,0:T(8,128)S(1)} %get-tuple-element.19), channel_id=1, source_target_pairs={{4,10},{6,8},{8,6},{10,4},{5,11},{7,9},{9,7},{11,5},{20,26},{22,24... | collective-permute-start | bytes 208904 | tf_op jit(solution)/shard_map/ppermute | solution.py:572
  13.8 0.5 %collective-permute-done.refs_1_ = f32[12,8,128]{2,1,0:T(8,128)S(1)} collective-permute-done((f32[12,8,128]{2,1,0:T(8,128)S(1)}, f32[12,8,128]{2,1,0:T(8,128)S(1)}, u32[]{:S(2)}, u32[]{:S(2)}) %collective-permute-start) | collective-permute-done | bytes 49184 | tf_op jit(solution)/shard_map/ppermute | solution.py:600
  14.4 2.2 %collective-permute-start.5 = (f32[17,8,128]{2,1,0:T(8,128)S(1)}, f32[17,8,128]{2,1,0:T(8,128)S(1)}, u32[]{:S(2)}, u32[]{:S(2)}) collective-permute-start(f32[17,8,128]{2,1,0:T(8,128)S(1)} %get-tuple-element.20), channel_id=1, source_target_pairs={{0,6},{2,4},{4,2},{6,0},{8,14},{10,12},{12,10},{14,8},{1,7},{3,5},... | collective-permute-start | bytes 208904 | tf_op jit(solution)/shard_map/ppermute | solution.py:572
  16.6 0.3 begin_block.1
  16.9 4.9 %collective-permute-done.5.refs_5_.refs_7_ = f32[17,8,128]{2,1,0:T(8,128)S(1)} collective-permute-done((f32[17,8,128]{2,1,0:T(8,128)S(1)}, f32[17,8,128]{2,1,0:T(8,128)S(1)}, u32[]{:S(2)}, u32[]{:S(2)}) %collective-permute-start.5) | collective-permute-done | bytes 69664 | tf_op jit(solution)/shard_map/ppermute | solution.py:572
  21.8 0.5 %pack_strips.1 = f32[26,8,128]{2,1,0:T(8,128)S(1)} custom-call(s32[8,1024]{1,0:T(8,128)S(1)} %get-tuple-element.14.after.refs_0_.refs_4_, f32[12,20,24,128]{3,2,1,0:T(8,128)S(1)} %get-tuple-element.15.refs_0_.refs_1_, f32[12,20,24,128]{3,2,1,0:T(8,128)S(1)} %get-tuple-element.21.refs_2_.refs_1_, ...), custom_call_target="tpu_custom_call" | custom-call | tf_op jit(solution)/shard_map/pack_strips/pallas_call | solution.py:613
  22.3 0.1 collective-permute-start.6
  23.1 0.2 assemble.1.refs_0_
  23.2 0.5 %collective-permute-done.6.refs_2_ = f32[26,8,128]{2,1,0:T(8,128)S(1)} collective-permute-done((f32[26,8,128]{2,1,0:T(8,128)S(1)}, f32[26,8,128]{2,1,0:T(8,128)S(1)}, u32[]{:S(2)}, u32[]{:S(2)}) %collective-permute-start.6) | collective-permute-done | bytes 106528 | tf_op jit(solution)/shard_map/ppermute | solution.py:621
  23.7 0.0 copy-done.2
  23.7 5.7 %two_steps.1 = (f32[12,20,24,128]{3,2,1,0:T(8,128)S(1)}, f32[12,20,24,128]{3,2,1,0:T(8,128)S(1)}, f32[3,8,16,128]{3,2,1,0:T(8,128)}, f32[8,12,256]{2,1,0:T(8,128)S(1)}) custom-call(f32[12,20,24,128]{3,2,1,0:T(8,128)S(1)} %assemble.1.refs_0_, f32[12,20,24,128]{3,2,1,0:T(8,128)S(1)} %get-tuple-element.21.refs_2_.refs_1_, ...), custom_call_target="tpu_custom_call", output_to_operand_aliasing={{0}: (0, {}), {1}: (1, {})} | custom-call | tf_op jit(solution)/shard_map/two_steps/pallas_call | solution.py:633
  29.4 11.0 %all_to_all.5 = f32[8,12,256]{2,1,0:T(8,128)S(1)} all-to-all(f32[8,12,256]{2,1,0:T(8,128)S(1)} %get-tuple-element.25), channel_id=1, replica_groups=mesh['runs'=2,'gx'=4,'gy'=2,'gz'=2] {'gx','gy'}, dimensions={0} | all-to-all | bytes 196608 | tf_op jit(solution)/shard_map/all_to_all | solution.py:659
  40.4 0.1 copy.12
  40.5 0.7 %reshape.16 = f32[1,12,2048]{2,0,1:T(1,128)} reshape(f32[12,8,256]{2,1,0:T(8,128)S(1)} %copy.12) | data formatting | bytes 196608 | tf_op jit(solution)/shard_map/reshape | solution.py:660
  (7 shorter events, 0.0 us)
Async XLA Ops:
  2.1 19.8 %collective-permute-start.2 = (f32[59,16,128]{2,1,0:T(8,128)S(1)}, f32[59,16,128]{2,1,0:T(8,128)S(1)}, u32[]{:S(2)}, u32[]{:S(2)}) collective-permute-start(f32[59,16,128]{2,1,0:T(8,128)S(1)} %get-tuple-element.17), channel_id=1, source_target_pairs={{4,8},{8,4},{5,9},{9,5},{6,10},{10,6},{7,11},{11,7},{20,24},{24,20... | collective-permute-start | bytes 1449992 | tf_op jit(solution)/shard_map/ppermute | solution.py:563
  2.8 19.1 %collective-permute-start.3 = (f32[59,16,128]{2,1,0:T(8,128)S(1)}, f32[59,16,128]{2,1,0:T(8,128)S(1)}, u32[]{:S(2)}, u32[]{:S(2)}) collective-permute-start(f32[59,16,128]{2,1,0:T(8,128)S(1)} %get-tuple-element.18), channel_id=1, source_target_pairs={{0,4},{4,0},{8,12},{12,8},{1,5},{5,1},{9,13},{13,9},{2,6},{6,2},{1... | collective-permute-start | bytes 1449992 | tf_op jit(solution)/shard_map/ppermute | solution.py:563
  8.7 13.2 %collective-permute-start.1 = (f32[12,8,8,128]{3,2,1,0:T(8,128)S(1)}, f32[12,8,8,128]{3,2,1,0:T(8,128)S(1)}, u32[]{:S(2)}, u32[]{:S(2)}) collective-permute-start(f32[12,8,8,128]{3,2,1,0:T(8,128)S(1)} %get-tuple-element.16), channel_id=1, source_target_pairs={{0,2},{2,0},{1,3},{3,1},{4,6},{6,4},{5,7},{7,5},{8,10},{10,8},{9,1... | collective-permute-start | bytes 1179656 | tf_op jit(solution)/shard_map/ppermute | solution.py:565
  10.1 0.7 %copy-start = (s32[1,1,1,1024]{3,2,1,0:T(1,128)S(1)}, s32[1,1,1,1024]{3,2,1,0:T(1,128)}, u32[]{:S(2)}) copy-start(s32[1,1,1,1024]{3,2,1,0:T(1,128)} %param.12) | copy-start | bytes 12292
  10.8 0.7 %copy-start.1 = (s32[1,1,1,1024,1]{3,4,2,1,0:T(1,128)S(1)}, s32[1,1,1,1024,1]{3,4,2,1,0:T(1,128)}, u32[]{:S(2)}) copy-start(s32[1,1,1,1024,1]{3,4,2,1,0:T(1,128)} %param.13) | copy-start | bytes 12292
  13.1 1.3 %collective-permute-start = (f32[12,8,128]{2,1,0:T(8,128)S(1)}, f32[12,8,128]{2,1,0:T(8,128)S(1)}, u32[]{:S(2)}, u32[]{:S(2)}) collective-permute-start(f32[12,8,128]{2,1,0:T(8,128)S(1)} %pack_own_strips.1), channel_id=1, source_target_pairs={{0,1},{1,0},{2,3},{3,2},{4,5},{5,4},{6,7},{7,6},{8,9},{9,8},{10,11... | collective-permute-start | bytes 147464 | tf_op jit(solution)/shard_map/ppermute | solution.py:600
  13.1 3.8 %collective-permute-start.4 = (f32[17,8,128]{2,1,0:T(8,128)S(1)}, f32[17,8,128]{2,1,0:T(8,128)S(1)}, u32[]{:S(2)}, u32[]{:S(2)}) collective-permute-start(f32[17,8,128]{2,1,0:T(8,128)S(1)} %get-tuple-element.19), channel_id=1, source_target_pairs={{4,10},{6,8},{8,6},{10,4},{5,11},{7,9},{9,7},{11,5},{20,26},{22,24... | collective-permute-start | bytes 208904 | tf_op jit(solution)/shard_map/ppermute | solution.py:572
  14.4 7.5 %collective-permute-start.5 = (f32[17,8,128]{2,1,0:T(8,128)S(1)}, f32[17,8,128]{2,1,0:T(8,128)S(1)}, u32[]{:S(2)}, u32[]{:S(2)}) collective-permute-start(f32[17,8,128]{2,1,0:T(8,128)S(1)} %get-tuple-element.20), channel_id=1, source_target_pairs={{0,6},{2,4},{4,2},{6,0},{8,14},{10,12},{12,10},{14,8},{1,7},{3,5},... | collective-permute-start | bytes 208904 | tf_op jit(solution)/shard_map/ppermute | solution.py:572
  22.3 1.4 %collective-permute-start.6 = (f32[26,8,128]{2,1,0:T(8,128)S(1)}, f32[26,8,128]{2,1,0:T(8,128)S(1)}, u32[]{:S(2)}, u32[]{:S(2)}) collective-permute-start(f32[26,8,128]{2,1,0:T(8,128)S(1)} %pack_strips.1), channel_id=1, source_target_pairs={{0,1},{1,0},{2,3},{3,2},{4,5},{5,4},{6,7},{7,6},{8,9},{9,8},{10,11... | collective-permute-start | bytes 319496 | tf_op jit(solution)/shard_map/ppermute | solution.py:621
  23.0 0.7 %copy-start.2 = (f32[2,3]{1,0:T(2,128)S(1)}, f32[2,3]{1,0:T(2,128)}, u32[]{:S(2)}) copy-start(f32[2,3]{1,0:T(2,128)} %refs_7_.1) | copy-start | bytes 76

commit v4 on v3

--- a/solution.py
+++ b/solution.py
@@ -42,8 +42,6 @@
 CORNERS = len(CORNER_TILES)
 SLOT_STEP = 256
 VMEM_LIMIT = 40 * 1024 * 1024
-UNROLL = 8
-SAMPLE_UNROLL = 4
 PART = 6
 VMEM = pl.BlockSpec(memory_space=pltpu.VMEM)
 HBM = pl.BlockSpec(memory_space=pltpu.HBM)
@@ -163,10 +161,11 @@
     return ref[at]
 
 
-def strip_kernel(grid, *refs):
+def strip_kernel(grid, own, *refs):
     out = refs[-1]
     head = jnp.where(lax.axis_index("gz") == 0, STRIP, 0)
-    base = 0
+    base = own.shape[0]
+    out[0:base] = own[...]
     for (name, count), ref in zip(grid.pieces(), refs[:-1]):
         for g in range(groups(count)):
             tiles = [
@@ -298,14 +297,13 @@
 
 
 def begin_kernel(grid, *refs):
-    fields, own_strips, ext, beside = refs
+    fields, ext = refs
 
     def own(at):
         x, r = at // grid.tiles_y % grid.cx, at % grid.tiles_y
         return fields[at // (grid.tiles_y * grid.cx), x, ROWS * r : ROWS * r + ROWS, :]
 
     lay_own(grid, ext, own)
-    lay_own(grid, beside, functools.partial(unpack, own_strips, 0))
 
 
 def assemble_kernel(grid, *refs):
@@ -318,9 +316,9 @@
 
 
 def main_kernel(grid, width, capacity, *refs):
-    strips, lanes_ref, rows_ref, spans_vmem, site_hbm, wavelet_hbm = refs[2:8]
-    ext, beside, velocity_out, table_out = refs[8:12]
-    sampled, compact, site_ref, wavelet_ref, spans_ref, sems = refs[12:]
+    strips, lanes_ref, rows_ref, spans_vmem, site_hbm, wavelet_hbm = refs[1:7]
+    ext, velocity_out, table_out = refs[7:10]
+    beside, sampled, compact, site_ref, wavelet_ref, spans_ref, sems = refs[10:]
     copies = (
         pltpu.make_async_copy(site_hbm, site_ref, sems.at[0]),
         pltpu.make_async_copy(wavelet_hbm, wavelet_ref, sems.at[1]),
@@ -333,7 +331,8 @@
     half = lax.axis_index("gz")
     sub = iota(0)
     lane = iota(1)
-    bases = [0]
+    lay_own(grid, beside, functools.partial(unpack, strips, 0))
+    bases = [groups(FIELDS * cx * grid.tiles_y)]
     for _, count in grid.pieces():
         bases.append(bases[-1] + groups(count))
     lay_halos(grid, beside, [functools.partial(unpack, strips, base) for base in bases[:-1]])
@@ -432,12 +431,12 @@
             ):
                 block[f, x, 0:kept] = block[f, x, 0:kept] + change
 
-    def loop(first, last, body, unroll=UNROLL):
+    def loop(first, last, body):
         def step(x, carry):
             body(x)
             return carry
 
-        lax.fori_loop(HALO + first, HALO + last + 1, step, 0, unroll=unroll)
+        lax.fori_loop(HALO + first, HALO + last + 1, step, 0, unroll=True)
 
     loop(-5, cx + 3, velocity_layer)
     for copy in copies:
@@ -531,7 +530,7 @@
     leaving.start()
     loop(0, cx - 1, functools.partial(stress_layer, last=True))
     loop(0, cx - 1, functools.partial(strain_layer, 1))
-    lax.fori_loop(0, lanes_ref.shape[1] // SLOT_STEP, sample, 0, unroll=SAMPLE_UNROLL)
+    lax.fori_loop(0, lanes_ref.shape[1] // SLOT_STEP, sample, 0, unroll=True)
     spread()
     leaving.wait()
 
@@ -597,27 +596,26 @@
         cost_estimate=IDLE,
         name="pack_own_strips",
     )(rows, fields)
-    own_strips = lax.ppermute(own_strips, "gz", swap)
 
     extended = f32(FIELDS, grid.layers, grid.rows, grid.cz)
-    block, beside = pl.pallas_call(
+    block = pl.pallas_call(
         lambda *refs: begin_kernel(grid, *refs),
-        out_shape=[extended] * 2,
-        in_specs=[VMEM] * 2,
-        out_specs=[VMEM] * 2,
+        out_shape=extended,
+        in_specs=[VMEM],
+        out_specs=VMEM,
         compiler_params=params,
         cost_estimate=IDLE,
         name="begin_block",
-    )(fields, own_strips)
+    )(fields)
 
     strips = pl.pallas_call(
-        lambda *refs: strip_kernel(grid, *refs[3:]),
-        out_shape=f32(sum(groups(c) for _, c in pieces), ROWS, LANES),
+        lambda *refs: strip_kernel(grid, *refs[2:]),
+        out_shape=f32(groups(own_tiles) + sum(groups(c) for _, c in pieces), ROWS, LANES),
         in_specs=[VMEM] * (len(pieces) + 3),
         out_specs=VMEM,
         compiler_params=params,
         name="pack_strips",
-    )(rows, block, beside, *arrived)
+    )(rows, block, own_strips, *arrived)
     strips = lax.ppermute(strips, "gz", swap)
 
     block = pl.pallas_call(
@@ -630,17 +628,17 @@
         name="assemble",
     )(block, *arrived)
 
-    _, _, velocity, table = pl.pallas_call(
+    _, velocity, table = pl.pallas_call(
         functools.partial(main_kernel, grid, width, capacity),
         out_shape=[
-            extended,
             extended,
             f32(*velocity_start.shape),
             f32(slots // 256, 6 * STEPS, 256),
         ],
-        in_specs=[VMEM] * 6 + [HBM] * 2,
-        out_specs=[VMEM, VMEM, HBM, VMEM],
+        in_specs=[VMEM] * 5 + [HBM] * 2,
+        out_specs=[VMEM, HBM, VMEM],
         scratch_shapes=[
+            pltpu.VMEM(extended.shape, jnp.float32),
             pltpu.VMEM((STEPS * 6 * grid.cx * grid.cy, 2 * grid.cz), jnp.bfloat16),
             pltpu.VMEM((16, count + 4 * LANES), jnp.float32),
             pltpu.SMEM(force_site.shape, jnp.int32),
@@ -648,10 +646,10 @@
             pltpu.SMEM(spans.shape, jnp.int32),
             pltpu.SemaphoreType.DMA((4,)),
         ],
-        input_output_aliases={0: 0, 1: 1},
+        input_output_aliases={0: 0},
         compiler_params=params,
         name="two_steps",
-    )(block, beside, strips, lanes, rows, spans, force_site, force_wavelet)
+    )(block, strips, lanes, rows, spans, force_site, force_wavelet)
 
     values = 6 * STEPS
     if capacity != 256:

time: 41.5 us -> 40.7 us (0.981)
  local copies, waits for them, and re-layouts: 2.21 us -> 0.82 us
  waiting for transfers between devices: 5.96 us -> 7.18 us
  Pallas kernels: 8.32 us -> 7.42 us
    ppermute x2, waiting for transfers between devices: 4.93 us -> 6.62 us  [per_device(): arrived.append(lax.ppermute(piece, ('gx', 'gy'), pairs))]
    unnamed x6, local copies, waits for them, and re-layouts: 1.41 us -> 0.01 us
    pallas_call x1, Pallas kernels: 5.7 us -> 5.03 us  [per_device(): pl.pallas_call(functools.partial(main_kernel, grid, width, capacity), out...]
    ppermute x1 -> x0, waiting for transfers between devices: 0.54 us -> none  [per_device(): own_strips = lax.ppermute(own_strips, 'gz', swap)]
    ppermute x2, starting transfers between devices: 2.86 us -> 3.39 us  [per_device(): arrived.append(lax.ppermute(piece, ('gx', 'gy'), pairs))]
  transfers between devices with their start and end apart: 7 -> 6, of which waited for: 3 -> 2; matrix products, arithmetic and copies ran while one was open for 0% -> 0% of each run, Pallas kernels for 5% -> 4%
where the time goes in v4:
time: 40.7 us; the launch traced here: 40.4 us
  starting transfers between devices  11.5 us (28%)
  blocking collectives  10.8 us (27%)
  Pallas kernels  7.42 us (18%)
  waiting for transfers between devices  7.18 us (18%)
  between operations  1.42 us (3%)
  other arithmetic  1.28 us (3%)
  local copies, waits for them, and re-layouts  0.82 us (2%)
    all_to_all x1, blocking collectives, per_device(): lax.all_to_all(table, ('gx', 'gy'), split_axis=0, concat_axis=0, tiled=True)  10.8 us
    ppermute x2, waiting for transfers between devices, per_device(): arrived.append(lax.ppermute(piece, ('gx', 'gy'), pairs))  6.62 us
    ppermute x2, starting transfers between devices, per_device(): arrived.append(lax.ppermute(piece, 'gx', grid.pairs(grid.gx, name[1])))  6.57 us
    pallas_call x1, Pallas kernels, per_device(): pl.pallas_call(functools.partial(main_kernel, grid, width, capacity), out...  5.03 us
    ppermute x2, starting transfers between devices, per_device(): arrived.append(lax.ppermute(piece, ('gx', 'gy'), pairs))  3.39 us
    ppermute x1, starting transfers between devices, per_device(): arrived.append(lax.ppermute(piece, 'gy', grid.pairs(grid.gy, name[1])))  1.49 us
    add x1, other arithmetic, per_device(): sum((lax.pad(part, jnp.float32(0.0), [(first, FIELDS - first - part.shape...  1.28 us
    pallas_call x1, Pallas kernels, per_device(): pl.pallas_call(functools.partial(slot_kernel, width, grid.cz), out_shape=...  1.26 us
  transfers between devices with their start and end apart: 6, of which 2 were waited for; matrix products, arithmetic and copies ran while one was open for 0% of the time, Pallas kernels for 4%

profile of v4, /device:TPU:0, one launch (start us, length us, event | category | flops | bytes accessed | tf_op | source)
XLA Modules:
  0.0 40.4 jit_solution(8820777767709680351)
XLA Ops:
  0.7 1.3 %pad_add_fusion.refs_0_.fields = f32[12,8,16,128]{3,2,1,0:T(8,128)S(1)} fusion(f32[3,8,16,128]{3,2,1,0:T(8,128)} %param.9, f32[3,8,16,128]{3,2,1,0:T(8,128)} %param.7, f32[6,8,16,128]{3,2,1,0:T(8,128)} %param.8), kind=kLoop, calls=%fused_computation | loop fusion | flops 393216 | bytes 1572864 | tf_op jit(solution)/shard_map/add | solution.py:546
  1.9 0.2 pack_halos.1
  2.1 0.7 %collective-permute-start.1 = (f32[59,16,128]{2,1,0:T(8,128)S(1)}, f32[59,16,128]{2,1,0:T(8,128)S(1)}, u32[]{:S(2)}, u32[]{:S(2)}) collective-permute-start(f32[59,16,128]{2,1,0:T(8,128)S(1)} %get-tuple-element.13), channel_id=1, source_target_pairs={{4,8},{8,4},{5,9},{9,5},{6,10},{10,6},{7,11},{11,7},{20,24},{24,20... | collective-permute-start | bytes 1449992 | tf_op jit(solution)/shard_map/ppermute | solution.py:562
  2.8 5.9 %collective-permute-start.2 = (f32[59,16,128]{2,1,0:T(8,128)S(1)}, f32[59,16,128]{2,1,0:T(8,128)S(1)}, u32[]{:S(2)}, u32[]{:S(2)}) collective-permute-start(f32[59,16,128]{2,1,0:T(8,128)S(1)} %get-tuple-element.14), channel_id=1, source_target_pairs={{0,4},{4,0},{8,12},{12,8},{1,5},{5,1},{9,13},{13,9},{2,6},{6,2},{1... | collective-permute-start | bytes 1449992 | tf_op jit(solution)/shard_map/ppermute | solution.py:562
  8.7 1.5 %collective-permute-start = (f32[12,8,8,128]{3,2,1,0:T(8,128)S(1)}, f32[12,8,8,128]{3,2,1,0:T(8,128)S(1)}, u32[]{:S(2)}, u32[]{:S(2)}) collective-permute-start(f32[12,8,8,128]{3,2,1,0:T(8,128)S(1)} %get-tuple-element.12), channel_id=1, source_target_pairs={{0,2},{2,0},{1,3},{3,1},{4,6},{6,4},{5,7},{7,5},{8,10},{10,8},{9,1... | collective-permute-start | bytes 1179656 | tf_op jit(solution)/shard_map/ppermute | solution.py:564
  10.2 0.7 %collective-permute-start.3 = (f32[17,8,128]{2,1,0:T(8,128)S(1)}, f32[17,8,128]{2,1,0:T(8,128)S(1)}, u32[]{:S(2)}, u32[]{:S(2)}) collective-permute-start(f32[17,8,128]{2,1,0:T(8,128)S(1)} %get-tuple-element.15), channel_id=1, source_target_pairs={{4,10},{6,8},{8,6},{10,4},{5,11},{7,9},{9,7},{11,5},{20,26},{22,24... | collective-permute-start | bytes 208904 | tf_op jit(solution)/shard_map/ppermute | solution.py:571
  10.8 2.7 %collective-permute-start.4 = (f32[17,8,128]{2,1,0:T(8,128)S(1)}, f32[17,8,128]{2,1,0:T(8,128)S(1)}, u32[]{:S(2)}, u32[]{:S(2)}) collective-permute-start(f32[17,8,128]{2,1,0:T(8,128)S(1)} %get-tuple-element.16), channel_id=1, source_target_pairs={{0,6},{2,4},{4,2},{6,0},{8,14},{10,12},{12,10},{14,8},{1,7},{3,5},... | collective-permute-start | bytes 208904 | tf_op jit(solution)/shard_map/ppermute | solution.py:571
  13.6 0.1 begin_block.1.refs_0_.refs_1_
  13.7 1.3 %slot_tables.1 = (bf16[256,1024]{1,0:T(8,128)(2,1)S(1)}, s32[8,1024]{1,0:T(8,128)S(1)}, s32[16,128]{1,0:T(8,128)S(1)}) custom-call(s32[1,1024]{1,0:T(1,128)S(1)} %bitcast.3, s32[1,1024]{1,0:T(1,128)S(1)} %bitcast.4), custom_call_target="tpu_custom_call" | custom-call | tf_op jit(solution)/shard_map/slot_tables/pallas_call | solution.py:576
  14.9 0.3 pack_own_strips.1.refs_2_
  15.2 0.0 collective-permute-done.3.refs_4_.refs_6_
  15.2 6.6 %collective-permute-done.4.refs_5_.refs_7_ = f32[17,8,128]{2,1,0:T(8,128)S(1)} collective-permute-done((f32[17,8,128]{2,1,0:T(8,128)S(1)}, f32[17,8,128]{2,1,0:T(8,128)S(1)}, u32[]{:S(2)}, u32[]{:S(2)}) %collective-permute-start.4) | collective-permute-done | bytes 69664 | tf_op jit(solution)/shard_map/ppermute | solution.py:571
  21.9 0.0 collective-permute-done.refs_1_.refs_3_
  21.9 0.0 collective-permute-done.1.refs_2_.refs_4_
  21.9 0.0 collective-permute-done.2.refs_3_.refs_5_
  21.9 0.5 %pack_strips.1 = f32[38,8,128]{2,1,0:T(8,128)S(1)} custom-call(s32[8,1024]{1,0:T(8,128)S(1)} %get-tuple-element.17.after.refs_0_.refs_3_, f32[12,20,24,128]{3,2,1,0:T(8,128)S(1)} %begin_block.1.refs_0_.refs_1_, f32[12,8,128]{2,1,0:T(8,128)S(1)} %pack_own_strips.1.refs_2_, f32[12,8,8,128]{3,2,1,0:T(8,128)S(1)} %collective-permute-done.refs_1_.refs_3_, ...), custom_call_target="tpu_custom_call" | custom-call | tf_op jit(solution)/shard_map/pack_strips/pallas_call | solution.py:611
  22.3 0.1 collective-permute-start.5
  23.1 0.0 copy-start.2
  23.1 0.2 assemble.1.refs_0_
  23.2 0.6 %collective-permute-done.5.refs_1_ = f32[38,8,128]{2,1,0:T(8,128)S(1)} collective-permute-done((f32[38,8,128]{2,1,0:T(8,128)S(1)}, f32[38,8,128]{2,1,0:T(8,128)S(1)}, u32[]{:S(2)}, u32[]{:S(2)}) %collective-permute-start.5) | collective-permute-done | bytes 155680 | tf_op jit(solution)/shard_map/ppermute | solution.py:619
  23.8 5.0 %two_steps.1 = (f32[12,20,24,128]{3,2,1,0:T(8,128)S(1)}, f32[3,8,16,128]{3,2,1,0:T(8,128)}, f32[8,12,256]{2,1,0:T(8,128)S(1)}) custom-call(f32[12,20,24,128]{3,2,1,0:T(8,128)S(1)} %assemble.1.refs_0_, f32[38,8,128]{2,1,0:T(8,128)S(1)} %collective-permute-done.5.refs_1_, ...), custom_call_target="tpu_custom_call", output_to_operand_aliasing={{0}: (0, {})} | custom-call | tf_op jit(solution)/shard_map/two_steps/pallas_call | solution.py:631
  28.8 10.8 %all_to_all.5 = f32[8,12,256]{2,1,0:T(8,128)S(1)} all-to-all(f32[8,12,256]{2,1,0:T(8,128)S(1)} %get-tuple-element.21), channel_id=1, replica_groups=mesh['runs'=2,'gx'=4,'gy'=2,'gz'=2] {'gx','gy'}, dimensions={0} | all-to-all | bytes 196608 | tf_op jit(solution)/shard_map/all_to_all | solution.py:657
  39.6 0.1 copy.11
  39.7 0.7 %reshape.16 = f32[1,12,2048]{2,0,1:T(1,128)} reshape(f32[12,8,256]{2,1,0:T(8,128)S(1)} %copy.11) | data formatting | bytes 196608 | tf_op jit(solution)/shard_map/reshape | solution.py:658
  (5 shorter events, 0.0 us)
Async XLA Ops:
  0.6 13.0 %copy-start = (s32[1,1,1,1024]{3,2,1,0:T(1,128)S(1)}, s32[1,1,1,1024]{3,2,1,0:T(1,128)}, u32[]{:S(2)}) copy-start(s32[1,1,1,1024]{3,2,1,0:T(1,128)} %param.12) | copy-start | bytes 12292
  0.6 13.0 %copy-start.1 = (s32[1,1,1,1024,1]{3,4,2,1,0:T(1,128)S(1)}, s32[1,1,1,1024,1]{3,4,2,1,0:T(1,128)}, u32[]{:S(2)}) copy-start(s32[1,1,1,1024,1]{3,4,2,1,0:T(1,128)} %param.13) | copy-start | bytes 12292
  2.1 19.8 %collective-permute-start.1 = (f32[59,16,128]{2,1,0:T(8,128)S(1)}, f32[59,16,128]{2,1,0:T(8,128)S(1)}, u32[]{:S(2)}, u32[]{:S(2)}) collective-permute-start(f32[59,16,128]{2,1,0:T(8,128)S(1)} %get-tuple-element.13), channel_id=1, source_target_pairs={{4,8},{8,4},{5,9},{9,5},{6,10},{10,6},{7,11},{11,7},{20,24},{24,20... | collective-permute-start | bytes 1449992 | tf_op jit(solution)/shard_map/ppermute | solution.py:562
  2.8 19.1 %collective-permute-start.2 = (f32[59,16,128]{2,1,0:T(8,128)S(1)}, f32[59,16,128]{2,1,0:T(8,128)S(1)}, u32[]{:S(2)}, u32[]{:S(2)}) collective-permute-start(f32[59,16,128]{2,1,0:T(8,128)S(1)} %get-tuple-element.14), channel_id=1, source_target_pairs={{0,4},{4,0},{8,12},{12,8},{1,5},{5,1},{9,13},{13,9},{2,6},{6,2},{1... | collective-permute-start | bytes 1449992 | tf_op jit(solution)/shard_map/ppermute | solution.py:562
  8.7 13.2 %collective-permute-start = (f32[12,8,8,128]{3,2,1,0:T(8,128)S(1)}, f32[12,8,8,128]{3,2,1,0:T(8,128)S(1)}, u32[]{:S(2)}, u32[]{:S(2)}) collective-permute-start(f32[12,8,8,128]{3,2,1,0:T(8,128)S(1)} %get-tuple-element.12), channel_id=1, source_target_pairs={{0,2},{2,0},{1,3},{3,1},{4,6},{6,4},{5,7},{7,5},{8,10},{10,8},{9,1... | collective-permute-start | bytes 1179656 | tf_op jit(solution)/shard_map/ppermute | solution.py:564
  10.2 5.1 %collective-permute-start.3 = (f32[17,8,128]{2,1,0:T(8,128)S(1)}, f32[17,8,128]{2,1,0:T(8,128)S(1)}, u32[]{:S(2)}, u32[]{:S(2)}) collective-permute-start(f32[17,8,128]{2,1,0:T(8,128)S(1)} %get-tuple-element.15), channel_id=1, source_target_pairs={{4,10},{6,8},{8,6},{10,4},{5,11},{7,9},{9,7},{11,5},{20,26},{22,24... | collective-permute-start | bytes 208904 | tf_op jit(solution)/shard_map/ppermute | solution.py:571
  10.8 11.0 %collective-permute-start.4 = (f32[17,8,128]{2,1,0:T(8,128)S(1)}, f32[17,8,128]{2,1,0:T(8,128)S(1)}, u32[]{:S(2)}, u32[]{:S(2)}) collective-permute-start(f32[17,8,128]{2,1,0:T(8,128)S(1)} %get-tuple-element.16), channel_id=1, source_target_pairs={{0,6},{2,4},{4,2},{6,0},{8,14},{10,12},{12,10},{14,8},{1,7},{3,5},... | collective-permute-start | bytes 208904 | tf_op jit(solution)/shard_map/ppermute | solution.py:571
  22.3 1.4 %collective-permute-start.5 = (f32[38,8,128]{2,1,0:T(8,128)S(1)}, f32[38,8,128]{2,1,0:T(8,128)S(1)}, u32[]{:S(2)}, u32[]{:S(2)}) collective-permute-start(f32[38,8,128]{2,1,0:T(8,128)S(1)} %pack_strips.1), channel_id=1, source_target_pairs={{0,1},{1,0},{2,3},{3,2},{4,5},{5,4},{6,7},{7,6},{8,9},{9,8},{10,11... | collective-permute-start | bytes 466952 | tf_op jit(solution)/shard_map/ppermute | solution.py:619
  23.1 0.7 %copy-start.2 = (f32[2,3]{1,0:T(2,128)S(1)}, f32[2,3]{1,0:T(2,128)}, u32[]{:S(2)}) copy-start(f32[2,3]{1,0:T(2,128)} %refs_6_.1) | copy-start | bytes 76

commit v5 on v4

--- a/solution.py
+++ b/solution.py
@@ -45,6 +45,7 @@
 PART = 6
 VMEM = pl.BlockSpec(memory_space=pltpu.VMEM)
 HBM = pl.BlockSpec(memory_space=pltpu.HBM)
+SMEM = pl.BlockSpec(memory_space=pltpu.SMEM)
 IDLE = pl.CostEstimate(flops=0, bytes_accessed=0, transcendentals=0)
 
 
@@ -161,12 +162,9 @@
     return ref[at]
 
 
-def strip_kernel(grid, own, *refs):
-    out = refs[-1]
+def strip_kernel(grid, pieces, base, refs, out):
     head = jnp.where(lax.axis_index("gz") == 0, STRIP, 0)
-    base = own.shape[0]
-    out[0:base] = own[...]
-    for (name, count), ref in zip(grid.pieces(), refs[:-1]):
+    for (name, count), ref in zip(pieces, refs):
         for g in range(groups(count)):
             tiles = [
                 piece_tile(name, ref, at, grid) for at in range(16 * g, min(16 * g + 16, count))
@@ -175,7 +173,25 @@
         base += groups(count)
 
 
-def slot_kernel(width, cz, cells_ref, writers_ref, lanes_ref, rows_ref, spans_ref):
+def face_strip_kernel(grid, pieces, *refs):
+    own, out = refs[2], refs[-1]
+    out[0 : own.shape[0]] = own[...]
+    strip_kernel(grid, pieces, own.shape[0], refs[3:-1], out)
+
+
+def slot_kernel(
+    width,
+    cz,
+    cells_ref,
+    writers_ref,
+    site_ref,
+    wavelet_ref,
+    lanes_ref,
+    rows_ref,
+    spans_ref,
+    force_ref,
+):
+    force_ref[0 : wavelet_ref.shape[0], 0 : wavelet_ref.shape[1]] = wavelet_ref[...]
     count = cells_ref.shape[1]
     cells = cells_ref[...]
     writers = writers_ref[...]
@@ -199,7 +215,8 @@
             preferred_element_type=jnp.float32,
         ).astype(jnp.int32)
 
-    spans_ref[0:ROWS, :] = across(fewer)[0:ROWS]
+    first = across(fewer)[0:ROWS]
+    spans_ref[0:ROWS, :] = jnp.where(iota(0, first.shape) == 1, site_ref[0], first)
     spans_ref[ROWS : 2 * ROWS, :] = across(named)[0:ROWS]
     which = iota(0, (16, count))
     values = jnp.where(which == 0, lax.rem(cells, cz), jnp.where(which == 1, lax.div(cells, cz), 0))
@@ -316,13 +333,12 @@
 
 
 def main_kernel(grid, width, capacity, *refs):
-    strips, lanes_ref, rows_ref, spans_vmem, site_hbm, wavelet_hbm = refs[1:7]
-    ext, velocity_out, table_out = refs[7:10]
-    beside, sampled, compact, site_ref, wavelet_ref, spans_ref, sems = refs[10:]
+    strips, lanes_ref, rows_ref, spans_vmem, force_vmem = refs[1:6]
+    ext, velocity_out, table_out = refs[6:9]
+    beside, sampled, compact, wavelet_ref, spans_ref, sems = refs[9:]
     copies = (
-        pltpu.make_async_copy(site_hbm, site_ref, sems.at[0]),
-        pltpu.make_async_copy(wavelet_hbm, wavelet_ref, sems.at[1]),
-        pltpu.make_async_copy(spans_vmem, spans_ref, sems.at[2]),
+        pltpu.make_async_copy(force_vmem, wavelet_ref, sems.at[0]),
+        pltpu.make_async_copy(spans_vmem, spans_ref, sems.at[1]),
     )
     for copy in copies:
         copy.start()
@@ -441,7 +457,7 @@
     loop(-5, cx + 3, velocity_layer)
     for copy in copies:
         copy.wait()
-    site = site_ref[0]
+    site = spans_ref[1, 0]
     total_y, total_z = cy * grid.gy, cz * grid.gz
     site_x = lax.div(site, total_y * total_z) - lax.axis_index("gx") * cx
     site_y = lax.rem(lax.div(site, total_z), total_y) - lax.axis_index("gy") * cy
@@ -525,7 +541,7 @@
     loop(-2, cx, velocity_layer)
     inject(1)
     leaving = pltpu.make_async_copy(
-        ext.at[VX : VX + 3, HALO : HALO + cx, 0:cy, :], velocity_out, sems.at[3]
+        ext.at[VX : VX + 3, HALO : HALO + cx, 0:cy, :], velocity_out, sems.at[2]
     )
     leaving.start()
     loop(0, cx - 1, functools.partial(stress_layer, last=True))
@@ -573,19 +589,20 @@
     width = grid.gx * grid.gy
     capacity = max(2, 2 * count // width)
     slots = width * capacity
-    lanes, rows, spans = pl.pallas_call(
+    lanes, rows, spans, force = pl.pallas_call(
         functools.partial(slot_kernel, width, grid.cz),
         out_shape=[
             jax.ShapeDtypeStruct((2 * grid.cz, count), jnp.bfloat16),
             jax.ShapeDtypeStruct((ROWS, count), jnp.int32),
             jax.ShapeDtypeStruct((2 * ROWS, max(LANES, width)), jnp.int32),
+            f32(ROWS, LANES),
         ],
-        in_specs=[VMEM] * 2,
-        out_specs=[VMEM] * 3,
+        in_specs=[VMEM] * 2 + [SMEM, VMEM],
+        out_specs=[VMEM] * 4,
         compiler_params=params,
         cost_estimate=IDLE,
         name="slot_tables",
-    )(save_cells.reshape(1, count), save_writer.reshape(1, count))
+    )(save_cells.reshape(1, count), save_writer.reshape(1, count), force_site, force_wavelet)
 
     own_strips = pl.pallas_call(
         functools.partial(own_strip_kernel, grid),
@@ -608,14 +625,26 @@
         name="begin_block",
     )(fields)
 
+    faces = len(grid.y_pairs) + len(grid.x_pairs)
+    first_corner = groups(own_tiles) + sum(groups(c) for _, c in pieces[:faces])
+    all_strips = f32(first_corner + sum(groups(c) for _, c in pieces[faces:]), ROWS, LANES)
     strips = pl.pallas_call(
-        lambda *refs: strip_kernel(grid, *refs[2:]),
-        out_shape=f32(groups(own_tiles) + sum(groups(c) for _, c in pieces), ROWS, LANES),
-        in_specs=[VMEM] * (len(pieces) + 3),
+        functools.partial(face_strip_kernel, grid, pieces[:faces]),
+        out_shape=all_strips,
+        in_specs=[VMEM] * (faces + 3),
         out_specs=VMEM,
         compiler_params=params,
-        name="pack_strips",
-    )(rows, block, own_strips, *arrived)
+        name="pack_face_strips",
+    )(rows, block, own_strips, *arrived[:faces])
+    strips = pl.pallas_call(
+        lambda *refs: strip_kernel(grid, pieces[faces:], first_corner, refs[1:-1], refs[-1]),
+        out_shape=all_strips,
+        in_specs=[VMEM] * (1 + len(pieces) - faces),
+        out_specs=VMEM,
+        input_output_aliases={0: 0},
+        compiler_params=params,
+        name="pack_corner_strips",
+    )(strips, *arrived[faces:])
     strips = lax.ppermute(strips, "gz", swap)
 
     block = pl.pallas_call(
@@ -635,21 +664,20 @@
             f32(*velocity_start.shape),
             f32(slots // 256, 6 * STEPS, 256),
         ],
-        in_specs=[VMEM] * 5 + [HBM] * 2,
+        in_specs=[VMEM] * 6,
         out_specs=[VMEM, HBM, VMEM],
         scratch_shapes=[
             pltpu.VMEM(extended.shape, jnp.float32),
             pltpu.VMEM((STEPS * 6 * grid.cx * grid.cy, 2 * grid.cz), jnp.bfloat16),
             pltpu.VMEM((16, count + 4 * LANES), jnp.float32),
-            pltpu.SMEM(force_site.shape, jnp.int32),
-            pltpu.SMEM(force_wavelet.shape, jnp.float32),
+            pltpu.SMEM(force.shape, jnp.float32),
             pltpu.SMEM(spans.shape, jnp.int32),
-            pltpu.SemaphoreType.DMA((4,)),
+            pltpu.SemaphoreType.DMA((3,)),
         ],
         input_output_aliases={0: 0},
         compiler_params=params,
         name="two_steps",
-    )(block, strips, lanes, rows, spans, force_site, force_wavelet)
+    )(block, strips, lanes, rows, spans, force)
 
     values = 6 * STEPS
     if capacity != 256:

time: 40.7 us -> 40.3 us (level)
  waiting for transfers between devices: 7.18 us -> 6.75 us
    ppermute x2, waiting for transfers between devices: 6.62 us -> 1.24 us  [per_device(): arrived.append(lax.ppermute(piece, ('gx', 'gy'), pairs))]
    ppermute x1, waiting for transfers between devices: 0.01 us -> 3.08 us  [per_device(): arrived.append(lax.ppermute(piece, 'gy', grid.pairs(grid.gy, name[1])))]
    ppermute x2, waiting for transfers between devices: 0.01 us -> 1.22 us  [per_device(): arrived.append(lax.ppermute(piece, 'gx', grid.pairs(grid.gx, name[1])))]
    ppermute x1, waiting for transfers between devices: 0.55 us -> 1.21 us  [per_device(): strips = lax.ppermute(strips, 'gz', swap)]
  transfers between devices with their start and end apart: 6 -> 6, of which waited for: 2 -> 4; matrix products, arithmetic and copies ran while one was open for 0% -> 0% of each run, Pallas kernels for 4% -> 5%
where the time goes in v5:
time: 40.3 us; the launch traced here: 40.1 us
  starting transfers between devices  11.5 us (29%)
  blocking collectives  10.5 us (26%)
  Pallas kernels  7.79 us (19%)
  waiting for transfers between devices  6.75 us (17%)
  between operations  1.43 us (4%)
  other arithmetic  1.28 us (3%)
  local copies, waits for them, and re-layouts  0.82 us (2%)
    all_to_all x1, blocking collectives, per_device(): lax.all_to_all(table, ('gx', 'gy'), split_axis=0, concat_axis=0, tiled=True)  10.5 us
    ppermute x2, starting transfers between devices, per_device(): arrived.append(lax.ppermute(piece, 'gx', grid.pairs(grid.gx, name[1])))  6.57 us
    pallas_call x1, Pallas kernels, per_device(): pl.pallas_call(functools.partial(main_kernel, grid, width, capacity), out...  5.34 us
    ppermute x2, starting transfers between devices, per_device(): arrived.append(lax.ppermute(piece, ('gx', 'gy'), pairs))  3.39 us
    ppermute x1, waiting for transfers between devices, per_device(): arrived.append(lax.ppermute(piece, 'gy', grid.pairs(grid.gy, name[1])))  3.08 us
    ppermute x1, starting transfers between devices, per_device(): arrived.append(lax.ppermute(piece, 'gy', grid.pairs(grid.gy, name[1])))  1.49 us
    add x1, other arithmetic, per_device(): sum((lax.pad(part, jnp.float32(0.0), [(first, FIELDS - first - part.shape...  1.28 us
    pallas_call x1, Pallas kernels, per_device(): pl.pallas_call(functools.partial(slot_kernel, width, grid.cz), out_shape=...  1.26 us
  transfers between devices with their start and end apart: 6, of which 4 were waited for; matrix products, arithmetic and copies ran while one was open for 0% of the time, Pallas kernels for 5%

profile of v5, /device:TPU:0, one launch (start us, length us, event | category | flops | bytes accessed | tf_op | source)
XLA Modules:
  0.0 40.1 jit_solution(5255485487728514393)
XLA Ops:
  0.7 1.3 %pad_add_fusion.refs_0_.fields = f32[12,8,16,128]{3,2,1,0:T(8,128)S(1)} fusion(f32[3,8,16,128]{3,2,1,0:T(8,128)} %param.9, f32[3,8,16,128]{3,2,1,0:T(8,128)} %param.7, f32[6,8,16,128]{3,2,1,0:T(8,128)} %param.8), kind=kLoop, calls=%fused_computation | loop fusion | flops 393216 | bytes 1572864 | tf_op jit(solution)/shard_map/add | solution.py:562
  2.0 0.2 pack_halos.1
  2.1 0.7 %collective-permute-start.1 = (f32[59,16,128]{2,1,0:T(8,128)S(1)}, f32[59,16,128]{2,1,0:T(8,128)S(1)}, u32[]{:S(2)}, u32[]{:S(2)}) collective-permute-start(f32[59,16,128]{2,1,0:T(8,128)S(1)} %get-tuple-element.14), channel_id=1, source_target_pairs={{4,8},{8,4},{5,9},{9,5},{6,10},{10,6},{7,11},{11,7},{20,24},{24,20... | collective-permute-start | bytes 1449992 | tf_op jit(solution)/shard_map/ppermute | solution.py:578
  2.8 5.9 %collective-permute-start.2 = (f32[59,16,128]{2,1,0:T(8,128)S(1)}, f32[59,16,128]{2,1,0:T(8,128)S(1)}, u32[]{:S(2)}, u32[]{:S(2)}) collective-permute-start(f32[59,16,128]{2,1,0:T(8,128)S(1)} %get-tuple-element.15), channel_id=1, source_target_pairs={{0,4},{4,0},{8,12},{12,8},{1,5},{5,1},{9,13},{13,9},{2,6},{6,2},{1... | collective-permute-start | bytes 1449992 | tf_op jit(solution)/shard_map/ppermute | solution.py:578
  8.7 1.5 %collective-permute-start = (f32[12,8,8,128]{3,2,1,0:T(8,128)S(1)}, f32[12,8,8,128]{3,2,1,0:T(8,128)S(1)}, u32[]{:S(2)}, u32[]{:S(2)}) collective-permute-start(f32[12,8,8,128]{3,2,1,0:T(8,128)S(1)} %get-tuple-element.13), channel_id=1, source_target_pairs={{0,2},{2,0},{1,3},{3,1},{4,6},{6,4},{5,7},{7,5},{8,10},{10,8},{9,1... | collective-permute-start | bytes 1179656 | tf_op jit(solution)/shard_map/ppermute | solution.py:580
  10.2 0.7 %collective-permute-start.3 = (f32[17,8,128]{2,1,0:T(8,128)S(1)}, f32[17,8,128]{2,1,0:T(8,128)S(1)}, u32[]{:S(2)}, u32[]{:S(2)}) collective-permute-start(f32[17,8,128]{2,1,0:T(8,128)S(1)} %get-tuple-element.16), channel_id=1, source_target_pairs={{4,10},{6,8},{8,6},{10,4},{5,11},{7,9},{9,7},{11,5},{20,26},{22,24... | collective-permute-start | bytes 208904 | tf_op jit(solution)/shard_map/ppermute | solution.py:587
  10.8 2.7 %collective-permute-start.4 = (f32[17,8,128]{2,1,0:T(8,128)S(1)}, f32[17,8,128]{2,1,0:T(8,128)S(1)}, u32[]{:S(2)}, u32[]{:S(2)}) collective-permute-start(f32[17,8,128]{2,1,0:T(8,128)S(1)} %get-tuple-element.17), channel_id=1, source_target_pairs={{0,6},{2,4},{4,2},{6,0},{8,14},{10,12},{12,10},{14,8},{1,7},{3,5},... | collective-permute-start | bytes 208904 | tf_op jit(solution)/shard_map/ppermute | solution.py:587
  13.6 0.1 begin_block.1.refs_0_.refs_1_
  14.4 1.3 %slot_tables.1 = (bf16[256,1024]{1,0:T(8,128)(2,1)S(1)}, s32[8,1024]{1,0:T(8,128)S(1)}, s32[16,128]{1,0:T(8,128)S(1)}, f32[8,128]{1,0:T(8,128)S(1)}) custom-call(s32[1,1024]{1,0:T(1,128)S(1)} %bitcast.3, s32[1,1024]{1,0:T(1,128)S(1)} %bitcast.4, s32[1]{0:T(128)S(6)} %copy.17.site_ref, f32[2,3]{1,0:T(2,128)S(1)} %copy-done.2), custom_call_target="tpu_custom_call" | custom-call | tf_op jit(solution)/shard_map/slot_tables/pallas_call | solution.py:592
  15.6 0.3 pack_own_strips.1.refs_2_
  15.9 3.1 %collective-permute-done.refs_1_.refs_3_ = f32[12,8,8,128]{3,2,1,0:T(8,128)S(1)} collective-permute-done((f32[12,8,8,128]{3,2,1,0:T(8,128)S(1)}, f32[12,8,8,128]{3,2,1,0:T(8,128)S(1)}, u32[]{:S(2)}, u32[]{:S(2)}) %collective-permute-start) | collective-permute-done | bytes 393248 | tf_op jit(solution)/shard_map/ppermute | solution.py:580
  19.0 0.0 collective-permute-done.1.refs_2_.refs_4_
  19.0 1.2 %collective-permute-done.2.refs_3_.refs_5_ = f32[59,16,128]{2,1,0:T(8,128)S(1)} collective-permute-done((f32[59,16,128]{2,1,0:T(8,128)S(1)}, f32[59,16,128]{2,1,0:T(8,128)S(1)}, u32[]{:S(2)}, u32[]{:S(2)}) %collective-permute-start.2) | collective-permute-done | bytes 483360 | tf_op jit(solution)/shard_map/ppermute | solution.py:578
  20.2 0.4 %pack_face_strips.1.refs_0_ = f32[38,8,128]{2,1,0:T(8,128)S(1)} custom-call(s32[8,1024]{1,0:T(8,128)S(1)} %get-tuple-element.18.after.refs_0_.refs_3_, f32[12,20,24,128]{3,2,1,0:T(8,128)S(1)} %begin_block.1.refs_0_.refs_1_, f32[12,8,128]{2,1,0:T(8,128)S(1)} %pack_own_strips.1.refs_2_, f32[12,8,8,128]{3,2,1,0:T(8,128)S(1)} %collective-permute-done.refs_1_.refs_3_, ...), custom_call_target="tpu_custom_call" | custom-call | tf_op jit(solution)/shard_map/pack_face_strips/pallas_call | solution.py:631
  20.6 0.0 collective-permute-done.3.refs_4_.refs_1_
  20.6 1.2 %collective-permute-done.4.refs_5_.refs_2_ = f32[17,8,128]{2,1,0:T(8,128)S(1)} collective-permute-done((f32[17,8,128]{2,1,0:T(8,128)S(1)}, f32[17,8,128]{2,1,0:T(8,128)S(1)}, u32[]{:S(2)}, u32[]{:S(2)}) %collective-permute-start.4) | collective-permute-done | bytes 69664 | tf_op jit(solution)/shard_map/ppermute | solution.py:587
  21.9 0.1 pack_corner_strips.1
  22.0 0.1 collective-permute-start.5
  22.1 0.2 assemble.1.refs_0_
  22.2 1.2 %collective-permute-done.5.refs_1_ = f32[38,8,128]{2,1,0:T(8,128)S(1)} collective-permute-done((f32[38,8,128]{2,1,0:T(8,128)S(1)}, f32[38,8,128]{2,1,0:T(8,128)S(1)}, u32[]{:S(2)}, u32[]{:S(2)}) %collective-permute-start.5) | collective-permute-done | bytes 155680 | tf_op jit(solution)/shard_map/ppermute | solution.py:648
  23.4 5.3 %two_steps.1 = (f32[12,20,24,128]{3,2,1,0:T(8,128)S(1)}, f32[3,8,16,128]{3,2,1,0:T(8,128)}, f32[8,12,256]{2,1,0:T(8,128)S(1)}) custom-call(f32[12,20,24,128]{3,2,1,0:T(8,128)S(1)} %assemble.1.refs_0_, f32[38,8,128]{2,1,0:T(8,128)S(1)} %collective-permute-done.5.refs_1_, ...), custom_call_target="tpu_custom_call", output_to_operand_aliasing={{0}: (0, {})} | custom-call | tf_op jit(solution)/shard_map/two_steps/pallas_call | solution.py:660
  28.8 10.5 %all_to_all.5 = f32[8,12,256]{2,1,0:T(8,128)S(1)} all-to-all(f32[8,12,256]{2,1,0:T(8,128)S(1)} %get-tuple-element.23), channel_id=1, replica_groups=mesh['runs'=2,'gx'=4,'gy'=2,'gz'=2] {'gx','gy'}, dimensions={0} | all-to-all | bytes 196608 | tf_op jit(solution)/shard_map/all_to_all | solution.py:685
  39.3 0.1 copy.12
  39.4 0.7 %reshape.16 = f32[1,12,2048]{2,0,1:T(1,128)} reshape(f32[12,8,256]{2,1,0:T(8,128)S(1)} %copy.12) | data formatting | bytes 196608 | tf_op jit(solution)/shard_map/reshape | solution.py:686
  (6 shorter events, 0.0 us)
Async XLA Ops:
  0.6 13.7 %copy-start.1 = (s32[1,1,1,1024,1]{3,4,2,1,0:T(1,128)S(1)}, s32[1,1,1,1024,1]{3,4,2,1,0:T(1,128)}, u32[]{:S(2)}) copy-start(s32[1,1,1,1024,1]{3,4,2,1,0:T(1,128)} %param.13) | copy-start | bytes 12292
  0.6 13.7 %copy-start = (s32[1,1,1,1024]{3,2,1,0:T(1,128)S(1)}, s32[1,1,1,1024]{3,2,1,0:T(1,128)}, u32[]{:S(2)}) copy-start(s32[1,1,1,1024]{3,2,1,0:T(1,128)} %param.12) | copy-start | bytes 12292
  0.7 13.7 %copy-start.2 = (f32[2,3]{1,0:T(2,128)S(1)}, f32[2,3]{1,0:T(2,128)}, u32[]{:S(2)}) copy-start(f32[2,3]{1,0:T(2,128)} %wavelet_ref.1) | copy-start | bytes 76
  2.1 16.9 %collective-permute-start.1 = (f32[59,16,128]{2,1,0:T(8,128)S(1)}, f32[59,16,128]{2,1,0:T(8,128)S(1)}, u32[]{:S(2)}, u32[]{:S(2)}) collective-permute-start(f32[59,16,128]{2,1,0:T(8,128)S(1)} %get-tuple-element.14), channel_id=1, source_target_pairs={{4,8},{8,4},{5,9},{9,5},{6,10},{10,6},{7,11},{11,7},{20,24},{24,20... | collective-permute-start | bytes 1449992 | tf_op jit(solution)/shard_map/ppermute | solution.py:578
  2.8 17.4 %collective-permute-start.2 = (f32[59,16,128]{2,1,0:T(8,128)S(1)}, f32[59,16,128]{2,1,0:T(8,128)S(1)}, u32[]{:S(2)}, u32[]{:S(2)}) collective-permute-start(f32[59,16,128]{2,1,0:T(8,128)S(1)} %get-tuple-element.15), channel_id=1, source_target_pairs={{0,4},{4,0},{8,12},{12,8},{1,5},{5,1},{9,13},{13,9},{2,6},{6,2},{1... | collective-permute-start | bytes 1449992 | tf_op jit(solution)/shard_map/ppermute | solution.py:578
  8.7 10.3 %collective-permute-start = (f32[12,8,8,128]{3,2,1,0:T(8,128)S(1)}, f32[12,8,8,128]{3,2,1,0:T(8,128)S(1)}, u32[]{:S(2)}, u32[]{:S(2)}) collective-permute-start(f32[12,8,8,128]{3,2,1,0:T(8,128)S(1)} %get-tuple-element.13), channel_id=1, source_target_pairs={{0,2},{2,0},{1,3},{3,1},{4,6},{6,4},{5,7},{7,5},{8,10},{10,8},{9,1... | collective-permute-start | bytes 1179656 | tf_op jit(solution)/shard_map/ppermute | solution.py:580
  10.2 10.5 %collective-permute-start.3 = (f32[17,8,128]{2,1,0:T(8,128)S(1)}, f32[17,8,128]{2,1,0:T(8,128)S(1)}, u32[]{:S(2)}, u32[]{:S(2)}) collective-permute-start(f32[17,8,128]{2,1,0:T(8,128)S(1)} %get-tuple-element.16), channel_id=1, source_target_pairs={{4,10},{6,8},{8,6},{10,4},{5,11},{7,9},{9,7},{11,5},{20,26},{22,24... | collective-permute-start | bytes 208904 | tf_op jit(solution)/shard_map/ppermute | solution.py:587
  10.8 11.0 %collective-permute-start.4 = (f32[17,8,128]{2,1,0:T(8,128)S(1)}, f32[17,8,128]{2,1,0:T(8,128)S(1)}, u32[]{:S(2)}, u32[]{:S(2)}) collective-permute-start(f32[17,8,128]{2,1,0:T(8,128)S(1)} %get-tuple-element.17), channel_id=1, source_target_pairs={{0,6},{2,4},{4,2},{6,0},{8,14},{10,12},{12,10},{14,8},{1,7},{3,5},... | collective-permute-start | bytes 208904 | tf_op jit(solution)/shard_map/ppermute | solution.py:587
  22.0 1.4 %collective-permute-start.5 = (f32[38,8,128]{2,1,0:T(8,128)S(1)}, f32[38,8,128]{2,1,0:T(8,128)S(1)}, u32[]{:S(2)}, u32[]{:S(2)}) collective-permute-start(f32[38,8,128]{2,1,0:T(8,128)S(1)} %pack_corner_strips.1), channel_id=1, source_target_pairs={{0,1},{1,0},{2,3},{3,2},{4,5},{5,4},{6,7},{7,6},{8,9},{9,8},{10,11... | collective-permute-start | bytes 466952 | tf_op jit(solution)/shard_map/ppermute | solution.py:648

commit v6 on v5

--- a/solution.py
+++ b/solution.py
@@ -67,7 +67,20 @@
     for at, tile in enumerate(tiles):
         turned = pltpu.roll(tile, (STRIP * at + head) & (LANES - 1), 1)
         packed = turned if packed is None else jnp.where(slot == at, turned, packed)
-    return packed
+    within = iota(1) % STRIP
+    first = jnp.where(head == 0, 0, STRIP - HALO)
+    sent = jnp.logical_and(within >= first, within < first + HALO)
+    return jnp.where(sent, packed, 0.0)
+
+
+class Fields:
+    def __init__(self, moving, material):
+        self.parts = moving, material
+
+    def __getitem__(self, key):
+        if key[0] < LAM:
+            return self.parts[0][key]
+        return self.parts[1][(key[0] - LAM, *key[1:])]
 
 
 class Grid:
@@ -107,8 +120,8 @@
 
 
 def pack_kernel(grid, *refs):
-    fields = refs[0]
-    outs = refs[1:]
+    fields = Fields(*refs[:2])
+    outs = refs[2:]
     sub = iota(0)
     for (name, _), out in zip(grid.pieces(), outs):
         if name[0] == "x":
@@ -143,7 +156,8 @@
                 out[i] = packed
 
 
-def own_strip_kernel(grid, after, fields, own):
+def own_strip_kernel(grid, after, moving, material, own):
+    fields = Fields(moving, material)
     head = jnp.where(lax.axis_index("gz") == 0, STRIP, 0)
     tiles = [(f, x, r) for f in range(FIELDS) for x in range(grid.cx) for r in range(grid.tiles_y)]
     for g in range(groups(len(tiles))):
@@ -301,20 +315,13 @@
                 put(f, d, turned)
 
 
-def known_lanes():
+def unpack(ref, base, at):
     lead = jnp.where(lax.axis_index("gz") == 0, 0, LANES - STRIP)
-    lane = iota(1)
-    return lead, jnp.logical_and(lane >= lead, lane < lead + STRIP)
-
-
-def unpack(ref, base, at):
-    lead, known = known_lanes()
-    turned = pltpu.roll(ref[base + at // 16], (lead - STRIP * (at % 16)) & (LANES - 1), 1)
-    return jnp.where(known, turned, 0.0)
+    return pltpu.roll(ref[base + at // 16], (lead - STRIP * (at % 16)) & (LANES - 1), 1)
 
 
 def begin_kernel(grid, *refs):
-    fields, ext = refs
+    fields, ext = Fields(*refs[:2]), refs[2]
 
     def own(at):
         x, r = at // grid.tiles_y % grid.cx, at % grid.tiles_y
@@ -560,17 +567,17 @@
     params = pltpu.CompilerParams(vmem_limit_bytes=VMEM_LIMIT)
     own_tiles = FIELDS * grid.cx * grid.tiles_y
     fields = sum(
-        lax.pad(part, jnp.float32(0.0), [(first, FIELDS - first - part.shape[0], 0)] + [(0, 0, 0)] * 3)
-        for first, part in ((SXX, stress_start), (VX, velocity_start), (LAM, material))
+        lax.pad(part, jnp.float32(0.0), [(first, LAM - first - part.shape[0], 0)] + [(0, 0, 0)] * 3)
+        for first, part in ((SXX, stress_start), (VX, velocity_start))
     )
     packed = pl.pallas_call(
         lambda *refs: pack_kernel(grid, *refs),
         out_shape=[f32(*grid.shape(name)) for name, _ in pieces],
-        in_specs=[VMEM],
+        in_specs=[VMEM] * 2,
         out_specs=[VMEM] * len(pieces),
         compiler_params=params,
         name="pack_halos",
-    )(fields)
+    )(fields, material)
     swap = [(0, 1), (1, 0)]
     arrived = []
     for (name, _), piece in zip(pieces, packed):
@@ -607,23 +614,23 @@
     own_strips = pl.pallas_call(
         functools.partial(own_strip_kernel, grid),
         out_shape=f32(groups(own_tiles), ROWS, LANES),
+        in_specs=[VMEM] * 3,
+        out_specs=VMEM,
+        compiler_params=params,
+        cost_estimate=IDLE,
+        name="pack_own_strips",
+    )(rows, fields, material)
+
+    extended = f32(FIELDS, grid.layers, grid.rows, grid.cz)
+    block = pl.pallas_call(
+        lambda *refs: begin_kernel(grid, *refs),
+        out_shape=extended,
         in_specs=[VMEM] * 2,
         out_specs=VMEM,
         compiler_params=params,
         cost_estimate=IDLE,
-        name="pack_own_strips",
-    )(rows, fields)
-
-    extended = f32(FIELDS, grid.layers, grid.rows, grid.cz)
-    block = pl.pallas_call(
-        lambda *refs: begin_kernel(grid, *refs),
-        out_shape=extended,
-        in_specs=[VMEM],
-        out_specs=VMEM,
-        compiler_params=params,
-        cost_estimate=IDLE,
         name="begin_block",
-    )(fields)
+    )(fields, material)
 
     faces = len(grid.y_pairs) + len(grid.x_pairs)
     first_corner = groups(own_tiles) + sum(groups(c) for _, c in pieces[:faces])

time: 40.3 us -> 41.2 us (1.022)
  local copies, waits for them, and re-layouts: 0.82 us -> 1.74 us
    unnamed x6 -> x10, local copies, waits for them, and re-layouts: 0.01 us -> 0.94 us
where the time goes in v6:
time: 41.2 us; the launch traced here: 40.9 us
  starting transfers between devices  11.5 us (28%)
  blocking collectives  10.5 us (25%)
  Pallas kernels  7.77 us (19%)
  waiting for transfers between devices  6.73 us (16%)
  local copies, waits for them, and re-layouts  1.74 us (4%)
  between operations  1.45 us (4%)
  other arithmetic  1.18 us (3%)
    all_to_all x1, blocking collectives, per_device(): lax.all_to_all(table, ('gx', 'gy'), split_axis=0, concat_axis=0, tiled=True)  10.5 us
    ppermute x2, starting transfers between devices, per_device(): arrived.append(lax.ppermute(piece, 'gx', grid.pairs(grid.gx, name[1])))  6.57 us
    pallas_call x1, Pallas kernels, per_device(): pl.pallas_call(functools.partial(main_kernel, grid, width, capacity), out...  5.33 us
    ppermute x2, starting transfers between devices, per_device(): arrived.append(lax.ppermute(piece, ('gx', 'gy'), pairs))  3.39 us
    ppermute x1, waiting for transfers between devices, per_device(): arrived.append(lax.ppermute(piece, 'gy', grid.pairs(grid.gy, name[1])))  3.07 us
    ppermute x1, starting transfers between devices, per_device(): arrived.append(lax.ppermute(piece, 'gy', grid.pairs(grid.gy, name[1])))  1.49 us
    pallas_call x1, Pallas kernels, per_device(): pl.pallas_call(functools.partial(slot_kernel, width, grid.cz), out_shape=...  1.26 us
    ppermute x2, waiting for transfers between devices, per_device(): arrived.append(lax.ppermute(piece, ('gx', 'gy'), pairs))  1.23 us
  transfers between devices with their start and end apart: 6, of which 4 were waited for; matrix products, arithmetic and copies ran while one was open for 0% of the time, Pallas kernels for 5%

profile of v6, /device:TPU:0, one launch (start us, length us, event | category | flops | bytes accessed | tf_op | source)
XLA Modules:
  0.0 40.9 jit_solution(7482580644007941466)
XLA Ops:
  0.6 0.0 copy-start.1
  0.7 1.2 %pad_add_fusion.refs_0_.moving = f32[9,8,16,128]{3,2,1,0:T(8,128)S(1)} fusion(f32[3,8,16,128]{3,2,1,0:T(8,128)} %param.7, f32[6,8,16,128]{3,2,1,0:T(8,128)} %param.8), kind=kLoop, calls=%fused_computation | loop fusion | flops 147456 | bytes 1179648 | tf_op jit(solution)/shard_map/add | solution.py:569
  1.9 0.9 %copy-done = f32[3,8,16,128]{3,2,1,0:T(8,128)S(1)} copy-done((f32[3,8,16,128]{3,2,1,0:T(8,128)S(1)}, f32[3,8,16,128]{3,2,1,0:T(8,128)}, u32[]{:S(2)}) %copy-start) | copy-done | bytes 196632
  2.8 0.1 pack_halos.1
  2.9 0.7 %collective-permute-start.1 = (f32[59,16,128]{2,1,0:T(8,128)S(1)}, f32[59,16,128]{2,1,0:T(8,128)S(1)}, u32[]{:S(2)}, u32[]{:S(2)}) collective-permute-start(f32[59,16,128]{2,1,0:T(8,128)S(1)} %get-tuple-element.14), channel_id=1, source_target_pairs={{4,8},{8,4},{5,9},{9,5},{6,10},{10,6},{7,11},{11,7},{20,24},{24,20... | collective-permute-start | bytes 1449992 | tf_op jit(solution)/shard_map/ppermute | solution.py:585
  3.6 5.9 %collective-permute-start.2 = (f32[59,16,128]{2,1,0:T(8,128)S(1)}, f32[59,16,128]{2,1,0:T(8,128)S(1)}, u32[]{:S(2)}, u32[]{:S(2)}) collective-permute-start(f32[59,16,128]{2,1,0:T(8,128)S(1)} %get-tuple-element.15), channel_id=1, source_target_pairs={{0,4},{4,0},{8,12},{12,8},{1,5},{5,1},{9,13},{13,9},{2,6},{6,2},{1... | collective-permute-start | bytes 1449992 | tf_op jit(solution)/shard_map/ppermute | solution.py:585
  9.5 1.5 %collective-permute-start = (f32[12,8,8,128]{3,2,1,0:T(8,128)S(1)}, f32[12,8,8,128]{3,2,1,0:T(8,128)S(1)}, u32[]{:S(2)}, u32[]{:S(2)}) collective-permute-start(f32[12,8,8,128]{3,2,1,0:T(8,128)S(1)} %get-tuple-element.13), channel_id=1, source_target_pairs={{0,2},{2,0},{1,3},{3,1},{4,6},{6,4},{5,7},{7,5},{8,10},{10,8},{9,1... | collective-permute-start | bytes 1179656 | tf_op jit(solution)/shard_map/ppermute | solution.py:587
  11.0 0.7 %collective-permute-start.3 = (f32[17,8,128]{2,1,0:T(8,128)S(1)}, f32[17,8,128]{2,1,0:T(8,128)S(1)}, u32[]{:S(2)}, u32[]{:S(2)}) collective-permute-start(f32[17,8,128]{2,1,0:T(8,128)S(1)} %get-tuple-element.16), channel_id=1, source_target_pairs={{4,10},{6,8},{8,6},{10,4},{5,11},{7,9},{9,7},{11,5},{20,26},{22,24... | collective-permute-start | bytes 208904 | tf_op jit(solution)/shard_map/ppermute | solution.py:594
  11.7 2.7 %collective-permute-start.4 = (f32[17,8,128]{2,1,0:T(8,128)S(1)}, f32[17,8,128]{2,1,0:T(8,128)S(1)}, u32[]{:S(2)}, u32[]{:S(2)}) collective-permute-start(f32[17,8,128]{2,1,0:T(8,128)S(1)} %get-tuple-element.17), channel_id=1, source_target_pairs={{0,6},{2,4},{4,2},{6,0},{8,14},{10,12},{12,10},{14,8},{1,7},{3,5},... | collective-permute-start | bytes 208904 | tf_op jit(solution)/shard_map/ppermute | solution.py:594
  14.4 0.1 begin_block.1.refs_0_.refs_1_
  15.2 1.3 %slot_tables.1 = (bf16[256,1024]{1,0:T(8,128)(2,1)S(1)}, s32[8,1024]{1,0:T(8,128)S(1)}, s32[16,128]{1,0:T(8,128)S(1)}, f32[8,128]{1,0:T(8,128)S(1)}) custom-call(s32[1,1024]{1,0:T(1,128)S(1)} %bitcast.3, s32[1,1024]{1,0:T(1,128)S(1)} %bitcast.4, s32[1]{0:T(128)S(6)} %copy.17.site_ref, f32[2,3]{1,0:T(2,128)S(1)} %copy-done.4), custom_call_target="tpu_custom_call" | custom-call | tf_op jit(solution)/shard_map/slot_tables/pallas_call | solution.py:599
  16.4 0.3 pack_own_strips.1.refs_2_
  16.7 3.1 %collective-permute-done.refs_1_.refs_3_ = f32[12,8,8,128]{3,2,1,0:T(8,128)S(1)} collective-permute-done((f32[12,8,8,128]{3,2,1,0:T(8,128)S(1)}, f32[12,8,8,128]{3,2,1,0:T(8,128)S(1)}, u32[]{:S(2)}, u32[]{:S(2)}) %collective-permute-start) | collective-permute-done | bytes 393248 | tf_op jit(solution)/shard_map/ppermute | solution.py:587
  19.8 1.2 %collective-permute-done.2.refs_3_.refs_5_ = f32[59,16,128]{2,1,0:T(8,128)S(1)} collective-permute-done((f32[59,16,128]{2,1,0:T(8,128)S(1)}, f32[59,16,128]{2,1,0:T(8,128)S(1)}, u32[]{:S(2)}, u32[]{:S(2)}) %collective-permute-start.2) | collective-permute-done | bytes 483360 | tf_op jit(solution)/shard_map/ppermute | solution.py:585
  21.0 0.4 %pack_face_strips.1.refs_0_ = f32[38,8,128]{2,1,0:T(8,128)S(1)} custom-call(s32[8,1024]{1,0:T(8,128)S(1)} %get-tuple-element.18.after.refs_0_.refs_3_, f32[12,20,24,128]{3,2,1,0:T(8,128)S(1)} %begin_block.1.refs_0_.refs_1_, f32[12,8,128]{2,1,0:T(8,128)S(1)} %pack_own_strips.1.refs_2_, f32[12,8,8,128]{3,2,1,0:T(8,128)S(1)} %collective-permute-done.refs_1_.refs_3_, ...), custom_call_target="tpu_custom_call" | custom-call | tf_op jit(solution)/shard_map/pack_face_strips/pallas_call | solution.py:638
  21.5 1.2 %collective-permute-done.4.refs_5_.refs_2_ = f32[17,8,128]{2,1,0:T(8,128)S(1)} collective-permute-done((f32[17,8,128]{2,1,0:T(8,128)S(1)}, f32[17,8,128]{2,1,0:T(8,128)S(1)}, u32[]{:S(2)}, u32[]{:S(2)}) %collective-permute-start.4) | collective-permute-done | bytes 69664 | tf_op jit(solution)/shard_map/ppermute | solution.py:594
  22.7 0.1 pack_corner_strips.1
  22.8 0.1 collective-permute-start.5
  22.9 0.2 assemble.1.refs_0_
  23.0 1.2 %collective-permute-done.5.refs_1_ = f32[38,8,128]{2,1,0:T(8,128)S(1)} collective-permute-done((f32[38,8,128]{2,1,0:T(8,128)S(1)}, f32[38,8,128]{2,1,0:T(8,128)S(1)}, u32[]{:S(2)}, u32[]{:S(2)}) %collective-permute-start.5) | collective-permute-done | bytes 155680 | tf_op jit(solution)/shard_map/ppermute | solution.py:655
  24.3 5.3 %two_steps.1 = (f32[12,20,24,128]{3,2,1,0:T(8,128)S(1)}, f32[3,8,16,128]{3,2,1,0:T(8,128)}, f32[8,12,256]{2,1,0:T(8,128)S(1)}) custom-call(f32[12,20,24,128]{3,2,1,0:T(8,128)S(1)} %assemble.1.refs_0_, f32[38,8,128]{2,1,0:T(8,128)S(1)} %collective-permute-done.5.refs_1_, ...), custom_call_target="tpu_custom_call", output_to_operand_aliasing={{0}: (0, {})} | custom-call | tf_op jit(solution)/shard_map/two_steps/pallas_call | solution.py:667
  29.6 10.5 %all_to_all.5 = f32[8,12,256]{2,1,0:T(8,128)S(1)} all-to-all(f32[8,12,256]{2,1,0:T(8,128)S(1)} %get-tuple-element.23), channel_id=1, replica_groups=mesh['runs'=2,'gx'=4,'gy'=2,'gz'=2] {'gx','gy'}, dimensions={0} | all-to-all | bytes 196608 | tf_op jit(solution)/shard_map/all_to_all | solution.py:692
  40.1 0.1 copy.12
  40.2 0.7 %reshape.16 = f32[1,12,2048]{2,0,1:T(1,128)} reshape(f32[12,8,256]{2,1,0:T(8,128)S(1)} %copy.12) | data formatting | bytes 196608 | tf_op jit(solution)/shard_map/reshape | solution.py:693
  (10 shorter events, 0.0 us)
Async XLA Ops:
  0.6 15.8 %copy-start.1 = (f32[3,8,16,128]{3,2,1,0:T(8,128)S(1)}, f32[3,8,16,128]{3,2,1,0:T(8,128)}, u32[]{:S(2)}) copy-start(f32[3,8,16,128]{3,2,1,0:T(8,128)} %material.1) | copy-start | bytes 589828
  0.6 14.5 %copy-start.3 = (s32[1,1,1,1024,1]{3,4,2,1,0:T(1,128)S(1)}, s32[1,1,1,1024,1]{3,4,2,1,0:T(1,128)}, u32[]{:S(2)}) copy-start(s32[1,1,1,1024,1]{3,4,2,1,0:T(1,128)} %param.13) | copy-start | bytes 12292
  0.7 14.5 %copy-start.2 = (s32[1,1,1,1024]{3,2,1,0:T(1,128)S(1)}, s32[1,1,1,1024]{3,2,1,0:T(1,128)}, u32[]{:S(2)}) copy-start(s32[1,1,1,1024]{3,2,1,0:T(1,128)} %param.12) | copy-start | bytes 12292
  0.7 14.5 %copy-start.4 = (f32[2,3]{1,0:T(2,128)S(1)}, f32[2,3]{1,0:T(2,128)}, u32[]{:S(2)}) copy-start(f32[2,3]{1,0:T(2,128)} %wavelet_ref.1) | copy-start | bytes 76
  1.9 0.9 %copy-start = (f32[3,8,16,128]{3,2,1,0:T(8,128)S(1)}, f32[3,8,16,128]{3,2,1,0:T(8,128)}, u32[]{:S(2)}) copy-start(f32[3,8,16,128]{3,2,1,0:T(8,128)} %material.1) | copy-start | bytes 589828
  2.9 16.9 %collective-permute-start.1 = (f32[59,16,128]{2,1,0:T(8,128)S(1)}, f32[59,16,128]{2,1,0:T(8,128)S(1)}, u32[]{:S(2)}, u32[]{:S(2)}) collective-permute-start(f32[59,16,128]{2,1,0:T(8,128)S(1)} %get-tuple-element.14), channel_id=1, source_target_pairs={{4,8},{8,4},{5,9},{9,5},{6,10},{10,6},{7,11},{11,7},{20,24},{24,20... | collective-permute-start | bytes 1449992 | tf_op jit(solution)/shard_map/ppermute | solution.py:585
  3.6 17.4 %collective-permute-start.2 = (f32[59,16,128]{2,1,0:T(8,128)S(1)}, f32[59,16,128]{2,1,0:T(8,128)S(1)}, u32[]{:S(2)}, u32[]{:S(2)}) collective-permute-start(f32[59,16,128]{2,1,0:T(8,128)S(1)} %get-tuple-element.15), channel_id=1, source_target_pairs={{0,4},{4,0},{8,12},{12,8},{1,5},{5,1},{9,13},{13,9},{2,6},{6,2},{1... | collective-permute-start | bytes 1449992 | tf_op jit(solution)/shard_map/ppermute | solution.py:585
  9.5 10.3 %collective-permute-start = (f32[12,8,8,128]{3,2,1,0:T(8,128)S(1)}, f32[12,8,8,128]{3,2,1,0:T(8,128)S(1)}, u32[]{:S(2)}, u32[]{:S(2)}) collective-permute-start(f32[12,8,8,128]{3,2,1,0:T(8,128)S(1)} %get-tuple-element.13), channel_id=1, source_target_pairs={{0,2},{2,0},{1,3},{3,1},{4,6},{6,4},{5,7},{7,5},{8,10},{10,8},{9,1... | collective-permute-start | bytes 1179656 | tf_op jit(solution)/shard_map/ppermute | solution.py:587
  11.0 10.5 %collective-permute-start.3 = (f32[17,8,128]{2,1,0:T(8,128)S(1)}, f32[17,8,128]{2,1,0:T(8,128)S(1)}, u32[]{:S(2)}, u32[]{:S(2)}) collective-permute-start(f32[17,8,128]{2,1,0:T(8,128)S(1)} %get-tuple-element.16), channel_id=1, source_target_pairs={{4,10},{6,8},{8,6},{10,4},{5,11},{7,9},{9,7},{11,5},{20,26},{22,24... | collective-permute-start | bytes 208904 | tf_op jit(solution)/shard_map/ppermute | solution.py:594
  11.7 11.0 %collective-permute-start.4 = (f32[17,8,128]{2,1,0:T(8,128)S(1)}, f32[17,8,128]{2,1,0:T(8,128)S(1)}, u32[]{:S(2)}, u32[]{:S(2)}) collective-permute-start(f32[17,8,128]{2,1,0:T(8,128)S(1)} %get-tuple-element.17), channel_id=1, source_target_pairs={{0,6},{2,4},{4,2},{6,0},{8,14},{10,12},{12,10},{14,8},{1,7},{3,5},... | collective-permute-start | bytes 208904 | tf_op jit(solution)/shard_map/ppermute | solution.py:594
  22.8 1.4 %collective-permute-start.5 = (f32[38,8,128]{2,1,0:T(8,128)S(1)}, f32[38,8,128]{2,1,0:T(8,128)S(1)}, u32[]{:S(2)}, u32[]{:S(2)}) collective-permute-start(f32[38,8,128]{2,1,0:T(8,128)S(1)} %pack_corner_strips.1), channel_id=1, source_target_pairs={{0,1},{1,0},{2,3},{3,2},{4,5},{5,4},{6,7},{7,6},{8,9},{9,8},{10,11... | collective-permute-start | bytes 466952 | tf_op jit(solution)/shard_map/ppermute | solution.py:655

commit v7 on v5

--- a/solution.py
+++ b/solution.py
@@ -67,7 +67,10 @@
     for at, tile in enumerate(tiles):
         turned = pltpu.roll(tile, (STRIP * at + head) & (LANES - 1), 1)
         packed = turned if packed is None else jnp.where(slot == at, turned, packed)
-    return packed
+    within = iota(1) % STRIP
+    first = jnp.where(head == 0, 0, STRIP - HALO)
+    sent = jnp.logical_and(within >= first, within < first + HALO)
+    return jnp.where(sent, packed, 0.0)
 
 
 class Grid:
@@ -301,16 +304,9 @@
                 put(f, d, turned)
 
 
-def known_lanes():
+def unpack(ref, base, at):
     lead = jnp.where(lax.axis_index("gz") == 0, 0, LANES - STRIP)
-    lane = iota(1)
-    return lead, jnp.logical_and(lane >= lead, lane < lead + STRIP)
-
-
-def unpack(ref, base, at):
-    lead, known = known_lanes()
-    turned = pltpu.roll(ref[base + at // 16], (lead - STRIP * (at % 16)) & (LANES - 1), 1)
-    return jnp.where(known, turned, 0.0)
+    return pltpu.roll(ref[base + at // 16], (lead - STRIP * (at % 16)) & (LANES - 1), 1)
 
 
 def begin_kernel(grid, *refs):

time: 40.3 us -> 40.3 us (level)
  no operation moved by 1% of the time
where the time goes in v7:
time: 40.3 us; the launch traced here: 40.1 us
  starting transfers between devices  11.5 us (29%)
  blocking collectives  10.5 us (26%)
  Pallas kernels  7.78 us (19%)
  waiting for transfers between devices  6.74 us (17%)
  between operations  1.43 us (4%)
  other arithmetic  1.28 us (3%)
  local copies, waits for them, and re-layouts  0.82 us (2%)
    all_to_all x1, blocking collectives, per_device(): lax.all_to_all(table, ('gx', 'gy'), split_axis=0, concat_axis=0, tiled=True)  10.5 us
    ppermute x2, starting transfers between devices, per_device(): arrived.append(lax.ppermute(piece, 'gx', grid.pairs(grid.gx, name[1])))  6.57 us
    pallas_call x1, Pallas kernels, per_device(): pl.pallas_call(functools.partial(main_kernel, grid, width, capacity), out...  5.33 us
    ppermute x2, starting transfers between devices, per_device(): arrived.append(lax.ppermute(piece, ('gx', 'gy'), pairs))  3.39 us
    ppermute x1, waiting for transfers between devices, per_device(): arrived.append(lax.ppermute(piece, 'gy', grid.pairs(grid.gy, name[1])))  3.08 us
    ppermute x1, starting transfers between devices, per_device(): arrived.append(lax.ppermute(piece, 'gy', grid.pairs(grid.gy, name[1])))  1.49 us
    add x1, other arithmetic, per_device(): sum((lax.pad(part, jnp.float32(0.0), [(first, FIELDS - first - part.shape...  1.28 us
    pallas_call x1, Pallas kernels, per_device(): pl.pallas_call(functools.partial(slot_kernel, width, grid.cz), out_shape=...  1.26 us
  transfers between devices with their start and end apart: 6, of which 4 were waited for; matrix products, arithmetic and copies ran while one was open for 0% of the time, Pallas kernels for 5%

profile of v7, /device:TPU:0, one launch (start us, length us, event | category | flops | bytes accessed | tf_op | source)
XLA Modules:
  0.0 40.1 jit_solution(14874165521385147512)
XLA Ops:
  0.7 1.3 %pad_add_fusion.refs_0_.fields = f32[12,8,16,128]{3,2,1,0:T(8,128)S(1)} fusion(f32[3,8,16,128]{3,2,1,0:T(8,128)} %param.9, f32[3,8,16,128]{3,2,1,0:T(8,128)} %param.7, f32[6,8,16,128]{3,2,1,0:T(8,128)} %param.8), kind=kLoop, calls=%fused_computation | loop fusion | flops 393216 | bytes 1572864 | tf_op jit(solution)/shard_map/add | solution.py:558
  2.0 0.2 pack_halos.1
  2.1 0.7 %collective-permute-start.1 = (f32[59,16,128]{2,1,0:T(8,128)S(1)}, f32[59,16,128]{2,1,0:T(8,128)S(1)}, u32[]{:S(2)}, u32[]{:S(2)}) collective-permute-start(f32[59,16,128]{2,1,0:T(8,128)S(1)} %get-tuple-element.14), channel_id=1, source_target_pairs={{4,8},{8,4},{5,9},{9,5},{6,10},{10,6},{7,11},{11,7},{20,24},{24,20... | collective-permute-start | bytes 1449992 | tf_op jit(solution)/shard_map/ppermute | solution.py:574
  2.8 5.9 %collective-permute-start.2 = (f32[59,16,128]{2,1,0:T(8,128)S(1)}, f32[59,16,128]{2,1,0:T(8,128)S(1)}, u32[]{:S(2)}, u32[]{:S(2)}) collective-permute-start(f32[59,16,128]{2,1,0:T(8,128)S(1)} %get-tuple-element.15), channel_id=1, source_target_pairs={{0,4},{4,0},{8,12},{12,8},{1,5},{5,1},{9,13},{13,9},{2,6},{6,2},{1... | collective-permute-start | bytes 1449992 | tf_op jit(solution)/shard_map/ppermute | solution.py:574
  8.7 1.5 %collective-permute-start = (f32[12,8,8,128]{3,2,1,0:T(8,128)S(1)}, f32[12,8,8,128]{3,2,1,0:T(8,128)S(1)}, u32[]{:S(2)}, u32[]{:S(2)}) collective-permute-start(f32[12,8,8,128]{3,2,1,0:T(8,128)S(1)} %get-tuple-element.13), channel_id=1, source_target_pairs={{0,2},{2,0},{1,3},{3,1},{4,6},{6,4},{5,7},{7,5},{8,10},{10,8},{9,1... | collective-permute-start | bytes 1179656 | tf_op jit(solution)/shard_map/ppermute | solution.py:576
  10.2 0.7 %collective-permute-start.3 = (f32[17,8,128]{2,1,0:T(8,128)S(1)}, f32[17,8,128]{2,1,0:T(8,128)S(1)}, u32[]{:S(2)}, u32[]{:S(2)}) collective-permute-start(f32[17,8,128]{2,1,0:T(8,128)S(1)} %get-tuple-element.16), channel_id=1, source_target_pairs={{4,10},{6,8},{8,6},{10,4},{5,11},{7,9},{9,7},{11,5},{20,26},{22,24... | collective-permute-start | bytes 208904 | tf_op jit(solution)/shard_map/ppermute | solution.py:583
  10.8 2.7 %collective-permute-start.4 = (f32[17,8,128]{2,1,0:T(8,128)S(1)}, f32[17,8,128]{2,1,0:T(8,128)S(1)}, u32[]{:S(2)}, u32[]{:S(2)}) collective-permute-start(f32[17,8,128]{2,1,0:T(8,128)S(1)} %get-tuple-element.17), channel_id=1, source_target_pairs={{0,6},{2,4},{4,2},{6,0},{8,14},{10,12},{12,10},{14,8},{1,7},{3,5},... | collective-permute-start | bytes 208904 | tf_op jit(solution)/shard_map/ppermute | solution.py:583
  13.6 0.1 begin_block.1.refs_0_.refs_1_
  14.4 1.3 %slot_tables.1 = (bf16[256,1024]{1,0:T(8,128)(2,1)S(1)}, s32[8,1024]{1,0:T(8,128)S(1)}, s32[16,128]{1,0:T(8,128)S(1)}, f32[8,128]{1,0:T(8,128)S(1)}) custom-call(s32[1,1024]{1,0:T(1,128)S(1)} %bitcast.3, s32[1,1024]{1,0:T(1,128)S(1)} %bitcast.4, s32[1]{0:T(128)S(6)} %copy.17.site_ref, f32[2,3]{1,0:T(2,128)S(1)} %copy-done.2), custom_call_target="tpu_custom_call" | custom-call | tf_op jit(solution)/shard_map/slot_tables/pallas_call | solution.py:588
  15.6 0.3 pack_own_strips.1.refs_2_
  15.9 3.1 %collective-permute-done.refs_1_.refs_3_ = f32[12,8,8,128]{3,2,1,0:T(8,128)S(1)} collective-permute-done((f32[12,8,8,128]{3,2,1,0:T(8,128)S(1)}, f32[12,8,8,128]{3,2,1,0:T(8,128)S(1)}, u32[]{:S(2)}, u32[]{:S(2)}) %collective-permute-start) | collective-permute-done | bytes 393248 | tf_op jit(solution)/shard_map/ppermute | solution.py:576
  19.0 0.0 collective-permute-done.1.refs_2_.refs_4_
  19.0 1.2 %collective-permute-done.2.refs_3_.refs_5_ = f32[59,16,128]{2,1,0:T(8,128)S(1)} collective-permute-done((f32[59,16,128]{2,1,0:T(8,128)S(1)}, f32[59,16,128]{2,1,0:T(8,128)S(1)}, u32[]{:S(2)}, u32[]{:S(2)}) %collective-permute-start.2) | collective-permute-done | bytes 483360 | tf_op jit(solution)/shard_map/ppermute | solution.py:574
  20.2 0.4 %pack_face_strips.1.refs_0_ = f32[38,8,128]{2,1,0:T(8,128)S(1)} custom-call(s32[8,1024]{1,0:T(8,128)S(1)} %get-tuple-element.18.after.refs_0_.refs_3_, f32[12,20,24,128]{3,2,1,0:T(8,128)S(1)} %begin_block.1.refs_0_.refs_1_, f32[12,8,128]{2,1,0:T(8,128)S(1)} %pack_own_strips.1.refs_2_, f32[12,8,8,128]{3,2,1,0:T(8,128)S(1)} %collective-permute-done.refs_1_.refs_3_, ...), custom_call_target="tpu_custom_call" | custom-call | tf_op jit(solution)/shard_map/pack_face_strips/pallas_call | solution.py:627
  20.6 0.0 collective-permute-done.3.refs_4_.refs_1_
  20.6 1.2 %collective-permute-done.4.refs_5_.refs_2_ = f32[17,8,128]{2,1,0:T(8,128)S(1)} collective-permute-done((f32[17,8,128]{2,1,0:T(8,128)S(1)}, f32[17,8,128]{2,1,0:T(8,128)S(1)}, u32[]{:S(2)}, u32[]{:S(2)}) %collective-permute-start.4) | collective-permute-done | bytes 69664 | tf_op jit(solution)/shard_map/ppermute | solution.py:583
  21.9 0.1 pack_corner_strips.1
  22.0 0.1 collective-permute-start.5
  22.1 0.2 assemble.1.refs_0_
  22.2 1.2 %collective-permute-done.5.refs_1_ = f32[38,8,128]{2,1,0:T(8,128)S(1)} collective-permute-done((f32[38,8,128]{2,1,0:T(8,128)S(1)}, f32[38,8,128]{2,1,0:T(8,128)S(1)}, u32[]{:S(2)}, u32[]{:S(2)}) %collective-permute-start.5) | collective-permute-done | bytes 155680 | tf_op jit(solution)/shard_map/ppermute | solution.py:644
  23.4 5.3 %two_steps.1 = (f32[12,20,24,128]{3,2,1,0:T(8,128)S(1)}, f32[3,8,16,128]{3,2,1,0:T(8,128)}, f32[8,12,256]{2,1,0:T(8,128)S(1)}) custom-call(f32[12,20,24,128]{3,2,1,0:T(8,128)S(1)} %assemble.1.refs_0_, f32[38,8,128]{2,1,0:T(8,128)S(1)} %collective-permute-done.5.refs_1_, ...), custom_call_target="tpu_custom_call", output_to_operand_aliasing={{0}: (0, {})} | custom-call | tf_op jit(solution)/shard_map/two_steps/pallas_call | solution.py:656
  28.8 10.5 %all_to_all.5 = f32[8,12,256]{2,1,0:T(8,128)S(1)} all-to-all(f32[8,12,256]{2,1,0:T(8,128)S(1)} %get-tuple-element.23), channel_id=1, replica_groups=mesh['runs'=2,'gx'=4,'gy'=2,'gz'=2] {'gx','gy'}, dimensions={0} | all-to-all | bytes 196608 | tf_op jit(solution)/shard_map/all_to_all | solution.py:681
  39.3 0.1 copy.12
  39.4 0.7 %reshape.16 = f32[1,12,2048]{2,0,1:T(1,128)} reshape(f32[12,8,256]{2,1,0:T(8,128)S(1)} %copy.12) | data formatting | bytes 196608 | tf_op jit(solution)/shard_map/reshape | solution.py:682
  (6 shorter events, 0.0 us)
Async XLA Ops:
  0.6 13.7 %copy-start.1 = (s32[1,1,1,1024,1]{3,4,2,1,0:T(1,128)S(1)}, s32[1,1,1,1024,1]{3,4,2,1,0:T(1,128)}, u32[]{:S(2)}) copy-start(s32[1,1,1,1024,1]{3,4,2,1,0:T(1,128)} %param.13) | copy-start | bytes 12292
  0.6 13.7 %copy-start = (s32[1,1,1,1024]{3,2,1,0:T(1,128)S(1)}, s32[1,1,1,1024]{3,2,1,0:T(1,128)}, u32[]{:S(2)}) copy-start(s32[1,1,1,1024]{3,2,1,0:T(1,128)} %param.12) | copy-start | bytes 12292
  0.7 13.7 %copy-start.2 = (f32[2,3]{1,0:T(2,128)S(1)}, f32[2,3]{1,0:T(2,128)}, u32[]{:S(2)}) copy-start(f32[2,3]{1,0:T(2,128)} %wavelet_ref.1) | copy-start | bytes 76
  2.1 16.9 %collective-permute-start.1 = (f32[59,16,128]{2,1,0:T(8,128)S(1)}, f32[59,16,128]{2,1,0:T(8,128)S(1)}, u32[]{:S(2)}, u32[]{:S(2)}) collective-permute-start(f32[59,16,128]{2,1,0:T(8,128)S(1)} %get-tuple-element.14), channel_id=1, source_target_pairs={{4,8},{8,4},{5,9},{9,5},{6,10},{10,6},{7,11},{11,7},{20,24},{24,20... | collective-permute-start | bytes 1449992 | tf_op jit(solution)/shard_map/ppermute | solution.py:574
  2.8 17.4 %collective-permute-start.2 = (f32[59,16,128]{2,1,0:T(8,128)S(1)}, f32[59,16,128]{2,1,0:T(8,128)S(1)}, u32[]{:S(2)}, u32[]{:S(2)}) collective-permute-start(f32[59,16,128]{2,1,0:T(8,128)S(1)} %get-tuple-element.15), channel_id=1, source_target_pairs={{0,4},{4,0},{8,12},{12,8},{1,5},{5,1},{9,13},{13,9},{2,6},{6,2},{1... | collective-permute-start | bytes 1449992 | tf_op jit(solution)/shard_map/ppermute | solution.py:574
  8.7 10.3 %collective-permute-start = (f32[12,8,8,128]{3,2,1,0:T(8,128)S(1)}, f32[12,8,8,128]{3,2,1,0:T(8,128)S(1)}, u32[]{:S(2)}, u32[]{:S(2)}) collective-permute-start(f32[12,8,8,128]{3,2,1,0:T(8,128)S(1)} %get-tuple-element.13), channel_id=1, source_target_pairs={{0,2},{2,0},{1,3},{3,1},{4,6},{6,4},{5,7},{7,5},{8,10},{10,8},{9,1... | collective-permute-start | bytes 1179656 | tf_op jit(solution)/shard_map/ppermute | solution.py:576
  10.2 10.5 %collective-permute-start.3 = (f32[17,8,128]{2,1,0:T(8,128)S(1)}, f32[17,8,128]{2,1,0:T(8,128)S(1)}, u32[]{:S(2)}, u32[]{:S(2)}) collective-permute-start(f32[17,8,128]{2,1,0:T(8,128)S(1)} %get-tuple-element.16), channel_id=1, source_target_pairs={{4,10},{6,8},{8,6},{10,4},{5,11},{7,9},{9,7},{11,5},{20,26},{22,24... | collective-permute-start | bytes 208904 | tf_op jit(solution)/shard_map/ppermute | solution.py:583
  10.8 11.0 %collective-permute-start.4 = (f32[17,8,128]{2,1,0:T(8,128)S(1)}, f32[17,8,128]{2,1,0:T(8,128)S(1)}, u32[]{:S(2)}, u32[]{:S(2)}) collective-permute-start(f32[17,8,128]{2,1,0:T(8,128)S(1)} %get-tuple-element.17), channel_id=1, source_target_pairs={{0,6},{2,4},{4,2},{6,0},{8,14},{10,12},{12,10},{14,8},{1,7},{3,5},... | collective-permute-start | bytes 208904 | tf_op jit(solution)/shard_map/ppermute | solution.py:583
  22.0 1.4 %collective-permute-start.5 = (f32[38,8,128]{2,1,0:T(8,128)S(1)}, f32[38,8,128]{2,1,0:T(8,128)S(1)}, u32[]{:S(2)}, u32[]{:S(2)}) collective-permute-start(f32[38,8,128]{2,1,0:T(8,128)S(1)} %pack_corner_strips.1), channel_id=1, source_target_pairs={{0,1},{1,0},{2,3},{3,2},{4,5},{5,4},{6,7},{7,6},{8,9},{9,8},{10,11... | collective-permute-start | bytes 466952 | tf_op jit(solution)/shard_map/ppermute | solution.py:644
